TPU v7x, 32 devices: a whole 2x2x4 slice. The times are simulated.
32 devices in a mesh: layer: 4 (over z), dp: 8 (over y, x, core).
Axes of the slice: x: 2, y: 2, z: 4, core: 2. Of those that a mesh axis runs over, the one named last changes fastest.
Arguments:
- pixels: bfloat16 [8, 20, 196, 768], P('dp', 'layer')
- teacher: bfloat16 [4, 8, 20, 196, 768], P('layer', 'dp'), may hold values from -6 to 6
- masked_at: int32 [8, 20, 196], P('dp', 'layer'), may hold values from 0 to 195, each once within a row
- mask_count: int32 [8, 20], P('dp', 'layer'), may hold values from 39 to 136, as said below
- wide_master: float32 [768, 7680], P('dp'), may hold values from -0.21875 to 0.21875
- wide_first: float32 [768, 7680], P('dp'), may hold values from -2.670288e-05 to 2.670288e-05
- wide_second: float32 [768, 7680], P('dp'), may hold values from 2.9681848e-13 to 1.1872739e-12
- tall_master: float32 [3287, 768], P(None, 'dp')
- tall_first: float32 [3287, 768], P(None, 'dp'), may hold values from -2.670288e-05 to 2.670288e-05
- tall_second: float32 [3287, 768], P(None, 'dp'), may hold values from 2.9681848e-13 to 1.1872739e-12
Outputs:
- loss_sum: float32 [], replicated
- mask_total: float32 [], replicated
- grad_norm: float32 [], replicated
- wide_new: float32 [768, 7680], P('dp')
- wide_first_new: float32 [768, 7680], P('dp')
- wide_second_new: float32 [768, 7680], P('dp')
- wide_copy: bfloat16 [768, 7680], P('dp')
- tall_new: float32 [3287, 768], P(None, 'dp')
- tall_first_new: float32 [3287, 768], P(None, 'dp')
- tall_second_new: float32 [3287, 768], P(None, 'dp')
- tall_copy: bfloat16 [3287, 768], P(None, 'dp')
- query_gradient: float32 [768], P('dp')
Inputs may be any that keep to these rules, and one draw needn't show every extreme that they name: `masked_at`: each image's row is an order of its 196 patches, the first mask_count of them masked. `mask_count`: the number of masked patches of each image; at most 136, reached in every draw.
All inputs are finite; a program needn't handle non-finite values.
Results may differ from a plain program's by a relative error of at most 0.017.
The roundings to bfloat16 on the way count: a program that leaves them out, or rounds other values in their place, can miss the bound.
Values may be sent and summed in bfloat16 or wider, within the bound.
No kernel may reach another device: no remote copies, remote signals or barrier semaphores. Data moves between devices by JAX's collectives and lax.ppermute only.
A program may use at most 256 MiB of HBM per device.

v0:
```python
import functools
import math

import jax
import jax.numpy as jnp
from jax import lax
from jax.experimental import pallas as pl
from jax.experimental.pallas import tpu as pltpu
from jax.sharding import PartitionSpec as P

D = 768
HEADS = 12
HD = 64
FF = 3072
PIX = 768
P_SIZE = 196
STEP = 10
VECS = 19
MOST = 144
TAIL = 256

HUBER_BETA = 2.0
CLIP_NORM = 0.05
LEARN_RATE = 0.08
FIRST_DECAY = 0.9
SECOND_DECAY = 0.999
WEIGHT_DECAY = 0.05
ADAM_EPSILON = 1e-08
NORM_EPSILON = 1e-06
INSTANCE_EPSILON = 1e-05
LOW = jnp.bfloat16
F32 = jnp.float32


def flip(size, bit):
    return [(i, i ^ bit) for i in range(size)]


def swap(value, axis, bit):
    return lax.ppermute(value, axis, flip(lax.axis_size(axis), bit))


def over_link(value):
    return lax.ppermute(value, "dp", [(i, i ^ (4 if i & 1 else 2)) for i in range(8)])


def over_other(value):
    return lax.ppermute(value, "dp", [(i, i ^ (2 if i & 1 else 4)) for i in range(8)])


def blocks_of(me):
    link = jnp.where(me & 1 == 1, 4, 2)
    other = 6 - link
    return jnp.stack([me, me ^ 1, me ^ link, me ^ link ^ 1, me ^ 6, me ^ other ^ 1, me ^ other, me ^ 7])


def gather_part(shard, after=None):
    if lax.axis_size("dp") != 8:
        return [lax.all_gather(shard, "dp", axis=0, tiled=True)]
    twin = swap(shard, "dp", 1)
    first, second = over_link(shard), over_link(twin)
    diagonal = over_other(first if after is None else copied(first, after))
    return [shard, twin, first, second, diagonal] + [swap(piece, "dp", 1) for piece in (first, second, diagonal)]


def arrived(pieces, *indices):
    return [pieces[index] for index in indices] if len(pieces) > 1 else []


class Steps:
    def __init__(self):
        self.made = {}
        self.plain = lax.axis_size("dp") != 8 or lax.axis_size("layer") != 4

    def step(self, name, make):
        if self.plain:
            return []
        if name not in self.made:
            self.made[name] = list(make())
        return self.made[name]


class Part(Steps):
    def __init__(self, grads):
        super().__init__()
        self.grads = grads

    def core(self):
        return self.step("core", lambda: [swap(self.grads[2], "dp", 1)])

    def sums(self, after=()):
        def make():
            plan = [[[(0, block), (1, block)]] for block in range(3)]
            return add([self.grads[1], *self.core()], plan, [F32, LOW, LOW], after)

        return self.step("sums", make)

    def crossed(self):
        def make():
            _, second, diagonal = self.sums()
            return [over_other(diagonal), over_link(second)]

        return self.step("crossed", make)


    def sums_out(self, after=()):
        def make():
            diagonal, second = self.crossed()
            arrays = [self.sums()[0], diagonal, self.grads[0], second]
            return add(arrays, [[[(0, None), (1, None)]], [[(2, 1), (3, None)]]], [LOW, LOW], after)

        return self.step("sums_out", make)

    def last(self):
        def make():
            ahead, twin = self.sums_out()
            return [over_link(ahead), swap(twin, "dp", 1)]

        return self.step("last", make)

    def terms(self):
        return [1, self.grads[0], *self.last()]


def blocks_by_chip(me):
    chips, core = 2 * jnp.arange(4), me & 1
    return jnp.concatenate([chips + core, chips + 1 - core])


class Direct(Steps):
    def __init__(self, grads):
        super().__init__()
        self.grads = grads

    def core(self):
        return self.step("core", lambda: [swap(self.grads[1], "dp", 1)])

    def sums(self, after=()):
        return self.step("sums", lambda: [pair_sums(self.grads[0], *self.core(), after)])

    def last(self):
        groups = [[0, 2, 4, 6], [1, 3, 5, 7]]
        spread = functools.partial(lax.all_to_all, axis_name="dp", split_axis=0, concat_axis=0)
        return self.step("last", lambda: [spread(*self.sums(), axis_index_groups=groups, tiled=True)])

    def terms(self):
        return [4, *self.last()]


class Owned(Steps):
    def __init__(self, parts, by_halves):
        super().__init__()
        self.parts, self.by_halves = parts, by_halves
        self.place = lax.axis_index("layer")

    def shares(self, after=()):
        def make():
            if self.by_halves:
                return share_halves((self.place & 1)[None], [part.terms() for part in self.parts], after)
            terms = self.parts[0].terms()[1:]
            plan = [[[(0, 0), (1, None), (2, None)]]] * 2
            return add(terms, plan, [F32, LOW], after)

        return self.step("shares", make)

    def near(self):
        def make():
            sent = self.shares()[1]
            if self.by_halves:
                return [swap(sent, "layer", 1)]
            return [lax.ppermute(sent, "layer", [(0, 1), (3, 2)])]

        return self.step("near", make)

    def pairs(self, after=()):
        plan = [[[(0, None), (1, None)]]]
        return self.step("pairs", lambda: add([self.shares()[0], *self.near()], plan, [LOW], after))

    def far(self):
        def make():
            if self.by_halves:
                return [swap(*self.pairs(), "layer", 2)]
            return [lax.ppermute(*self.pairs(), "layer", [(1, 2), (2, 1)])]

        return self.step("far", make)

    def sum_all(self, after=()):
        plan = [[[(0, None), (1, None)]]]
        return self.step("all", lambda: add([*self.pairs(), *self.far()], plan, [LOW], after))

    def back(self):
        def make():
            if self.by_halves:
                return [swap(*self.sum_all(), "layer", 1)]
            return [lax.ppermute(*self.sum_all(), "layer", [(1, 0), (2, 3)])]

        return self.step("back", make)

    def scattered(self):
        grads = [part.grads[0].reshape(D, -1) for part in self.parts]
        shares = [lax.psum_scatter(grad, "dp", scatter_dimension=0, tiled=True) for grad in grads]
        return jnp.concatenate(shares, axis=1)

    def total(self):
        if self.plain:
            return lax.psum(self.scattered(), "layer").astype(F32)
        (mine,), (other,) = self.sum_all(), self.back()
        if not self.by_halves:
            return jnp.where((self.place == 1) | (self.place == 2), mine, other).astype(F32)
        even = self.place & 1 == 0
        halves = [jnp.where(even, mine, other), jnp.where(even, other, mine)]
        return jnp.concatenate(halves, axis=0).astype(F32)


def layer_sums(*owned):
    lows = [one.shares()[1] if not one.plain else one.scattered() for one in owned]
    return [total.astype(F32) for total in lax.psum(tuple(lows), "layer")]


def gathered_sum(value, axes):
    size = lax.axis_size(axes)
    sent = jnp.broadcast_to(value, (size, *value.shape))
    return jnp.sum(lax.all_to_all(sent, axes, split_axis=0, concat_axis=0), axis=0)
NAT = 208
TILE = 256
CHUNK = 48
SPARE_VMEM = 6 * 2**20
COST_TEACHER = 1
HEAVY = 2.5e9
ROW = pl.BlockSpec(memory_space=pltpu.VMEM)
FAR = pl.BlockSpec(memory_space=pl.ANY)
NUMBERS = pl.BlockSpec(memory_space=pltpu.SMEM)


def late(dims, dtype):
    return pltpu.HBM(dims, dtype)


def shape(dims, dtype):
    return jax.ShapeDtypeStruct(dims, dtype)


def launch(kernel, us, in_specs, out_specs, out_shape, scratch_shapes=(), grid=(), prefetch=0, after=()):
    def call(*args):
        count = len(args)

        def body(*refs):
            kernel(*refs[:count], *refs[count + len(after) :])

        held = sum(
            math.prod(ref.shape) * jnp.dtype(ref.dtype).itemsize
            for ref in scratch_shapes
            if jnp.issubdtype(ref.dtype, jnp.floating)
        )
        spec = pltpu.PrefetchScalarGridSpec(
            num_scalar_prefetch=prefetch,
            grid=grid,
            in_specs=list(in_specs) + [FAR] * len(after),
            out_specs=out_specs,
            scratch_shapes=list(scratch_shapes),
        )
        return pl.pallas_call(
            body,
            grid_spec=spec,
            out_shape=out_shape,
            compiler_params=pltpu.CompilerParams(vmem_limit_bytes=held + SPARE_VMEM),
            cost_estimate=pl.CostEstimate(flops=int(us * HEAVY), bytes_accessed=1 << 20 if us else 1, transcendentals=0),
        )(*args, *after)

    return call


def dot(left, right):
    return jnp.dot(left, right, preferred_element_type=F32)


def dot_t(left, right):
    return lax.dot_general(left, right, (((1,), (1,)), ((), ())), preferred_element_type=F32)


def t_dot(left, right):
    return lax.dot_general(left, right, (((0,), (0,)), ((), ())), preferred_element_type=F32)


def fetch(order, pieces, weight, sems, columns=None):
    rows = pieces[0].shape[0]
    copies = []
    for index, piece in enumerate(pieces):
        source = piece if columns is None else piece.at[:, columns]
        at = pl.multiple_of(order[index] * rows, 16 if rows % 16 == 0 else 8)
        copies.append(pltpu.make_async_copy(source, weight.at[pl.ds(at, rows)], sems.at[index]))
    for copy in copies:
        copy.start()
    return copies


def wait_all(copies):
    for copy in copies:
        copy.wait()


def one_hot(masked, count, rows):
    patch = lax.broadcasted_iota(jnp.int32, (rows, MOST), 0)
    slot = lax.broadcasted_iota(jnp.int32, (rows, MOST), 1)
    return jnp.where((masked[:, :MOST] == patch) & (slot < count), 1.0, 0.0)


def normed_with(values):
    mean = jnp.mean(values, axis=-1, keepdims=True)
    centered = values - mean
    inv_std = lax.rsqrt(jnp.mean(centered * centered, axis=-1, keepdims=True) + NORM_EPSILON)
    lane = lax.broadcasted_iota(jnp.int32, (1, 128), 1)
    return centered * inv_std, jnp.where(lane == 0, mean, inv_std)


def normed(values):
    centered = values - jnp.mean(values, axis=-1, keepdims=True)
    inv_std = lax.rsqrt(jnp.mean(centered * centered, axis=-1, keepdims=True) + NORM_EPSILON)
    return centered * inv_std, inv_std


def norm_in(grad_in, hat, inv_std, gain):
    scaled = grad_in * gain
    return inv_std * (
        scaled
        - jnp.mean(scaled, axis=-1, keepdims=True)
        - hat * jnp.mean(scaled * hat, axis=-1, keepdims=True)
    )


def wide(column):
    return jnp.broadcast_to(column, (column.shape[0], 128))


def folded(values):
    return jnp.sum(values.reshape(-1, 8, values.shape[-1]), axis=0)


def total_row(values):
    return jnp.sum(values, axis=0, keepdims=True)


def split_store(outs, columns, grad):
    rows = outs[0].shape[1]
    low = grad.astype(LOW)
    at = 0
    for out in outs:
        for index in range(out.shape[0]):
            out[index, :, columns] = low[at : at + rows]
            at += rows


def split_shapes(blocks, columns, counts=(2, 3, 3)):
    if blocks == 1:
        counts = (1,)
    return [shape((count, D // blocks, columns), LOW) for count in counts]


def teacher_kernel(counts, teacher, masked, out):
    for index in range(teacher.shape[0]):
        pick = one_hot(masked[index], counts[index], P_SIZE).astype(LOW)
        rows = slice(index * MOST, (index + 1) * MOST)
        for at in range(0, D, TILE):
            low = teacher[index, :, at : at + TILE]
            values = low.astype(F32)
            mean = jnp.sum(values, axis=0, keepdims=True) * (1.0 / P_SIZE)
            centered = values - mean
            square = jnp.sum(centered * centered, axis=0, keepdims=True) * (1.0 / P_SIZE)
            inv = lax.rsqrt(square + INSTANCE_EPSILON)
            out[rows, at : at + TILE] = ((t_dot(pick, low) - mean) * inv).astype(LOW)


def teacher_rows(teacher, masks, block, after=()):
    images = masks.shape[0]
    return launch(
        teacher_kernel,
        COST_TEACHER,
        in_specs=[NUMBERS, ROW, ROW],
        out_specs=ROW,
        out_shape=shape((images * MOST, D), LOW),
        after=after,
    )(masks[:, P_SIZE], lax.dynamic_slice_in_dim(teacher, block * images, images), masks[:, None, :P_SIZE])


def part_kernel(spans, *refs):
    ins, out = refs[: len(spans)], refs[-1]
    at = 0
    for (source, start, size, *room), ref in zip(spans, ins):
        out[:, at : at + size] = ref[:, start : start + size].astype(LOW)
        at += size
        if room:
            out[:, at : at + room[0] - size] = jnp.zeros((out.shape[0], room[0] - size), LOW)
            at += room[0] - size


def part(spans, after=()):
    rows = spans[0][0].shape[0]
    return launch(
        functools.partial(part_kernel, spans),
        0.2,
        in_specs=[ROW] * len(spans),
        out_specs=ROW,
        out_shape=shape((rows, sum(span[-1] for span in spans)), LOW),
        after=after,
    )(*[span[0] for span in spans])


def embed_kernel(owners, order, counts, pixels, masked, *refs):
    pieces, refs = refs[:owners], refs[owners:]
    hat, inv, rows_in, position, vectors, hat_tab, inv_tab, tab_in, weight, sems = refs
    step = pl.program_id(0)

    @pl.when(step == 0)
    def _():
        wait_all(fetch(order, pieces, weight, sems, pl.ds(0, D + TAIL)))
        small = weight[:, D:].astype(F32).T
        vectors[...] = small[P_SIZE : P_SIZE + vectors.shape[0]]
        rows = small[:P_SIZE]
        zeros = jnp.zeros((NAT - P_SIZE, D), F32)
        position[...] = jnp.concatenate([rows, zeros], axis=0).astype(LOW)
        table, table_inv = normed(rows + small[P_SIZE + 14 : P_SIZE + 15])
        hat_tab[...] = jnp.concatenate([table, zeros], axis=0)
        inv_tab[...] = jnp.concatenate([wide(table_inv), zeros[:, :128]], axis=0)
        table = table * small[P_SIZE : P_SIZE + 1] + small[P_SIZE + 1 : P_SIZE + 2]
        tab_in[...] = jnp.concatenate([table, zeros], axis=0).astype(LOW)

    flag = jnp.sum(one_hot(masked[0], counts[step], P_SIZE), axis=1, keepdims=True)
    embedded = dot(pixels[0], weight[:, :D]) + vectors[13:14]
    start = flag * vectors[14:15] + (1.0 - flag) * embedded + position[...].astype(F32)[:P_SIZE]
    value, value_inv = normed(start)
    zeros = jnp.zeros((NAT - P_SIZE, D), F32)
    hat[0] = jnp.concatenate([value, zeros], axis=0)
    inv[0] = jnp.concatenate([wide(value_inv), zeros[:, :128]], axis=0)
    value = value * vectors[0:1] + vectors[1:2]
    rows_in[0] = jnp.concatenate([value, zeros], axis=0).astype(LOW)


def embed(order, counts, pixels, masked, pieces, after=()):
    images, owners = pixels.shape[0], len(pieces)
    whole = lambda *dims: pl.BlockSpec(dims, lambda i, order, counts: (0,) * len(dims))
    image = lambda *dims: pl.BlockSpec((1, *dims), lambda i, order, counts: (i,) + (0,) * len(dims))
    return launch(
        functools.partial(embed_kernel, owners),
        1,
        prefetch=2,
        grid=(images,),
        in_specs=[image(P_SIZE, PIX), image(1, P_SIZE)] + [FAR] * owners,
        out_specs=[
            image(NAT, D),
            image(NAT, 128),
            image(NAT, D),
            whole(NAT, D),
            whole(24, D),
            whole(NAT, D),
            whole(NAT, 128),
            whole(NAT, D),
        ],
        scratch_shapes=[pltpu.VMEM((D, D + TAIL), LOW), pltpu.SemaphoreType.DMA((owners,))],
        out_shape=[
            late((images, NAT, D), F32),
            late((images, NAT, 128), F32),
            shape((images, NAT, D), LOW),
            shape((NAT, D), LOW),
            shape((24, D), F32),
            late((NAT, D), F32),
            late((NAT, 128), F32),
            shape((NAT, D), LOW),
        ],
        after=after,
    )(order, counts, pixels, masked, *pieces)


def halves(pair):
    lane = lax.broadcasted_iota(jnp.int32, (1, 128), 1)
    first = jnp.where(lane < HD, 1.0, 0.0).astype(LOW)
    return jnp.concatenate([pair * first, pair * (1.0 - first.astype(F32)).astype(LOW)], axis=0)


def merged(both):
    lane = lax.broadcasted_iota(jnp.int32, (MOST, 128), 1)
    return jnp.where(lane < HD, both[:MOST], both[MOST:])


def attention_kernel(owners, order, counts, rows_in, masked, tab_in, vectors, *refs):
    pieces, refs = refs[:owners], refs[owners:]
    kv, queries, heads, weight, table, sems = refs
    step = pl.program_id(0)

    @pl.when(step == 0)
    def _():
        wait_all(fetch(order, pieces, weight, sems, pl.ds(D + TAIL, 3 * D)))
        table[...] = (dot(tab_in[...], weight[:, :D]) + vectors[2:3]).astype(LOW)

    kv[0, :, :D] = dot(rows_in[0], weight[:, D : 2 * D]).astype(LOW)
    kv[0, :, D:] = (dot(rows_in[0], weight[:, 2 * D :]) + vectors[3:4]).astype(LOW)
    pick = one_hot(masked[0], counts[step], NAT).astype(LOW)
    queries[0] = t_dot(pick, table[...]).astype(LOW)
    key_index = lax.broadcasted_iota(jnp.int32, (1, NAT), 1)
    for at in range(0, D, 128):
        pair = halves(queries[0, :, at : at + 128]) * jnp.asarray(1.0 / math.sqrt(HD), LOW)
        scores = dot_t(pair, kv[0, :, at : at + 128])
        scores = jnp.where(key_index < P_SIZE, scores, -1e30)
        shifted = jnp.exp(scores - jnp.max(scores, axis=1, keepdims=True))
        probs = (shifted * (1.0 / jnp.sum(shifted, axis=1, keepdims=True))).astype(LOW)
        heads[0, :, at : at + 128] = merged(dot(probs, kv[0, :, D + at : D + at + 128])).astype(LOW)


def attention(order, counts, rows_in, masked, tab_in, vectors, pieces, after=()):
    images, owners = rows_in.shape[0], len(pieces)
    whole = lambda *dims: pl.BlockSpec(dims, lambda i, order, counts: (0,) * len(dims))
    image = lambda *dims: pl.BlockSpec((1, *dims), lambda i, order, counts: (i,) + (0,) * len(dims))
    return launch(
        functools.partial(attention_kernel, owners),
        12,
        prefetch=2,
        grid=(images,),
        in_specs=[image(NAT, D), image(1, P_SIZE), whole(NAT, D), whole(24, D)] + [FAR] * owners,
        out_specs=[image(NAT, 2 * D), image(MOST, D), image(MOST, D)],
        scratch_shapes=[
            pltpu.VMEM((D, 3 * D), LOW),
            pltpu.VMEM((NAT, D), LOW),
            pltpu.SemaphoreType.DMA((owners,)),
        ],
        out_shape=[late((images, NAT, 2 * D), LOW), late((images, MOST, D), LOW), shape((images, MOST, D), LOW)],
        after=after,
    )(order, counts, rows_in, masked, tab_in, vectors, *pieces)


def chunks(count, body):
    lax.fori_loop(0, count, lambda k, _: (body(k), 0)[1], 0, unroll=3)


def at_chunk(k, rows=CHUNK):
    return pl.ds(pl.multiple_of(k * rows, 16), rows)


def gelu_parts(value):
    size = jnp.abs(value) * math.sqrt(0.5)
    t = 1.0 / (1.0 + 0.3275911 * size)
    bell = jnp.exp(-size * size)
    poly = t * (0.254829592 + t * (-0.284496736 + t * (1.421413741 + t * (-1.453152027 + t * 1.061405429))))
    below = 0.5 * poly * bell
    share = jnp.where(value < 0, below, 1.0 - below)
    return value * share, share + value * bell * (1.0 / math.sqrt(2.0 * math.pi))


def mid_kernel(owners, images, order, counts, masked, heads, position, vectors, *refs):
    pieces, refs = refs[:owners], refs[owners:]
    attn, hidden, stats, rows_in, weight, sems = refs
    copies = fetch(order, pieces, weight, sems, pl.ds(0, D))
    for index in range(images):
        pick = one_hot(masked[index], counts[index], NAT).astype(LOW)
        hidden[index * MOST : (index + 1) * MOST] = t_dot(pick, position[...]) + vectors[14:15]
    wait_all(copies)
    for at in range(0, D, TILE):
        attn[:, at : at + TILE] = dot(heads[...], weight[:, at : at + TILE])

    def first(k):
        rows = at_chunk(k)
        branch = attn[rows] + vectors[4:5]
        attn[rows] = branch
        value = hidden[rows] + vectors[5:6] * branch
        hidden[rows] = value
        value, stats[rows] = normed_with(value)
        rows_in[rows] = (value * vectors[6:7] + vectors[7:8]).astype(LOW)

    chunks(hidden.shape[0] // CHUNK, first)


def mid(order, counts, masked, heads, position, vectors, pieces, after=()):
    rows, owners = heads.shape[0], len(pieces)
    return launch(
        functools.partial(mid_kernel, owners, masked.shape[0]),
        6,
        in_specs=[NUMBERS, NUMBERS] + [ROW] * 4 + [FAR] * owners,
        out_specs=[ROW] * 4,
        out_shape=[
            shape((rows, D), F32),
            shape((rows, D), F32),
            shape((rows, 128), F32),
            shape((rows, D), LOW),
        ],
        scratch_shapes=[pltpu.VMEM((D, D), LOW), pltpu.SemaphoreType.DMA((owners,))],
        after=after,
    )(order, counts, masked, heads, position, vectors, *pieces)


def up_kernel(owners, first, order, rows_in, vectors, *refs):
    pieces, refs = refs[:owners], refs[owners:]
    active, slope, weight, pre_a, pre_b, sems = refs
    wait_all(fetch(order, pieces, weight, sems, pl.ds(D + first, active.shape[1])))

    def product(tile, into):
        into[...] = dot(rows_in[...], weight[:, pl.ds(pl.multiple_of(tile * TILE, TILE), TILE)])

    def finish(tile, source):
        columns = pl.ds(pl.multiple_of(tile * TILE, TILE), TILE)
        part = D // TILE
        row = 15 + first // D + tile // part
        bias = vectors[pl.ds(row, 1), pl.ds(pl.multiple_of((tile % part) * TILE, TILE), TILE)]
        for start in range(0, source.shape[0], 48):
            value, down = gelu_parts(source[start : start + 48] + bias)
            active[start : start + 48, columns] = value.astype(LOW)
            slope[start : start + 48, columns] = down.astype(LOW)

    tiles = active.shape[1] // TILE
    product(0, pre_a)

    def pair(k):
        product(2 * k + 1, pre_b)
        finish(2 * k, pre_a)
        product(jnp.minimum(2 * k + 2, tiles - 1), pre_a)
        finish(2 * k + 1, pre_b)

    chunks(tiles // 2, pair)


def up(first, columns, order, rows_in, vectors, pieces, after=()):
    rows, owners = rows_in.shape[0], len(pieces)
    return launch(
        functools.partial(up_kernel, owners, first),
        7,
        in_specs=[NUMBERS] + [ROW] * 2 + [FAR] * owners,
        out_specs=[ROW] * 2,
        out_shape=[shape((rows, columns), LOW)] * 2,
        scratch_shapes=[
            pltpu.VMEM((D, columns), LOW),
            pltpu.VMEM((rows, TILE), F32),
            pltpu.VMEM((rows, TILE), F32),
            pltpu.SemaphoreType.DMA((owners,)),
        ],
        after=after,
    )(order, rows_in, vectors, *pieces)


def place(order, source, turned, scratch):
    blocks = order.shape[0]
    if blocks == 1:
        turned[...] = source.T
        return
    rows = D // blocks
    scratch[...] = source.T
    for index in range(blocks):
        at = pl.multiple_of(order[index] * rows, 16 if rows % 16 == 0 else 8)
        turned[index * rows : (index + 1) * rows] = scratch[pl.ds(at, rows)]


def head_kernel(owners, order, active_a, active_b, hidden, vectors, *refs):
    pieces, refs = refs[:owners], refs[owners:]
    branch, stats, rows_in, work, weight, sems = refs
    wait_all(fetch(order, pieces, weight, sems))
    half = active_a.shape[1]
    for at in range(0, D, TILE):
        rows = slice(at, at + TILE)
        value = dot_t(active_a[...], weight[rows, :half])
        branch[:, rows] = value + dot_t(active_b[...], weight[rows, half:FF])

    def first(k):
        rows = at_chunk(k)
        value = branch[rows] + vectors[8:9]
        branch[rows] = value
        value, stats[rows] = normed_with(hidden[rows] + vectors[9:10] * value)
        rows_in[rows] = (value * vectors[10:11] + vectors[11:12]).astype(LOW)

    chunks(hidden.shape[0] // CHUNK, first)
    for at in range(0, D, TILE):
        work[:, at : at + TILE] = dot(rows_in[...], weight[:, FF + at : FF + at + TILE])


def head(order, active, hidden, vectors, pieces, after=()):
    rows, owners = hidden.shape[0], len(pieces)
    return launch(
        functools.partial(head_kernel, owners),
        10,
        in_specs=[NUMBERS] + [ROW] * 4 + [FAR] * owners,
        out_specs=[ROW] * 4,
        out_shape=[
            shape((rows, D), F32),
            shape((rows, 128), F32),
            shape((rows, D), LOW),
            shape((rows, D), F32),
        ],
        scratch_shapes=[pltpu.VMEM((D, FF + D), LOW), pltpu.SemaphoreType.DMA((owners,))],
        after=after,
    )(order, *active, hidden, vectors, *pieces)


def down_kernel(owners, parts, order, counts, work, stats, hidden, branch, active_a, active_b, vectors, rows_in, *refs):
    targets, pieces, refs = refs[:parts], refs[parts : parts + owners], refs[parts + owners :]
    outs = 3 if owners > 1 else 1
    grads = refs[:outs]
    loss, head_sums, grad, grad_low, sums, weight, error_low, turned, spare, sems = refs[outs:]
    copies = fetch(order, pieces, weight, sems, pl.ds(FF, D))
    head_sums[...] = jnp.zeros_like(head_sums)
    sums[...] = jnp.zeros_like(sums)
    steps = grad.shape[0] // CHUNK

    def errors(k):
        rows = at_chunk(k)
        target = targets[0][rows].astype(F32)
        for other in targets[1:]:
            target = target + other[rows].astype(F32)
        error = work[rows] + vectors[12:13] - target * (1.0 / lax.axis_size("layer"))
        size = jnp.abs(error)
        entry = jnp.where(size < HUBER_BETA, error * error * (0.5 / HUBER_BETA), size - 0.5 * HUBER_BETA)
        per_image = MOST // CHUNK
        row = lax.broadcasted_iota(jnp.int32, (CHUNK, 1), 0) + lax.rem(k, per_image) * CHUNK
        flag = row < counts[k // per_image]
        head_sums[0] += folded(jnp.where(flag, entry, 0.0))
        value = jnp.where(flag, jnp.clip(error * (1.0 / HUBER_BETA), -1.0, 1.0), 0.0)
        head_sums[1] += folded(value)
        error_low[rows] = value.astype(LOW)

    chunks(steps, errors)
    loss[0, 0] = jnp.sum(head_sums[0])
    wait_all(copies)
    for at in range(0, D, TILE):
        grad[:, at : at + TILE] = dot_t(error_low[...], weight[at : at + TILE])

    def back(k):
        rows = at_chunk(k)
        grad_in, branch_rows = grad[rows], branch[rows]
        block = hidden[rows] + vectors[9:10] * branch_rows
        value = (block - stats[rows, :1]) * stats[rows, 1:2]
        sums[0] += folded(grad_in * value)
        sums[1] += folded(grad_in)
        value = norm_in(grad_in, value, stats[rows, 1:2], vectors[10:11])
        grad[rows] = value
        sums[2] += folded(value * branch_rows)
        value = value * vectors[9:10]
        sums[3] += folded(value)
        grad_low[rows] = value.astype(LOW)

    chunks(steps, back)
    place(order, grad_low[...], turned, spare)
    half = active_a.shape[1]
    for at in range(0, FF, TILE):
        source = active_a[:, at : at + TILE] if at < half else active_b[:, at - half : at - half + TILE]
        split_store(grads, slice(at, at + TILE), dot(turned[...], source))
    place(order, rows_in[...], turned, spare)
    for at in range(0, D, TILE):
        columns = slice(FF + at, FF + at + TILE)
        split_store(grads, columns, dot(turned[...], error_low[:, at : at + TILE]))


def down(order, counts, work, stats, hidden, branch, active, vectors, rows_in, targets, pieces, after=()):
    rows, owners = hidden.shape[0], len(pieces)
    grads = split_shapes(owners, FF + D)
    return launch(
        functools.partial(down_kernel, owners, len(targets)),
        15,
        in_specs=[NUMBERS, NUMBERS] + [ROW] * (8 + len(targets)) + [FAR] * owners,
        out_specs=[ROW] * len(grads) + [NUMBERS] + [ROW] * 4,
        out_shape=grads
        + [
            shape((1, 1), F32),
            shape((2, 8, D), F32),
            shape((rows, D), F32),
            shape((rows, D), LOW),
            shape((4, 8, D), F32),
        ],
        scratch_shapes=[
            pltpu.VMEM((D, D), LOW),
            pltpu.VMEM((rows, D), LOW),
            pltpu.VMEM((D, rows), LOW),
            pltpu.VMEM((D, rows), LOW),
            pltpu.SemaphoreType.DMA((owners,)),
        ],
        after=after,
    )(order, counts, work, stats, hidden, branch, *active, vectors, rows_in, *targets, *pieces)


def pre_kernel(owners, order, grad_low, slope_a, slope_b, rows_in, *refs):
    pieces, refs = refs[:owners], refs[owners:]
    outs = 3 if owners > 1 else 1
    grads = refs[:outs]
    pre_low, bias, weight, turned, spare, sems = refs[outs:]
    copies = fetch(order, pieces, weight, sems, pl.ds(0, FF))
    place(order, rows_in[...], turned, spare)
    wait_all(copies)

    half = slope_a.shape[1]
    for at in range(0, FF, TILE):
        columns = slice(at, at + TILE)
        slope, start = (slope_a, at) if at < half else (slope_b, at - half)
        value = dot(grad_low[...], weight[:, columns]) * slope[:, start : start + TILE].astype(F32)
        bias[:, columns] = folded(value)
        pre_low[:, columns] = value.astype(LOW)
        split_store(grads, columns, dot(turned[...], pre_low[:, columns]))


def pre(order, grad_low, slope, rows_in, pieces, after=()):
    rows, owners = grad_low.shape[0], len(pieces)
    grads = split_shapes(owners, FF)
    return launch(
        functools.partial(pre_kernel, owners),
        12,
        in_specs=[NUMBERS] + [ROW] * 4 + [FAR] * owners,
        out_specs=[ROW] * (len(grads) + 2),
        out_shape=grads + [shape((rows, FF), LOW), shape((8, FF), F32)],
        scratch_shapes=[
            pltpu.VMEM((D, FF), LOW),
            pltpu.VMEM((D, rows), LOW),
            pltpu.VMEM((D, rows), LOW),
            pltpu.SemaphoreType.DMA((owners,)),
        ],
        after=after,
    )(order, grad_low, *slope, rows_in, *pieces)


def out_kernel(owners, images, order, counts, masked, pre_low, grad, stats, hidden, attn, vectors, *refs):
    pieces, refs = refs[:owners], refs[owners:]
    heads_grad, table, sums, attn_low, weight, work, high, rest, sems = refs
    wait_all(fetch(order, pieces, weight, sems))
    for at in range(0, D, TILE):
        work[:, at : at + TILE] = dot_t(pre_low[...], weight[at : at + TILE, D:])
    sums[...] = jnp.zeros_like(sums)

    def back(k):
        rows = at_chunk(k)
        grad_in = work[rows]
        value = (hidden[rows] - stats[rows, :1]) * stats[rows, 1:2]
        sums[0] += folded(grad_in * value)
        sums[1] += folded(grad_in)
        value = grad[rows] + norm_in(grad_in, value, stats[rows, 1:2], vectors[6:7])
        low = value.astype(LOW)
        high[rows] = low
        rest[rows] = (value - low.astype(F32)).astype(LOW)
        sums[2] += folded(value * attn[rows])
        value = value * vectors[5:6]
        sums[3] += folded(value)
        attn_low[rows] = value.astype(LOW)

    chunks(work.shape[0] // CHUNK, back)
    for at in range(0, D, TILE):
        heads_grad[:, at : at + TILE] = dot_t(attn_low[...], weight[at : at + TILE, :D]).astype(LOW)
    for index in range(images):
        pick = one_hot(masked[index], counts[index], NAT).astype(LOW)
        rows = slice(index * MOST, (index + 1) * MOST)
        value = dot(pick, high[rows]) + dot(pick, rest[rows])
        table[...] = value if index == 0 else table[...] + value


def out_back(order, counts, masked, pre_low, grad, stats, hidden, attn, vectors, pieces, after=()):
    rows, owners = grad.shape[0], len(pieces)
    return launch(
        functools.partial(out_kernel, owners, masked.shape[0]),
        14,
        in_specs=[NUMBERS, NUMBERS] + [ROW] * 7 + [FAR] * owners,
        out_specs=[ROW] * 4,
        out_shape=[shape((rows, D), LOW), shape((NAT, D), F32), shape((4, 8, D), F32), shape((rows, D), LOW)],
        scratch_shapes=[
            pltpu.VMEM((D, D + FF), LOW),
            pltpu.VMEM((rows, D), F32),
            pltpu.VMEM((rows, D), LOW),
            pltpu.VMEM((rows, D), LOW),
            pltpu.SemaphoreType.DMA((owners,)),
        ],
        after=after,
    )(order, counts, masked, pre_low, grad, stats, hidden, attn, vectors, *pieces)


def attention_back_kernel(counts, queries, kv, heads_grad, masked, kv_low, table, sums, query_low):
    step = pl.program_id(0)

    @pl.when(step == 0)
    def _():
        table[...] = jnp.zeros_like(table)
        sums[...] = jnp.zeros_like(sums)

    scale = 1.0 / math.sqrt(HD)
    key_index = lax.broadcasted_iota(jnp.int32, (NAT, 1), 0)
    for at in range(0, D, 128):
        lanes = slice(at, at + 128)
        high = slice(D + at, D + at + 128)
        pair = halves(queries[0, :, lanes]) * jnp.asarray(scale, LOW)
        grad = halves(heads_grad[0, :, lanes])
        keys, values = kv[0, :, lanes], kv[0, :, high]
        scores = jnp.where(key_index < P_SIZE, dot_t(keys, pair), -1e30)
        shifted = jnp.exp(scores - jnp.max(scores, axis=0, keepdims=True))
        probs = shifted * (1.0 / jnp.sum(shifted, axis=0, keepdims=True))
        prob_grad = dot_t(values, grad)
        value_grad = dot(probs.astype(LOW), grad).astype(LOW)
        kv_low[0, :, high] = value_grad
        sums[1, :, lanes] += folded(value_grad.astype(F32))
        inner = jnp.sum(probs * prob_grad, axis=0, keepdims=True)
        score_grad = (probs * (prob_grad - inner)).astype(LOW)
        kv_low[0, :, lanes] = dot(score_grad, pair).astype(LOW)
        query_grad = merged(t_dot(score_grad, keys) * scale).astype(LOW)
        query_low[:, lanes] = query_grad
        sums[0, :, lanes] += folded(query_grad.astype(F32))
    pick = one_hot(masked[0], counts[step], NAT).astype(LOW)
    table[...] += dot(pick, query_low[...])


def attention_back(counts, queries, kv, heads_grad, masked, after=()):
    images = kv.shape[0]
    whole = lambda *dims: pl.BlockSpec(dims, lambda i, counts: (0,) * len(dims))
    image = lambda *dims: pl.BlockSpec((1, *dims), lambda i, counts: (i,) + (0,) * len(dims))
    return launch(
        attention_back_kernel,
        15,
        prefetch=1,
        grid=(images,),
        in_specs=[image(MOST, D), image(NAT, 2 * D), image(MOST, D), image(1, P_SIZE)],
        out_specs=[image(NAT, 2 * D), whole(NAT, D), whole(2, 8, D)],
        scratch_shapes=[pltpu.VMEM((MOST, D), LOW)],
        out_shape=[shape((images, NAT, 2 * D), LOW), shape((NAT, D), F32), shape((2, 8, D), F32)],
        after=after,
    )(counts, queries, kv, heads_grad, masked)


def high_rest(value):
    high = value.astype(LOW)
    return jnp.concatenate([high, (value - high.astype(F32)).astype(LOW)], axis=0)


def qkv_kernel(blocks, order, rows_in, kv_low, tab_in, table, heads, attn_low, *refs):
    outs = 3 if blocks > 1 else 1
    grads = refs[:outs]
    turned, spare, tab_turned, tab_spare, heads_turned, heads_spare = refs[outs:]
    place(order, heads[...], heads_turned, heads_spare)
    for at in range(0, D, TILE):
        columns = slice(3 * D + at, 3 * D + at + TILE)
        split_store(grads, columns, dot(heads_turned[...], attn_low[:, at : at + TILE]))
    place(order, tab_in[...], tab_turned, tab_spare)
    both = high_rest(table[...])
    twice = jnp.concatenate([tab_turned[...], tab_turned[...]], axis=1)
    for at in range(0, D, TILE):
        split_store(grads, slice(at, at + TILE), dot(twice, both[:, at : at + TILE]))
    place(order, rows_in[...], turned, spare)

    for at in range(0, 2 * D, TILE):
        split_store(grads, slice(D + at, D + at + TILE), dot(turned[...], kv_low[:, at : at + TILE]))


def qkv_back(order, rows_in, kv_low, tab_in, table, heads, attn_low, after=()):
    blocks, rows = order.shape[0], rows_in.shape[0]
    grads = split_shapes(blocks, 4 * D)
    return launch(
        functools.partial(qkv_kernel, blocks),
        7,
        in_specs=[NUMBERS] + [ROW] * 6,
        out_specs=[ROW] * len(grads),
        out_shape=grads,
        scratch_shapes=[
            pltpu.VMEM((D, rows), LOW),
            pltpu.VMEM((D, rows), LOW),
            pltpu.VMEM((D, NAT), LOW),
            pltpu.VMEM((D, NAT), LOW),
            pltpu.VMEM((D, heads.shape[0]), LOW),
            pltpu.VMEM((D, heads.shape[0]), LOW),
        ],
        after=after,
    )(order, rows_in, kv_low, tab_in, table, heads, attn_low)


def start_kernel(owners, images, order, counts, masked, kv_low, table, hidden_tab, hat, inv, hat_tab, inv_tab, vectors, head_sums, down_sums, up_bias, out_sums, qkv_sums, *refs):
    pieces, refs = refs[:owners], refs[owners:]
    start_low, small_low, weight, work, small, sums, sems = refs
    copies = fetch(order, pieces, weight, sems, pl.ds(D + TAIL, 3 * D))
    wait_all(copies)
    for at in range(0, D, TILE):
        work[:, at : at + TILE] = dot_t(kv_low[...], weight[at : at + TILE, D:])
    both = high_rest(table[...])
    tab_in = dot_t(both, weight[:, :D])
    tab_in = tab_in[:NAT] + tab_in[NAT:]
    gain = vectors[0:1]
    sums[...] = jnp.zeros_like(sums)
    sums[0] += folded(tab_in * hat_tab[...])
    sums[1] += folded(tab_in)
    tab_grad = norm_in(tab_in, hat_tab[...], inv_tab[:, :1], gain) + hidden_tab[...]
    sums[2] += folded(tab_grad)
    small[:NAT] = tab_grad
    half = NAT // 2
    for index in range(images):
        flags = jnp.sum(one_hot(masked[index], counts[index], NAT), axis=1, keepdims=True)
        for part in range(2):
            rows = slice(index * NAT + part * half, index * NAT + (part + 1) * half)
            flag = flags[part * half : (part + 1) * half]
            grad_in, value = work[rows], hat[rows]
            sums[0] += folded(grad_in * value)
            sums[1] += folded(grad_in)
            value = norm_in(grad_in, value, inv[rows, :1], gain)
            small[part * half : (part + 1) * half] += value
            sums[2] += folded(value * flag)
            value = value * (1.0 - flag)
            sums[3] += folded(value)
            start_low[rows] = value.astype(LOW)
    line = [
        total_row(sums[0]),
        total_row(sums[1]),
        total_row(qkv_sums[0]),
        total_row(qkv_sums[1]),
        total_row(out_sums[3]),
        total_row(out_sums[2]),
        total_row(out_sums[0]),
        total_row(out_sums[1]),
        total_row(down_sums[3]),
        total_row(down_sums[2]),
        total_row(down_sums[0]),
        total_row(down_sums[1]),
        total_row(head_sums[1]),
        total_row(sums[3]),
        total_row(sums[2]),
    ]
    line += [total_row(up_bias[:, at : at + D]) for at in range(0, FF, D)]
    for index, value in enumerate(line):
        small[P_SIZE + index : P_SIZE + index + 1] = value
    small[P_SIZE + len(line) :] = jnp.zeros((TAIL - P_SIZE - len(line), D), F32)
    small_low[...] = small[...].T


def start_back(order, counts, masked, kv_low, table, hidden_tab, hat, inv, hat_tab, inv_tab, vectors, head_sums, down_sums, up_bias, out_sums, qkv_sums, pieces, after=()):
    rows, owners, images = kv_low.shape[0], len(pieces), masked.shape[0]
    return launch(
        functools.partial(start_kernel, owners, images),
        8,
        in_specs=[NUMBERS, NUMBERS] + [ROW] * 14 + [FAR] * owners,
        out_specs=[ROW] * 2,
        out_shape=[shape((rows, D), LOW), shape((D, TAIL), F32)],
        scratch_shapes=[
            pltpu.VMEM((D, 3 * D), LOW),
            pltpu.VMEM((rows, D), F32),
            pltpu.VMEM((TAIL, D), F32),
            pltpu.VMEM((4, 8, D), F32),
            pltpu.SemaphoreType.DMA((owners,)),
        ],
        after=after,
    )(order, counts, masked, kv_low, table, hidden_tab, hat, inv, hat_tab, inv_tab, vectors, head_sums, down_sums, up_bias, out_sums, qkv_sums, *pieces)


def embed_back_kernel(images, blocks, order, pixels, start_low, small_low, *refs):
    outs = 2 if blocks > 1 else 1
    grads = refs[:outs]
    turned, spare, pixel_rows = refs[outs:]
    for index in range(images):
        zeros = jnp.zeros((NAT - P_SIZE, PIX), F32)
        padded = jnp.concatenate([pixels[index].astype(F32), zeros], axis=0)
        pixel_rows[index * NAT : (index + 1) * NAT] = padded.astype(LOW)
    place(order, pixel_rows[...], turned, spare)
    rows = D // order.shape[0]
    block = 0
    for out in grads:
        for index in range(out.shape[0]):
            at = pl.multiple_of(order[block] * rows, 16 if rows % 16 == 0 else 8)
            out[index, :, D:] = small_low[pl.ds(at, rows)].astype(LOW)
            block += 1
    for at in range(0, D, TILE):
        split_store(grads, slice(at, at + TILE), dot(turned[...], start_low[:, at : at + TILE]))


def embed_back(order, pixels, start_low, small_low, after=()):
    rows, blocks = start_low.shape[0], order.shape[0]
    grads = split_shapes(blocks, D + TAIL, (4, 4))
    return launch(
        functools.partial(embed_back_kernel, pixels.shape[0], blocks),
        0.1,
        in_specs=[NUMBERS] + [ROW] * 3,
        out_specs=[ROW] * len(grads),
        out_shape=grads,
        scratch_shapes=[
            pltpu.VMEM((D, rows), LOW),
            pltpu.VMEM((D, rows), LOW),
            pltpu.VMEM((rows, D), LOW),
        ],
        after=after,
    )(order, pixels, start_low, small_low)


def add_kernel(plan, *refs):
    ins, outs = refs[: len(refs) - len(plan)], refs[len(refs) - len(plan) :]
    for segments, out in zip(plan, outs):
        at = 0
        for terms in segments:
            total = None
            for source, block in terms:
                value = (ins[source][...] if block is None else ins[source][block]).astype(F32)
                total = value if total is None else total + value
            out[:, at : at + total.shape[1]] = total.astype(out.dtype)
            at += total.shape[1]


def add(arrays, plan, types, after=(), us=0):
    rows = arrays[0].shape[-2]
    widths = [sum(arrays[terms[0][0]].shape[-1] for terms in segments) for segments in plan]
    return launch(
        functools.partial(add_kernel, plan),
        us,
        in_specs=[ROW] * len(arrays),
        out_specs=[ROW] * len(plan),
        out_shape=[shape((rows, width), kind) for width, kind in zip(widths, types)],
        after=after,
    )(*arrays)


def copy_kernel(source, out):
    out[...] = source[...]


def copied(array, after):
    return launch(
        copy_kernel, 1, in_specs=[ROW], out_specs=ROW, out_shape=shape(array.shape, array.dtype), after=after
    )(array)


def pair_kernel(first, second, out):
    out[...] = (first[...].astype(F32) + second[...].astype(F32)).astype(LOW)


def pair_sums(first, second, after=()):
    return launch(
        pair_kernel, 0, in_specs=[ROW] * 2, out_specs=ROW, out_shape=shape(first.shape, LOW), after=after
    )(first, second)


def share_kernel(counts, half, *refs):
    terms, (keep, send, spare) = list(refs[:-3]), refs[-3:]
    at = 0
    for count, blocks in counts:
        own, *others = [terms.pop(0) for _ in range(count)]
        total = own[0].astype(F32)
        for chip in range(1, blocks):
            total = total + own[chip].astype(F32)
        for other in others:
            total = total + other[...].astype(F32)
        spare[:, at : at + total.shape[1]] = total
        at += total.shape[1]
    rows = keep.shape[0]
    kept = half[0]
    keep[...] = spare[pl.ds(pl.multiple_of(kept * rows, 8), rows)]
    send[...] = spare[pl.ds(pl.multiple_of((1 - kept) * rows, 8), rows)].astype(LOW)


def share_halves(half, parts, after=()):
    rows = parts[0][1].shape[1]
    columns = sum(part[1].shape[2] for part in parts)
    terms = [term for part in parts for term in part[1:]]
    return launch(
        functools.partial(share_kernel, [(len(part) - 1, part[0]) for part in parts]),
        0,
        in_specs=[NUMBERS] + [ROW] * len(terms),
        out_specs=[ROW] * 2,
        out_shape=[shape((rows // 2, columns), F32), shape((rows // 2, columns), LOW)],
        scratch_shapes=[pltpu.VMEM((rows, columns), F32)],
        after=after,
    )(half, *terms)


def adam_update(master, first, second, grad, decay):
    first_new = FIRST_DECAY * first + (1.0 - FIRST_DECAY) * grad
    second_new = SECOND_DECAY * second + (1.0 - SECOND_DECAY) * grad * grad
    first_hat = first_new / (1.0 - FIRST_DECAY**STEP)
    second_hat = second_new / (1.0 - SECOND_DECAY**STEP)
    master_new = master - LEARN_RATE * (
        first_hat / (jnp.sqrt(second_hat) + ADAM_EPSILON) + WEIGHT_DECAY * decay * master
    )
    return (master_new, first_new, second_new)


def targets_of(teacher, masked, counts, after, twin, chips):
    layers, images = lax.axis_size("layer"), masked.shape[0]
    masks = jnp.concatenate([masked, counts[:, None]], axis=1)
    if layers != 4:
        masks = lax.all_gather(masks, "layer", axis=0, tiled=False)
        picked = [teacher_rows(teacher, masks[block], block) for block in range(layers)]
        total = lax.psum_scatter(jnp.stack(picked), "layer", scatter_dimension=0, tiled=False)
        return total, None, None, picked[0]
    at = lax.axis_index("layer")
    near, second, third = [swap(masks, "layer", bit) for bit in (1, 2, 3)]
    own_rows = teacher_rows(teacher, masks, at, after)
    far_rows = teacher_rows(teacher, third, at ^ 3, [own_rows, near, second])
    far = swap(far_rows, "layer", 1)
    second_rows = teacher_rows(teacher, second, at ^ 2, [far_rows, *twin, *chips])

    def near_sum(after):
        rows = teacher_rows(teacher, near, at ^ 1, after)
        return rows, swap(rows, "layer", 1)

    far_sum = lambda after: add([second_rows, far], [[[(0, None), (1, None)]]], [LOW], after, 1)[0]
    return own_rows, near_sum, far_sum, second_rows


def body(
    pixels,
    teacher,
    masked_at,
    mask_count,
    wide_master,
    wide_first,
    wide_second,
    tall_master,
    tall_first,
    tall_second,
):
    owners, layers = lax.axis_size("dp"), lax.axis_size("layer")
    counts, masked = mask_count[0], masked_at[0][:, None, :]
    images = counts.shape[0]
    order = blocks_of(lax.axis_index("dp")) if owners == 8 else jnp.zeros((1,), jnp.int32)
    by_chip = blocks_by_chip(lax.axis_index("dp")) if owners == 8 else order
    tall_low = tall_master.T.astype(LOW)
    wide_embed = part(
        [(wide_master, 0, D), (tall_low, FF, P_SIZE + VECS, TAIL), (wide_master, D, 3 * D)]
    )
    pieces_in = gather_part(wide_embed)
    own_rows, near_sum, far_sum, second_rows = targets_of(
        teacher[0, 0], masked_at[0], counts, [wide_embed], arrived(pieces_in, 1), arrived(pieces_in, 2)
    )
    wide_up = part([(wide_master, 4 * D, D + FF)], [second_rows] + arrived(pieces_in, 4))
    pieces_up = gather_part(wide_up)

    hat_nat, inv_nat, in_nat, position, vectors, hat_tab, inv_tab, in_tab = embed(
        order, counts, pixels[0], masked, pieces_in, after=[wide_up]
    )
    targets, waits = [own_rows], arrived(pieces_up, 2)
    if far_sum:
        near_rows, near = near_sum([in_tab])
        far = far_sum([near_rows])
        targets += [near, swap(far, "layer", 2)]
        waits += [far]
    kv, queries, heads = attention(order, counts, in_nat, masked, in_tab, vectors, pieces_in, after=waits)
    heads = heads.reshape(images * MOST, D)
    wide_down = part([(tall_low, 0, FF), (wide_master, 5 * D + FF, D)], [heads] + arrived(pieces_up, 4))
    pieces_down = gather_part(wide_down)
    attn, hidden, stats_mid, in_mid = mid(
        order, counts, masked, heads, position, vectors, pieces_up, after=[wide_down]
    )
    active_a, slope_a = up(0, FF // 2, order, in_mid, vectors, pieces_up)
    active_b, slope_b = up(
        FF // 2, FF // 2, order, in_mid, vectors, pieces_up, after=[active_a] + arrived(pieces_down, 2)
    )
    active, slope = (active_a, active_b), (slope_a, slope_b)
    branch, stats_out, in_out, work = head(order, active, hidden, vectors, pieces_down)
    *down_g, loss, head_sums, grad, grad_low, down_sums = down(
        order, counts, work, stats_out, hidden, branch, active, vectors, in_out, targets, pieces_down
    )
    down_p = Part(down_g)
    *up_g, pre_low, up_bias = pre(order, grad_low, slope, in_mid, pieces_down)
    up_p = Part(up_g)
    down_s, up_s = Owned([down_p], False), Owned([up_p], False)
    heads_grad, hidden_tab, out_sums, attn_low = out_back(
        order, counts, masked, pre_low, grad, stats_mid, hidden, attn, vectors, pieces_up,
        after=down_p.sums([pre_low]),
    )
    kv_low, table, qkv_sums = attention_back(
        counts, queries, kv, heads_grad.reshape(images, MOST, D), masked,
        after=down_p.sums_out([heads_grad]) + up_p.sums([heads_grad]),
    )
    flat = lambda value: value.reshape(images * NAT, -1)
    qkv_g = qkv_back(
        order, flat(in_nat), flat(kv_low), in_tab, table, heads, attn_low,
        after=down_s.shares([table]) + up_p.sums_out([table]),
    )
    qkv_p = Part(qkv_g)
    start_low, small_low = start_back(
        order, counts, masked, flat(kv_low), table, hidden_tab, flat(hat_nat), flat(inv_nat),
        hat_tab, inv_tab, vectors, head_sums, down_sums, up_bias, out_sums, qkv_sums, pieces_in,
        after=up_s.shares([qkv_g[0]]),
    )
    embed_g = embed_back(
        by_chip, pixels[0], start_low, small_low, after=qkv_p.sums([start_low]) + down_s.pairs([start_low])
    )
    embed_p = Direct(embed_g)
    last_s = Owned([qkv_p, embed_p], True)
    ready = qkv_p.sums_out([embed_g[0]])
    ready = embed_p.sums(ready)
    ready = up_s.pairs(ready)
    ready = down_s.sum_all(ready)
    ready = last_s.shares(ready)
    ready = up_s.sum_all(ready)
    last_s.pairs(ready)
    down_s, up_s, last_s = down_s.total(), up_s.total(), last_s.total()
    qkv_s, embed_s = last_s[:, : 4 * D], last_s[:, 4 * D :]
    wide_share = jnp.concatenate([embed_s[:, :D], qkv_s, up_s, down_s[:, FF:]], axis=1)
    tall_share = jnp.concatenate([down_s[:, :FF], embed_s[:, D : D + P_SIZE + VECS]], axis=1)
    squares = (jnp.sum(wide_share * wide_share) + jnp.sum(tall_share * tall_share)) / layers
    count = jnp.sum(mask_count.astype(F32))
    loss_sum, mask_total, squares = gathered_sum(jnp.stack([loss[0, 0], count, squares]), ("layer", "dp"))
    per_mask = 1.0 / mask_total
    grad_norm = jnp.sqrt(squares) * per_mask
    factor = CLIP_NORM / jnp.maximum(grad_norm, CLIP_NORM) * per_mask
    wide_new, wide_first_new, wide_second_new = adam_update(
        wide_master, wide_first, wide_second, factor * wide_share, 1.0
    )
    tall_decay = (lax.broadcasted_iota(jnp.int32, (tall_master.shape[0], 1), 0) < FF).astype(F32)
    tall_grad = factor * tall_share.T
    tall_new, tall_first_new, tall_second_new = adam_update(
        tall_master, tall_first, tall_second, tall_grad, tall_decay
    )
    return (
        loss_sum,
        mask_total,
        grad_norm,
        wide_new,
        wide_first_new,
        wide_second_new,
        wide_new.astype(LOW),
        tall_new,
        tall_first_new,
        tall_second_new,
        tall_new.astype(LOW),
        tall_grad[FF + P_SIZE + 2],
    )


def solution(mesh):
    in_specs = (
        P("dp", "layer", None, None),
        P("layer", "dp", None, None, None),
        P("dp", "layer", None),
        P("dp", "layer"),
        P("dp", None),
        P("dp", None),
        P("dp", None),
        P(None, "dp"),
        P(None, "dp"),
        P(None, "dp"),
    )
    out_specs = (
        P(),
        P(),
        P(),
        P("dp", None),
        P("dp", None),
        P("dp", None),
        P("dp", None),
        P(None, "dp"),
        P(None, "dp"),
        P(None, "dp"),
        P(None, "dp"),
        P("dp"),
    )
    return jax.shard_map(body, mesh=mesh, in_specs=in_specs, out_specs=out_specs, check_vma=False)
```

profile of v0, /device:TPU:0, one launch (start us, length us, event | category | flops | bytes accessed | tf_op | source)
XLA Modules:
  0.0 338.5 jit_solution(948430928873534418)
XLA Ops:
  3.9 3.0 collective-permute-start.1
  11.5 4.8 %dynamic-slice_bitcast_fusion = (bf16[5,196,768]{2,1,0:T(8,128)(2,1)S(1)}, bf16[5,196,768]{2,1,0:T(8,128)(2,1)}, bf16[5,196,768]{2,1,0:T(8,128)(2,1)}, bf16[5,196,768]{2,1,0:T(8,128)(2,1)S(1)}) fusion(bf16[1,1,20,196,768]{4,3,2,1,0:T(8,128)(2,1)} %param.11, s32[]{:T(128)S(6)} %select_n.48, s32[]{:T(128)S(6)} %select_n.46, s32[]{:T(128)S(6)} %select_n.45, ...), kind=kLoop, calls=%fused_computation.7 | loop fusion | bytes 12042256 | tf_op jit(solution)/shard_map/dynamic_slice | solution.py:382
  28.3 4.5 %collective-permute-done.3.refs_2_.refs_8_.refs_10_.refs_20_ = bf16[96,3328]{1,0:T(8,128)(2,1)S(1)} collective-permute-done((bf16[96,3328]{1,0:T(8,128)(2,1)}, bf16[96,3328]{1,0:T(8,128)(2,1)S(1)}, u32[]{:S(2)}, u32[]{:S(2)}) %collective-permute-start.3) | collective-permute-done | bytes 639008 | tf_op jit(solution)/shard_map/ppermute | solution.py:48
  37.3 7.2 %shard_map.198 = (f32[5,208,768]{2,1,0:T(8,128)}, f32[5,208,128]{2,1,0:T(8,128)}, bf16[5,208,768]{2,1,0:T(8,128)(2,1)S(1)}, bf16[208,768]{1,0:T(8,128)(2,1)S(1)}...) custom-call(s32[8]{0:T(128)S(1)} %stack.44.refs_0_, ...), custom_call_target="tpu_custom_call" | custom-call | flops 2500000000 | bytes 1048576 | tf_op jit(solution)/shard_map/pallas_call | solution.py:262
  46.3 7.2 %collective-permute-done.11.refs_1_ = bf16[720,768]{1,0:T(8,128)(2,1)S(1)} collective-permute-done((bf16[720,768]{1,0:T(8,128)(2,1)S(1)}, bf16[720,768]{1,0:T(8,128)(2,1)S(1)}, u32[]{:S(2)}, u32[]{:S(2)}) %collective-permute-start.11) | collective-permute-done | bytes 1105952 | tf_op jit(solution)/shard_map/ppermute | solution.py:40
  55.4 11.8 %shard_map.201 = (bf16[5,208,1536]{2,1,0:T(8,128)(2,1)}, bf16[5,144,768]{2,1,0:T(8,128)(2,1)}, bf16[5,144,768]{2,1,0:T(8,128)(2,1)S(1)}) custom-call(s32[8]{0:T(128)S(1)} %stack.44.refs_0_, s32[5]{0:T(128)S(1)} %bitcast.63, bf16[5,208,768]{2,1,0:T(8,128)(2,1)S(1)} %get-tuple-element.83.refs_2_, s32[5,1,196]{2,1,0:T(1,128)S(1)} %bitcast.55, ...), custom_call_target="tpu_custom_call" | custom-call | flops 30000001024 | bytes 1048576 | tf_op jit(solution)/shard_map/pallas_call | solution.py:262
  67.2 4.7 %collective-permute-done.13.refs_9_.refs_6_.refs_12_ = bf16[96,3840]{1,0:T(8,128)(2,1)S(1)} collective-permute-done((bf16[96,3840]{1,0:T(8,128)(2,1)S(1)}, bf16[96,3840]{1,0:T(8,128)(2,1)S(1)}, u32[]{:S(2)}, u32[]{:S(2)}) %collective-permute-start.13) | collective-permute-done | bytes 737312 | tf_op jit(solution)/shard_map/ppermute | solution.py:44
  79.1 5.8 %collective-permute-done.18.refs_12_.refs_7_.refs_15_ = bf16[96,3840]{1,0:T(8,128)(2,1)S(1)} collective-permute-done((bf16[96,3840]{1,0:T(8,128)(2,1)S(1)}, bf16[96,3840]{1,0:T(8,128)(2,1)S(1)}, u32[]{:S(2)}, u32[]{:S(2)}) %collective-permute-start.18) | collective-permute-done | bytes 737312 | tf_op jit(solution)/shard_map/ppermute | solution.py:44
  86.2 3.7 %shard_map.203 = (f32[720,768]{1,0:T(8,128)S(1)}, f32[720,768]{1,0:T(8,128)S(1)}, f32[720,128]{1,0:T(8,128)S(1)}, bf16[720,768]{1,0:T(8,128)(2,1)S(1)}) custom-call(s32[8]{0:T(128)S(1)} %stack.44.refs_0_, s32[5]{0:T(128)S(1)} %bitcast.64, s32[5,1,196]{2,1,0:T(1,128)S(1)} %bitcast.56, bf16[720,768]{1,0:T(8,128)(2,1)S(1)} %bitcast.50, ...), custom_call_target="tpu_custom_call" | custom-call | flops 15000000512 | bytes 1048576 | tf_op jit(solution)/shard_map/pallas_call | solution.py:262
  89.9 6.3 %shard_map.204 = (bf16[720,1536]{1,0:T(8,128)(2,1)S(1)}, bf16[720,1536]{1,0:T(8,128)(2,1)S(1)}) custom-call(s32[8]{0:T(128)S(1)} %stack.44.refs_0_, bf16[720,768]{1,0:T(8,128)(2,1)S(1)} %get-tuple-element.88.refs_1_.refs_4_, f32[24,768]{1,0:T(8,128)S(1)} %get-tuple-element.85.refs_5_.refs_2_.refs_4_.refs_8_.refs_10_, ...), custom_call_target="tpu_custom_call" | custom-call | flops 17500000256 | bytes 1048576 | tf_op jit(solution)/shard_map/pallas_call | solution.py:262
  96.2 6.3 %collective-permute-done.20.refs_8_.refs_16_ = bf16[96,3840]{1,0:T(8,128)(2,1)S(1)} collective-permute-done((bf16[96,3840]{1,0:T(8,128)(2,1)S(1)}, bf16[96,3840]{1,0:T(8,128)(2,1)S(1)}, u32[]{:S(2)}, u32[]{:S(2)}) %collective-permute-start.20) | collective-permute-done | bytes 737312 | tf_op jit(solution)/shard_map/ppermute | solution.py:44
  104.1 6.0 %shard_map.205 = (bf16[720,1536]{1,0:T(8,128)(2,1)S(1)}, bf16[720,1536]{1,0:T(8,128)(2,1)S(1)}) custom-call(s32[8]{0:T(128)S(1)} %stack.44.refs_0_, bf16[720,768]{1,0:T(8,128)(2,1)S(1)} %get-tuple-element.88.refs_1_.refs_4_, f32[24,768]{1,0:T(8,128)S(1)} %get-tuple-element.85.refs_5_.refs_2_.refs_4_.refs_8_.refs_10_, ...), custom_call_target="tpu_custom_call" | custom-call | flops 17500000256 | bytes 1048576 | tf_op jit(solution)/shard_map/pallas_call | solution.py:262
  110.1 11.4 %shard_map.206 = (f32[720,768]{1,0:T(8,128)S(1)}, f32[720,128]{1,0:T(8,128)S(1)}, bf16[720,768]{1,0:T(8,128)(2,1)S(1)}, f32[720,768]{1,0:T(8,128)S(1)}) custom-call(s32[8]{0:T(128)S(1)} %stack.44.refs_0_, bf16[720,1536]{1,0:T(8,128)(2,1)S(1)} %get-tuple-element.89.refs_11_.refs_1_.refs_6_, bf16[720,1536]{1,0:T(8,128)(2,1)S(1)} %get-tuple-element.90.refs_2_.refs_7_, ...), custom_call_target="tpu_custom_call" | custom-call | flops 24999999488 | bytes 1048576 | tf_op jit(solution)/shard_map/pallas_call | solution.py:262
  121.5 4.4 %collective-permute-done.26.refs_12_ = bf16[720,768]{1,0:T(8,128)(2,1)S(1)} collective-permute-done((bf16[720,768]{1,0:T(8,128)(2,1)S(1)}, bf16[720,768]{1,0:T(8,128)(2,1)S(1)}, u32[]{:S(2)}, u32[]{:S(2)}) %collective-permute-start.26) | collective-permute-done | bytes 1105952 | tf_op jit(solution)/shard_map/ppermute | solution.py:40
  126.0 12.4 %shard_map.207 = (bf16[2,96,3840]{2,1,0:T(8,128)(2,1)S(1)}, bf16[3,96,3840]{2,1,0:T(8,128)(2,1)S(1)}, bf16[3,96,3840]{2,1,0:T(8,128)(2,1)S(1)}, f32[1,1]{1,0:T(1...) custom-call(s32[8]{0:T(128)S(1)} %stack.44.refs_0_, ...), custom_call_target="tpu_custom_call" | custom-call | flops 37499998208 | bytes 1048576 | tf_op jit(solution)/shard_map/pallas_call | solution.py:262
  138.5 10.1 %shard_map.208 = (bf16[2,96,3072]{2,1,0:T(8,128)(2,1)S(1)}, bf16[3,96,3072]{2,1,0:T(8,128)(2,1)S(1)}, bf16[3,96,3072]{2,1,0:T(8,128)(2,1)S(1)}, bf16[720,3072]{1,0:T(8,128)(2,1)S(1)}, f32[8,3072]{1,0:T(8,128)S(1)}) custom-call(s32[8]{0:T(128)S(1)} %stack.44.refs_0_, bf16[720,768]{1,0:T(8,128)(2,1)S(1)} %get-tuple-element.99.refs_1_, ...), custom_call_target="tpu_custom_call" | custom-call | flops 30000001024 | bytes 1048576 | tf_op jit(solution)/shard_map/pallas_call | solution.py:262
  151.5 15.0 %shard_map.210 = (bf16[720,768]{1,0:T(8,128)(2,1)S(1)}, f32[208,768]{1,0:T(8,128)S(1)}, f32[4,8,768]{2,1,0:T(8,128)S(1)}, bf16[720,768]{1,0:T(8,128)(2,1)S(1)}) custom-call(s32[8]{0:T(128)S(1)} %stack.44.refs_0_, s32[5]{0:T(128)S(1)} %bitcast.66, s32[5,1,196]{2,1,0:T(1,128)S(1)} %bitcast.57, bf16[720,3072]{1,0:T(8,128)(2,1)S(1)} %get-tuple-element.102.refs_2_.refs_3_, ...), custom_call_target="tpu_custom_call" | custom-call | flops 35000000512 | bytes 1048576 | tf_op jit(solution)/shard_map/pallas_call | solution.py:262
  171.5 15.0 %shard_map.213 = (bf16[5,208,1536]{2,1,0:T(8,128)(2,1)S(1)}, f32[208,768]{1,0:T(8,128)S(1)}, f32[2,8,768]{2,1,0:T(8,128)S(1)}) custom-call(s32[5]{0:T(128)S(1)} %bitcast.67, bf16[5,144,768]{2,1,0:T(8,128)(2,1)S(1)} %copy-done.45, bf16[5,208,1536]{2,1,0:T(8,128)(2,1)S(1)} %copy-done.44, bf16[5,144,768]{2,1,0:T(8,128)(2,1)S(1)} %bitcast.46, ...), custom_call_target="tpu_custom_call" | custom-call | flops 37499998208 | bytes 1048576 | tf_op jit(solution)/shard_map/pallas_call | solution.py:262
  190.6 3.3 collective-permute-start.40
  194.0 5.8 %shard_map.216 = (bf16[2,96,3072]{2,1,0:T(8,128)(2,1)S(1)}, bf16[3,96,3072]{2,1,0:T(8,128)(2,1)S(1)}, bf16[3,96,3072]{2,1,0:T(8,128)(2,1)S(1)}) custom-call(s32[8]{0:T(128)S(1)} %stack.44.refs_0_, bf16[1040,768]{1,0:T(8,128)(2,1)S(1)} %bitcast.72, bf16[1040,1536]{1,0:T(8,128)(2,1)S(1)} %bitcast.70, bf16[208,768]{1,0:T(8,128)(2,1)S(1)} %copy-done.31, ...), custom_call_target="tpu_custom_call" | custom-call | flops 17500000256 | bytes 1048576 | tf_op jit(solution)/shard_map/pallas_call | solution.py:262
  202.7 7.6 %shard_map.218 = (bf16[1040,768]{1,0:T(8,128)(2,1)S(1)}, f32[768,256]{1,0:T(8,128)S(1)}) custom-call(s32[8]{0:T(128)S(1)} %stack.44.refs_0_, s32[5]{0:T(128)S(1)} %bitcast.68, s32[5,1,196]{2,1,0:T(1,128)S(1)} %bitcast.59, bf16[1040,1536]{1,0:T(8,128)(2,1)S(1)} %bitcast.71, f32[208,768]{1,0:T(8,128)S(1)} %get-tuple-element.121.refs_3_.refs_4_, ...), custom_call_target="tpu_custom_call" | custom-call | flops 20000000000 | bytes 1048576 | tf_op jit(solution)/shard_map/pallas_call | solution.py:262
  217.9 6.0 %collective-permute-start.45 = (bf16[96,3072]{1,0:T(8,128)(2,1)}, bf16[96,3072]{1,0:T(8,128)(2,1)S(1)}, u32[]{:S(2)}, u32[]{:S(2)}) collective-permute-start(bf16[96,3072]{1,0:T(8,128)(2,1)} %get-tuple-element.142.refs_25_), channel_id=1, source_target_pairs={{0,8},{24,16},{1,9},{25,17},{2,10},{26,18},{3,11},{27,19},{4,12},{... | collective-permute-start | bytes 1769480 | tf_op jit(solution)/shard_map/ppermute | solution.py:171
  223.9 7.6 %collective-permute-done.38.refs_1_ = bf16[96,3072]{1,0:T(8,128)(2,1)S(1)} collective-permute-done((bf16[96,3072]{1,0:T(8,128)(2,1)S(1)}, bf16[96,3072]{1,0:T(8,128)(2,1)S(1)}, u32[]{:S(2)}, u32[]{:S(2)}) %collective-permute-start.38) | collective-permute-done | bytes 589856 | tf_op jit(solution)/shard_map/ppermute | solution.py:48
  234.5 4.2 %all-to-all-start = ((bf16[4,96,1024]{2,1,0:T(8,128)(2,1)}), bf16[4,96,1024]{2,1,0:T(8,128)(2,1)}, u32[]{:S(2)}, u32[]{:S(2)}) async-start(bf16[4,96,1024]{2,1,0:T(8,128)(2,1)} %shard_map.223.refs_2_), calls=%async_computation | async-start | bytes 1572864 | tf_op jit(solution)/shard_map/all_to_all | solution.py:144
  246.2 5.2 %all-to-all-done.refs_4_ = bf16[4,96,1024]{2,1,0:T(8,128)(2,1)} async-done(((bf16[4,96,1024]{2,1,0:T(8,128)(2,1)}), bf16[4,96,1024]{2,1,0:T(8,128)(2,1)}, u32[]{:S(2)}, u32[]{:S(2)}) %all-to-all-start) | async-done | bytes 786464 | tf_op jit(solution)/shard_map/all_to_all | solution.py:144
  260.3 13.5 %collective-permute-done.46.refs_1_ = bf16[48,4096]{1,0:T(8,128)(2,1)S(1)} collective-permute-done((bf16[48,4096]{1,0:T(8,128)(2,1)}, bf16[48,4096]{1,0:T(8,128)(2,1)S(1)}, u32[]{:S(2)}, u32[]{:S(2)}) %collective-permute-start.46) | collective-permute-done | bytes 393248 | tf_op jit(solution)/shard_map/ppermute | solution.py:40
  275.4 17.6 %collective-permute-done.48.refs_1_ = bf16[48,4096]{1,0:T(8,128)(2,1)S(1)} collective-permute-done((bf16[48,4096]{1,0:T(8,128)(2,1)S(1)}, bf16[48,4096]{1,0:T(8,128)(2,1)S(1)}, u32[]{:S(2)}, u32[]{:S(2)}) %collective-permute-start.48) | collective-permute-done | bytes 393248 | tf_op jit(solution)/shard_map/ppermute | solution.py:40
  294.6 9.4 %collective-permute-done.49 = bf16[48,4096]{1,0:T(8,128)(2,1)S(1)} collective-permute-done((bf16[48,4096]{1,0:T(8,128)(2,1)S(1)}, bf16[48,4096]{1,0:T(8,128)(2,1)S(1)}, u32[]{:S(2)}, u32[]{:S(2)}) %collective-permute-start.49) | collective-permute-done | bytes 393248 | tf_op jit(solution)/shard_map/ppermute | solution.py:40
  310.4 4.6 %all-to-all-start.1 = ((f32[32,1,3]{2,1,0:T(1,128)}), f32[32,1,3]{2,1,0:T(1,128)}, u32[]{:S(2)}, u32[]{:S(2)}) async-start(f32[32,1,3]{2,1,0:T(1,128)} %broadcast_in_dim.19), calls=%async_computation.1 | async-start | bytes 32768 | tf_op jit(solution)/shard_map/all_to_all | solution.py:223
  315.0 7.0 %all-to-all-done.1 = f32[32,1,3]{2,1,0:T(1,128)} async-done(((f32[32,1,3]{2,1,0:T(1,128)}), f32[32,1,3]{2,1,0:T(1,128)}, u32[]{:S(2)}, u32[]{:S(2)}) %all-to-all-start.1) | async-done | bytes 416 | tf_op jit(solution)/shard_map/all_to_all | solution.py:223
  326.1 5.0 %fusion.4 = (bf16[3287,96]{0,1:T(8,128)(2,1)}, f32[3287,96]{0,1:T(8,128)}, f32[3287,96]{0,1:T(8,128)}, f32[3287,96]{0,1:T(8,128)}, f32[3287,96]{0,1:T(8,128)S(1)}) fusion(f32[3287,96]{0,1:T(8,128)} %param.17, f32[3287]{0:T(1024)S(1)} %fusion.2, f32[3287,96]{0,1:T(8,128)} %param.18, f32[3287,96]{0,1:T(8,128)} %param.19, f32[96,215]{1,0:T(8,128)} %copy-done.52, ...), kind=kLoop, calls=%fused_computation.41 | loop fusion | flops 5679936 | bytes 10741920 | tf_op jit(solution)/shard_map/convert_element_type | solution.py:1301
  332.5 4.7 %fusion.6 = (bf16[96,7680]{1,0:T(8,128)(2,1)}, f32[96,7680]{1,0:T(8,128)}, f32[96,7680]{1,0:T(8,128)}, f32[96,7680]{1,0:T(8,128)}) fusion(f32[96,7680]{1,0:T(8,128)S(1)} %copy-done.2, f32[96,768]{1,0:T(8,128)S(1)} %copy-done.49, f32[96,3072]{1,0:T(8,128)S(1)} %select_convert_fusion.1, f32[96,3072]{1,0:T(8,128)S(1)} %slice.57, f32[96,768]{1,0:T(8,128)S(1)} %copy-done.51, ...), kind=kLoop, calls=%fused_computation.42 | loop fusion | flops 14745600 | bytes 22118404 | tf_op jit(solution)/shard_map/convert_element_type | solution.py:1297
  (255 shorter events, 91.9 us)
Async XLA Ops:
  7.1 15.1 %collective-permute-start.7 = (s32[5,197]{1,0:T(8,128)S(1)}, s32[5,197]{1,0:T(8,128)S(1)}, u32[]{:S(2)}, u32[]{:S(2)}) collective-permute-start(s32[5,197]{1,0:T(8,128)S(1)} %pad_add_fusion), channel_id=1, source_target_pairs={{0,16},{8,24},{16,0},{24,8},{1,17},{9,25},{17,1},{25,9},{2,18},{10... | collective-permute-start | bytes 11828 | tf_op jit(solution)/shard_map/ppermute | solution.py:40
  16.3 16.5 %collective-permute-start.3 = (bf16[96,3328]{1,0:T(8,128)(2,1)}, bf16[96,3328]{1,0:T(8,128)(2,1)S(1)}, u32[]{:S(2)}, u32[]{:S(2)}) collective-permute-start(bf16[96,3328]{1,0:T(8,128)(2,1)} %collective-permute-done.1.refs_5_.refs_6_.refs_8_.refs_18_), channel_id=1, source_target_pairs={{0,4},{1,3},{2,6},{3,1},{4,0},{5,7},{6,2},{7,5},{8,12},{9,11},{10,... | collective-permute-start | bytes 1916936 | tf_op jit(solution)/shard_map/ppermute | solution.py:48
  17.8 15.0 %collective-permute-start.2 = (bf16[96,3328]{1,0:T(8,128)(2,1)}, bf16[96,3328]{1,0:T(8,128)(2,1)}, u32[]{:S(2)}, u32[]{:S(2)}) collective-permute-start(bf16[96,3328]{1,0:T(8,128)(2,1)} %collective-permute-done.refs_4_.refs_5_.refs_7_.refs_17_), channel_id=1, source_target_pairs={{0,2},{1,5},{2,0},{3,7},{4,6},{5,1},{6,4},{7,3},{8,10},{9,13},{10,... | collective-permute-start | bytes 1916936 | tf_op jit(solution)/shard_map/ppermute | solution.py:44
  26.7 26.8 %collective-permute-start.11 = (bf16[720,768]{1,0:T(8,128)(2,1)S(1)}, bf16[720,768]{1,0:T(8,128)(2,1)S(1)}, u32[]{:S(2)}, u32[]{:S(2)}) collective-permute-start(bf16[720,768]{1,0:T(8,128)(2,1)S(1)} %shard_map.195.refs_3_), channel_id=1, source_target_pairs={{0,8},{8,0},{16,24},{24,16},{1,9},{9,1},{17,25},{25,17},{2,10},{10... | collective-permute-start | bytes 3317768 | tf_op jit(solution)/shard_map/ppermute | solution.py:40
  35.5 18.3 %collective-permute-start.10 = (bf16[96,3840]{1,0:T(8,128)(2,1)S(1)}, bf16[96,3840]{1,0:T(8,128)(2,1)S(1)}, u32[]{:S(2)}, u32[]{:S(2)}) collective-permute-start(bf16[96,3840]{1,0:T(8,128)(2,1)S(1)} %shard_map.197.refs_12_.refs_6_.refs_3_.refs_9_), channel_id=1, source_target_pairs={{0,2},{1,5},{2,0},{3,7},{4,6},{5,1},{6,4},{7,3},{8,10},{9,13},{10,... | collective-permute-start | bytes 2211848 | tf_op jit(solution)/shard_map/ppermute | solution.py:44
  37.0 17.3 %collective-permute-start.12 = (bf16[96,3840]{1,0:T(8,128)(2,1)S(1)}, bf16[96,3840]{1,0:T(8,128)(2,1)S(1)}, u32[]{:S(2)}, u32[]{:S(2)}) collective-permute-start(bf16[96,3840]{1,0:T(8,128)(2,1)S(1)} %shard_map.197.refs_12_.refs_6_.refs_3_.refs_9_), channel_id=1, source_target_pairs={{0,1},{1,0},{2,3},{3,2},{4,5},{5,4},{6,7},{7,6},{8,9},{9,8},{10,11... | collective-permute-start | bytes 2211848 | tf_op jit(solution)/shard_map/ppermute | solution.py:40
  53.8 19.5 %collective-permute-start.14 = (bf16[96,3840]{1,0:T(8,128)(2,1)S(1)}, bf16[96,3840]{1,0:T(8,128)(2,1)S(1)}, u32[]{:S(2)}, u32[]{:S(2)}) collective-permute-start(bf16[96,3840]{1,0:T(8,128)(2,1)S(1)} %collective-permute-done.10.refs_14_.refs_8_.refs_5_.refs_11_), channel_id=1, source_target_pairs={{0,4},{1,3},{2,6},{3,1},{4,0},{5,7},{6,2},{7,5},{8,12},{9,11},{10,... | collective-permute-start | bytes 2211848 | tf_op jit(solution)/shard_map/ppermute | solution.py:48
  54.4 20.5 %collective-permute-start.15 = (bf16[96,3840]{1,0:T(8,128)(2,1)S(1)}, bf16[96,3840]{1,0:T(8,128)(2,1)S(1)}, u32[]{:S(2)}, u32[]{:S(2)}) collective-permute-start(bf16[96,3840]{1,0:T(8,128)(2,1)S(1)} %collective-permute-done.10.refs_14_.refs_8_.refs_5_.refs_11_), channel_id=1, source_target_pairs={{0,1},{1,0},{2,3},{3,2},{4,5},{5,4},{6,7},{7,6},{8,9},{9,8},{10,11... | collective-permute-start | bytes 2211848 | tf_op jit(solution)/shard_map/ppermute | solution.py:40
  54.4 17.6 %collective-permute-start.13 = (bf16[96,3840]{1,0:T(8,128)(2,1)S(1)}, bf16[96,3840]{1,0:T(8,128)(2,1)S(1)}, u32[]{:S(2)}, u32[]{:S(2)}) collective-permute-start(bf16[96,3840]{1,0:T(8,128)(2,1)S(1)} %collective-permute-done.12.refs_7_.refs_4_.refs_10_), channel_id=1, source_target_pairs={{0,2},{1,5},{2,0},{3,7},{4,6},{5,1},{6,4},{7,3},{8,10},{9,13},{10,... | collective-permute-start | bytes 2211848 | tf_op jit(solution)/shard_map/ppermute | solution.py:44
  74.9 51.0 %collective-permute-start.26 = (bf16[720,768]{1,0:T(8,128)(2,1)S(1)}, bf16[720,768]{1,0:T(8,128)(2,1)S(1)}, u32[]{:S(2)}, u32[]{:S(2)}) collective-permute-start(bf16[720,768]{1,0:T(8,128)(2,1)S(1)} %shard_map.200.refs_15_), channel_id=1, source_target_pairs={{0,16},{8,24},{16,0},{24,8},{1,17},{9,25},{17,1},{25,9},{2,18},{10... | collective-permute-start | bytes 3317768 | tf_op jit(solution)/shard_map/ppermute | solution.py:40
  77.4 48.6 %collective-permute-start.25 = (bf16[720,768]{1,0:T(8,128)(2,1)S(1)}, bf16[720,768]{1,0:T(8,128)(2,1)S(1)}, u32[]{:S(2)}, u32[]{:S(2)}) collective-permute-start(bf16[720,768]{1,0:T(8,128)(2,1)S(1)} %shard_map.199.refs_2_), channel_id=1, source_target_pairs={{0,8},{8,0},{16,24},{24,16},{1,9},{9,1},{17,25},{25,17},{2,10},{10... | collective-permute-start | bytes 3317768 | tf_op jit(solution)/shard_map/ppermute | solution.py:40
  84.9 19.2 %collective-permute-start.21 = (bf16[96,3840]{1,0:T(8,128)(2,1)S(1)}, bf16[96,3840]{1,0:T(8,128)(2,1)S(1)}, u32[]{:S(2)}, u32[]{:S(2)}) collective-permute-start(bf16[96,3840]{1,0:T(8,128)(2,1)S(1)} %collective-permute-done.18.refs_12_.refs_7_.refs_15_), channel_id=1, source_target_pairs={{0,4},{1,3},{2,6},{3,1},{4,0},{5,7},{6,2},{7,5},{8,12},{9,11},{10,... | collective-permute-start | bytes 2211848 | tf_op jit(solution)/shard_map/ppermute | solution.py:48
  85.2 24.9 %collective-permute-start.22 = (bf16[96,3840]{1,0:T(8,128)(2,1)S(1)}, bf16[96,3840]{1,0:T(8,128)(2,1)S(1)}, u32[]{:S(2)}, u32[]{:S(2)}) collective-permute-start(bf16[96,3840]{1,0:T(8,128)(2,1)S(1)} %collective-permute-done.18.refs_12_.refs_7_.refs_15_), channel_id=1, source_target_pairs={{0,1},{1,0},{2,3},{3,2},{4,5},{5,4},{6,7},{7,6},{8,9},{9,8},{10,11... | collective-permute-start | bytes 2211848 | tf_op jit(solution)/shard_map/ppermute | solution.py:40
  85.2 17.3 %collective-permute-start.20 = (bf16[96,3840]{1,0:T(8,128)(2,1)S(1)}, bf16[96,3840]{1,0:T(8,128)(2,1)S(1)}, u32[]{:S(2)}, u32[]{:S(2)}) collective-permute-start(bf16[96,3840]{1,0:T(8,128)(2,1)S(1)} %collective-permute-done.19.refs_6_.refs_14_), channel_id=1, source_target_pairs={{0,2},{1,5},{2,0},{3,7},{4,6},{5,1},{6,4},{7,3},{8,10},{9,13},{10,... | collective-permute-start | bytes 2211848 | tf_op jit(solution)/shard_map/ppermute | solution.py:44
  148.6 18.0 %collective-permute-start.30 = (bf16[3,96,3072]{2,1,0:T(8,128)(2,1)S(1)}, bf16[3,96,3072]{2,1,0:T(8,128)(2,1)S(1)}, u32[]{:S(2)}, u32[]{:S(2)}) collective-permute-start(bf16[3,96,3072]{2,1,0:T(8,128)(2,1)S(1)} %get-tuple-element.116), channel_id=1, source_target_pairs={{0,1},{1,0},{2,3},{3,2},{4,5},{5,4},{6,7},{7,6},{8,9},{9,8},{10,11... | collective-permute-start | bytes 5308424 | tf_op jit(solution)/shard_map/ppermute | solution.py:40
  149.7 19.6 %collective-permute-start.28 = (bf16[96,3840]{1,0:T(8,128)(2,1)S(1)}, bf16[96,3840]{1,0:T(8,128)(2,1)S(1)}, u32[]{:S(2)}, u32[]{:S(2)}) collective-permute-start(bf16[96,3840]{1,0:T(8,128)(2,1)S(1)} %get-tuple-element.110.refs_19_), channel_id=1, source_target_pairs={{0,4},{1,3},{2,6},{3,1},{4,0},{5,7},{6,2},{7,5},{8,12},{9,11},{10,... | collective-permute-start | bytes 2211848 | tf_op jit(solution)/shard_map/ppermute | solution.py:48
  150.7 18.6 %collective-permute-start.29 = (bf16[96,3840]{1,0:T(8,128)(2,1)S(1)}, bf16[96,3840]{1,0:T(8,128)(2,1)S(1)}, u32[]{:S(2)}, u32[]{:S(2)}) collective-permute-start(bf16[96,3840]{1,0:T(8,128)(2,1)S(1)} %get-tuple-element.109.refs_18_), channel_id=1, source_target_pairs={{0,2},{1,5},{2,0},{3,7},{4,6},{5,1},{6,4},{7,3},{8,10},{9,13},{10,... | collective-permute-start | bytes 2211848 | tf_op jit(solution)/shard_map/ppermute | solution.py:44
  166.9 19.6 %collective-permute-start.33 = (bf16[96,3072]{1,0:T(8,128)(2,1)S(1)}, bf16[96,3072]{1,0:T(8,128)(2,1)S(1)}, u32[]{:S(2)}, u32[]{:S(2)}) collective-permute-start(bf16[96,3072]{1,0:T(8,128)(2,1)S(1)} %get-tuple-element.119.refs_9_), channel_id=1, source_target_pairs={{0,4},{1,3},{2,6},{3,1},{4,0},{5,7},{6,2},{7,5},{8,12},{9,11},{10,... | collective-permute-start | bytes 1769480 | tf_op jit(solution)/shard_map/ppermute | solution.py:48
  168.5 18.0 %collective-permute-start.34 = (bf16[96,3072]{1,0:T(8,128)(2,1)S(1)}, bf16[96,3072]{1,0:T(8,128)(2,1)S(1)}, u32[]{:S(2)}, u32[]{:S(2)}) collective-permute-start(bf16[96,3072]{1,0:T(8,128)(2,1)S(1)} %get-tuple-element.118.refs_8_), channel_id=1, source_target_pairs={{0,2},{1,5},{2,0},{3,7},{4,6},{5,1},{6,4},{7,3},{8,10},{9,13},{10,... | collective-permute-start | bytes 1769480 | tf_op jit(solution)/shard_map/ppermute | solution.py:44
  169.6 20.4 %collective-permute-start.31 = (bf16[96,3840]{1,0:T(8,128)(2,1)S(1)}, bf16[96,3840]{1,0:T(8,128)(2,1)S(1)}, u32[]{:S(2)}, u32[]{:S(2)}) collective-permute-start(bf16[96,3840]{1,0:T(8,128)(2,1)S(1)} %get-tuple-element.113.refs_5_), channel_id=1, source_target_pairs={{0,2},{1,5},{2,0},{3,7},{4,6},{5,1},{6,4},{7,3},{8,10},{9,13},{10,... | collective-permute-start | bytes 2211848 | tf_op jit(solution)/shard_map/ppermute | solution.py:44
  170.9 19.2 %collective-permute-start.32 = (bf16[96,3840]{1,0:T(8,128)(2,1)S(1)}, bf16[96,3840]{1,0:T(8,128)(2,1)S(1)}, u32[]{:S(2)}, u32[]{:S(2)}) collective-permute-start(bf16[96,3840]{1,0:T(8,128)(2,1)S(1)} %get-tuple-element.114.refs_6_), channel_id=1, source_target_pairs={{0,1},{1,0},{2,3},{3,2},{4,5},{5,4},{6,7},{7,6},{8,9},{9,8},{10,11... | collective-permute-start | bytes 2211848 | tf_op jit(solution)/shard_map/ppermute | solution.py:40
  190.6 20.0 %collective-permute-start.40 = (bf16[96,3840]{1,0:T(8,128)(2,1)S(1)}, bf16[96,3840]{1,0:T(8,128)(2,1)S(1)}, u32[]{:S(2)}, u32[]{:S(2)}) collective-permute-start(bf16[96,3840]{1,0:T(8,128)(2,1)S(1)} %get-tuple-element.124.refs_8_), channel_id=1, source_target_pairs={{0,8},{24,16},{1,9},{25,17},{2,10},{26,18},{3,11},{27,19},{4,12},{... | collective-permute-start | bytes 2211848 | tf_op jit(solution)/shard_map/ppermute | solution.py:171
  215.0 18.5 %collective-permute-start.43 = (bf16[4,96,1024]{2,1,0:T(8,128)(2,1)S(1)}, bf16[4,96,1024]{2,1,0:T(8,128)(2,1)S(1)}, u32[]{:S(2)}, u32[]{:S(2)}) collective-permute-start(bf16[4,96,1024]{2,1,0:T(8,128)(2,1)S(1)} %get-tuple-element.151), channel_id=1, source_target_pairs={{0,1},{1,0},{2,3},{3,2},{4,5},{5,4},{6,7},{7,6},{8,9},{9,8},{10,11... | collective-permute-start | bytes 2359304 | tf_op jit(solution)/shard_map/ppermute | solution.py:40
  215.4 16.2 %collective-permute-start.38 = (bf16[96,3072]{1,0:T(8,128)(2,1)S(1)}, bf16[96,3072]{1,0:T(8,128)(2,1)S(1)}, u32[]{:S(2)}, u32[]{:S(2)}) collective-permute-start(bf16[96,3072]{1,0:T(8,128)(2,1)S(1)} %get-tuple-element.145.refs_6_), channel_id=1, source_target_pairs={{0,4},{1,3},{2,6},{3,1},{4,0},{5,7},{6,2},{7,5},{8,12},{9,11},{10,... | collective-permute-start | bytes 1769480 | tf_op jit(solution)/shard_map/ppermute | solution.py:48
  216.0 15.5 %collective-permute-start.39 = (bf16[96,3072]{1,0:T(8,128)(2,1)S(1)}, bf16[96,3072]{1,0:T(8,128)(2,1)S(1)}, u32[]{:S(2)}, u32[]{:S(2)}) collective-permute-start(bf16[96,3072]{1,0:T(8,128)(2,1)S(1)} %get-tuple-element.146.refs_5_), channel_id=1, source_target_pairs={{0,2},{1,5},{2,0},{3,7},{4,6},{5,1},{6,4},{7,3},{8,10},{9,13},{10,... | collective-permute-start | bytes 1769480 | tf_op jit(solution)/shard_map/ppermute | solution.py:44
  217.2 24.8 %collective-permute-start.44 = (bf16[96,3840]{1,0:T(8,128)(2,1)S(1)}, bf16[96,3840]{1,0:T(8,128)(2,1)S(1)}, u32[]{:S(2)}, u32[]{:S(2)}) collective-permute-start(bf16[96,3840]{1,0:T(8,128)(2,1)S(1)} %shard_map.220.refs_7_.refs_0_), channel_id=1, source_target_pairs={{8,16},{16,8},{9,17},{17,9},{10,18},{18,10},{11,19},{19,11},{12,20... | collective-permute-start | bytes 2211848 | tf_op jit(solution)/shard_map/ppermute | solution.py:183
  217.9 20.8 %collective-permute-start.45 = (bf16[96,3072]{1,0:T(8,128)(2,1)}, bf16[96,3072]{1,0:T(8,128)(2,1)S(1)}, u32[]{:S(2)}, u32[]{:S(2)}) collective-permute-start(bf16[96,3072]{1,0:T(8,128)(2,1)} %get-tuple-element.142.refs_25_), channel_id=1, source_target_pairs={{0,8},{24,16},{1,9},{25,17},{2,10},{26,18},{3,11},{27,19},{4,12},{... | collective-permute-start | bytes 1769480 | tf_op jit(solution)/shard_map/ppermute | solution.py:171
  234.5 16.9 %all-to-all-start = ((bf16[4,96,1024]{2,1,0:T(8,128)(2,1)}), bf16[4,96,1024]{2,1,0:T(8,128)(2,1)}, u32[]{:S(2)}, u32[]{:S(2)}) async-start(bf16[4,96,1024]{2,1,0:T(8,128)(2,1)} %shard_map.223.refs_2_), calls=%async_computation | async-start | bytes 1572864 | tf_op jit(solution)/shard_map/all_to_all | solution.py:144
  244.2 29.8 %collective-permute-start.51 = (bf16[96,3840]{1,0:T(8,128)(2,1)S(1)}, bf16[96,3840]{1,0:T(8,128)(2,1)}, u32[]{:S(2)}, u32[]{:S(2)}) collective-permute-start(bf16[96,3840]{1,0:T(8,128)(2,1)S(1)} %shard_map.225.refs_5_), channel_id=1, source_target_pairs={{8,0},{16,24},{9,1},{17,25},{10,2},{18,26},{11,3},{19,27},{12,4},{... | collective-permute-start | bytes 2211848 | tf_op jit(solution)/shard_map/ppermute | solution.py:195
  255.1 18.8 %collective-permute-start.46 = (bf16[48,4096]{1,0:T(8,128)(2,1)}, bf16[48,4096]{1,0:T(8,128)(2,1)S(1)}, u32[]{:S(2)}, u32[]{:S(2)}) collective-permute-start(bf16[48,4096]{1,0:T(8,128)(2,1)} %get-tuple-element.153.refs_3_), channel_id=1, source_target_pairs={{0,8},{8,0},{16,24},{24,16},{1,9},{9,1},{17,25},{25,17},{2,10},{10... | collective-permute-start | bytes 1179656 | tf_op jit(solution)/shard_map/ppermute | solution.py:40
  259.0 35.5 %collective-permute-start.50 = (bf16[96,3072]{1,0:T(8,128)(2,1)S(1)}, bf16[96,3072]{1,0:T(8,128)(2,1)S(1)}, u32[]{:S(2)}, u32[]{:S(2)}) collective-permute-start(bf16[96,3072]{1,0:T(8,128)(2,1)S(1)} %shard_map.227.refs_2_), channel_id=1, source_target_pairs={{8,0},{16,24},{9,1},{17,25},{10,2},{18,26},{11,3},{19,27},{12,4},{... | collective-permute-start | bytes 1769480 | tf_op jit(solution)/shard_map/ppermute | solution.py:195
  273.9 19.0 %collective-permute-start.48 = (bf16[48,4096]{1,0:T(8,128)(2,1)S(1)}, bf16[48,4096]{1,0:T(8,128)(2,1)S(1)}, u32[]{:S(2)}, u32[]{:S(2)}) collective-permute-start(bf16[48,4096]{1,0:T(8,128)(2,1)S(1)} %shard_map.228.refs_0_), channel_id=1, source_target_pairs={{0,16},{8,24},{16,0},{24,8},{1,17},{9,25},{17,1},{25,9},{2,18},{10... | collective-permute-start | bytes 1179656 | tf_op jit(solution)/shard_map/ppermute | solution.py:40
  (75 other events, 641.8 us)
where the time goes:
time: 344 us; the launch traced here: 338 us
  Pallas kernels  132 us (38%)
  waiting for transfers between devices  97.2 us (28%)
  starting transfers between devices  60.7 us (18%)
  local copies, waits for them, and re-layouts  24.6 us (7%)
  other arithmetic  18.3 us (5%)
  between operations  5.66 us (2%)
    pallas_call x37, Pallas kernels, call(): pl.pallas_call(body, grid_spec=spec, out_shape=out_shape, compiler_params...  132 us
    ppermute x28, waiting for transfers between devices, swap(): return lax.ppermute(value, axis, flip(lax.axis_size(axis), bit))  52.3 us
    ppermute x12, waiting for transfers between devices, over_link(): lax.ppermute(value, 'dp', [(i, i ^ (4 if i & 1 else 2)) for i in range(8)])  18.8 us
    ppermute x28, starting transfers between devices, swap(): return lax.ppermute(value, axis, flip(lax.axis_size(axis), bit))  18.4 us
    unnamed x107, local copies, waits for them, and re-layouts  16.1 us
    ppermute x12, starting transfers between devices, over_link(): lax.ppermute(value, 'dp', [(i, i ^ (4 if i & 1 else 2)) for i in range(8)])  14.7 us
    ppermute x6, waiting for transfers between devices, over_other(): lax.ppermute(value, 'dp', [(i, i ^ (2 if i & 1 else 4)) for i in range(8)])  12.1 us
    ppermute x2, starting transfers between devices, make(): return [lax.ppermute(sent, 'layer', [(0, 1), (3, 2)])]  9.35 us
  transfers between devices with their start and end apart: 54, of which 17 were waited for; matrix products, arithmetic and copies ran while one was open for 2% of the time, Pallas kernels for 34%

commit v1 on v0

--- a/solution.py
+++ b/solution.py
@@ -380,6 +380,25 @@
         out_shape=shape((images * MOST, D), LOW),
         after=after,
     )(masks[:, P_SIZE], lax.dynamic_slice_in_dim(teacher, block * images, images), masks[:, None, :P_SIZE])
+
+
+def far_kernel(mine, other, first, second):
+    total = (mine[...].astype(F32) + other[...].astype(F32)).astype(LOW)
+    half = first.shape[1]
+    first[...] = total[:, :half]
+    second[...] = total[:, half:]
+
+
+def far_sums(mine, other, after=()):
+    rows = mine.shape[0]
+    return launch(
+        far_kernel,
+        1,
+        in_specs=[ROW] * 2,
+        out_specs=[ROW] * 2,
+        out_shape=[shape((rows, D // 2), LOW)] * 2,
+        after=after,
+    )(mine, other)
 
 
 def part_kernel(spans, *refs):
@@ -515,13 +534,12 @@
         prefetch=2,
         grid=(images,),
         in_specs=[image(NAT, D), image(1, P_SIZE), whole(NAT, D), whole(24, D)] + [FAR] * owners,
-        out_specs=[image(NAT, 2 * D), image(MOST, D), image(MOST, D)],
+        out_specs=[image(NAT, 2 * D), image(MOST, D), image(MOST, D), whole(D, 3 * D)],
         scratch_shapes=[
-            pltpu.VMEM((D, 3 * D), LOW),
             pltpu.VMEM((NAT, D), LOW),
             pltpu.SemaphoreType.DMA((owners,)),
         ],
-        out_shape=[late((images, NAT, 2 * D), LOW), late((images, MOST, D), LOW), shape((images, MOST, D), LOW)],
+        out_shape=[late((images, NAT, 2 * D), LOW), late((images, MOST, D), LOW), shape((images, MOST, D), LOW), late((D, 3 * D), LOW)],
         after=after,
     )(order, counts, rows_in, masked, tab_in, vectors, *pieces)
 
@@ -546,8 +564,9 @@
 
 def mid_kernel(owners, images, order, counts, masked, heads, position, vectors, *refs):
     pieces, refs = refs[:owners], refs[owners:]
-    attn, hidden, stats, rows_in, weight, sems = refs
-    copies = fetch(order, pieces, weight, sems, pl.ds(0, D))
+    attn, hidden, stats, rows_in, weight, sems, up_sems = refs
+    copies = fetch(order, pieces, weight.at[:, pl.ds(0, D)], sems, pl.ds(0, D))
+    up_copies = fetch(order, pieces, weight.at[:, pl.ds(D, FF)], up_sems, pl.ds(D, FF))
     for index in range(images):
         pick = one_hot(masked[index], counts[index], NAT).astype(LOW)
         hidden[index * MOST : (index + 1) * MOST] = t_dot(pick, position[...]) + vectors[14:15]
@@ -565,6 +584,7 @@
         rows_in[rows] = (value * vectors[6:7] + vectors[7:8]).astype(LOW)
 
     chunks(hidden.shape[0] // CHUNK, first)
+    wait_all(up_copies)
 
 
 def mid(order, counts, masked, heads, position, vectors, pieces, after=()):
@@ -573,25 +593,22 @@
         functools.partial(mid_kernel, owners, masked.shape[0]),
         6,
         in_specs=[NUMBERS, NUMBERS] + [ROW] * 4 + [FAR] * owners,
-        out_specs=[ROW] * 4,
+        out_specs=[ROW] * 5,
         out_shape=[
             shape((rows, D), F32),
             shape((rows, D), F32),
             shape((rows, 128), F32),
             shape((rows, D), LOW),
+            shape((D, D + FF), LOW),
         ],
-        scratch_shapes=[pltpu.VMEM((D, D), LOW), pltpu.SemaphoreType.DMA((owners,))],
+        scratch_shapes=[pltpu.SemaphoreType.DMA((owners,))] * 2,
         after=after,
     )(order, counts, masked, heads, position, vectors, *pieces)
 
 
-def up_kernel(owners, first, order, rows_in, vectors, *refs):
-    pieces, refs = refs[:owners], refs[owners:]
-    active, slope, weight, pre_a, pre_b, sems = refs
-    wait_all(fetch(order, pieces, weight, sems, pl.ds(D + first, active.shape[1])))
-
+def up_kernel(first, rows_in, vectors, weight, active, slope, pre_a, pre_b):
     def product(tile, into):
-        into[...] = dot(rows_in[...], weight[:, pl.ds(pl.multiple_of(tile * TILE, TILE), TILE)])
+        into[...] = dot(rows_in[...], weight[:, pl.ds(pl.multiple_of(D + first + tile * TILE, TILE), TILE)])
 
     def finish(tile, source):
         columns = pl.ds(pl.multiple_of(tile * TILE, TILE), TILE)
@@ -615,22 +632,20 @@
     chunks(tiles // 2, pair)
 
 
-def up(first, columns, order, rows_in, vectors, pieces, after=()):
-    rows, owners = rows_in.shape[0], len(pieces)
-    return launch(
-        functools.partial(up_kernel, owners, first),
+def up(first, columns, rows_in, vectors, weight, after=()):
+    rows = rows_in.shape[0]
+    return launch(
+        functools.partial(up_kernel, first),
         7,
-        in_specs=[NUMBERS] + [ROW] * 2 + [FAR] * owners,
+        in_specs=[ROW] * 3,
         out_specs=[ROW] * 2,
         out_shape=[shape((rows, columns), LOW)] * 2,
         scratch_shapes=[
-            pltpu.VMEM((D, columns), LOW),
             pltpu.VMEM((rows, TILE), F32),
             pltpu.VMEM((rows, TILE), F32),
-            pltpu.SemaphoreType.DMA((owners,)),
         ],
         after=after,
-    )(order, rows_in, vectors, *pieces)
+    )(rows_in, vectors, weight)
 
 
 def place(order, source, turned, scratch):
@@ -647,8 +662,10 @@
 
 def head_kernel(owners, order, active_a, active_b, hidden, vectors, *refs):
     pieces, refs = refs[:owners], refs[owners:]
-    branch, stats, rows_in, work, weight, sems = refs
-    wait_all(fetch(order, pieces, weight, sems))
+    branch, stats, rows_in, work, weight, sems, head_sems = refs
+    copies = fetch(order, pieces, weight.at[:, pl.ds(0, FF)], sems, pl.ds(0, FF))
+    head_copies = fetch(order, pieces, weight.at[:, pl.ds(FF, D)], head_sems, pl.ds(FF, D))
+    wait_all(copies)
     half = active_a.shape[1]
     for at in range(0, D, TILE):
         rows = slice(at, at + TILE)
@@ -663,6 +680,7 @@
         rows_in[rows] = (value * vectors[10:11] + vectors[11:12]).astype(LOW)
 
     chunks(hidden.shape[0] // CHUNK, first)
+    wait_all(head_copies)
     for at in range(0, D, TILE):
         work[:, at : at + TILE] = dot(rows_in[...], weight[:, FF + at : FF + at + TILE])
 
@@ -673,24 +691,24 @@
         functools.partial(head_kernel, owners),
         10,
         in_specs=[NUMBERS] + [ROW] * 4 + [FAR] * owners,
-        out_specs=[ROW] * 4,
+        out_specs=[ROW] * 5,
         out_shape=[
             shape((rows, D), F32),
             shape((rows, 128), F32),
             shape((rows, D), LOW),
             shape((rows, D), F32),
+            shape((D, FF + D), LOW),
         ],
-        scratch_shapes=[pltpu.VMEM((D, FF + D), LOW), pltpu.SemaphoreType.DMA((owners,))],
+        scratch_shapes=[pltpu.SemaphoreType.DMA((owners,))] * 2,
         after=after,
     )(order, *active, hidden, vectors, *pieces)
 
 
-def down_kernel(owners, parts, order, counts, work, stats, hidden, branch, active_a, active_b, vectors, rows_in, *refs):
-    targets, pieces, refs = refs[:parts], refs[parts : parts + owners], refs[parts + owners :]
-    outs = 3 if owners > 1 else 1
+def down_kernel(parts, order, counts, work, stats, hidden, branch, active_a, active_b, vectors, rows_in, weight, *refs):
+    targets, refs = refs[:parts], refs[parts:]
+    outs = 3 if order.shape[0] > 1 else 1
     grads = refs[:outs]
-    loss, head_sums, grad, grad_low, sums, weight, error_low, turned, spare, sems = refs[outs:]
-    copies = fetch(order, pieces, weight, sems, pl.ds(FF, D))
+    loss, head_sums, grad, grad_low, sums, error_low, turned, spare = refs[outs:]
     head_sums[...] = jnp.zeros_like(head_sums)
     sums[...] = jnp.zeros_like(sums)
     steps = grad.shape[0] // CHUNK
@@ -698,8 +716,9 @@
     def errors(k):
         rows = at_chunk(k)
         target = targets[0][rows].astype(F32)
-        for other in targets[1:]:
-            target = target + other[rows].astype(F32)
+        if len(targets) > 1:
+            near, first, second = [other[rows].astype(F32) for other in targets[1:]]
+            target = target + near + jnp.concatenate([first, second], axis=1)
         error = work[rows] + vectors[12:13] - target * (1.0 / lax.axis_size("layer"))
         size = jnp.abs(error)
         entry = jnp.where(size < HUBER_BETA, error * error * (0.5 / HUBER_BETA), size - 0.5 * HUBER_BETA)
@@ -713,9 +732,8 @@
 
     chunks(steps, errors)
     loss[0, 0] = jnp.sum(head_sums[0])
-    wait_all(copies)
     for at in range(0, D, TILE):
-        grad[:, at : at + TILE] = dot_t(error_low[...], weight[at : at + TILE])
+        grad[:, at : at + TILE] = dot_t(error_low[...], weight[at : at + TILE, FF:])
 
     def back(k):
         rows = at_chunk(k)
@@ -743,13 +761,13 @@
         split_store(grads, columns, dot(turned[...], error_low[:, at : at + TILE]))
 
 
-def down(order, counts, work, stats, hidden, branch, active, vectors, rows_in, targets, pieces, after=()):
-    rows, owners = hidden.shape[0], len(pieces)
-    grads = split_shapes(owners, FF + D)
-    return launch(
-        functools.partial(down_kernel, owners, len(targets)),
+def down(order, counts, work, stats, hidden, branch, active, vectors, rows_in, targets, weight, after=()):
+    rows = hidden.shape[0]
+    grads = split_shapes(order.shape[0], FF + D)
+    return launch(
+        functools.partial(down_kernel, len(targets)),
         15,
-        in_specs=[NUMBERS, NUMBERS] + [ROW] * (8 + len(targets)) + [FAR] * owners,
+        in_specs=[NUMBERS, NUMBERS] + [ROW] * (9 + len(targets)),
         out_specs=[ROW] * len(grads) + [NUMBERS] + [ROW] * 4,
         out_shape=grads
         + [
@@ -760,24 +778,19 @@
             shape((4, 8, D), F32),
         ],
         scratch_shapes=[
-            pltpu.VMEM((D, D), LOW),
             pltpu.VMEM((rows, D), LOW),
             pltpu.VMEM((D, rows), LOW),
             pltpu.VMEM((D, rows), LOW),
-            pltpu.SemaphoreType.DMA((owners,)),
         ],
         after=after,
-    )(order, counts, work, stats, hidden, branch, *active, vectors, rows_in, *targets, *pieces)
-
-
-def pre_kernel(owners, order, grad_low, slope_a, slope_b, rows_in, *refs):
-    pieces, refs = refs[:owners], refs[owners:]
-    outs = 3 if owners > 1 else 1
+    )(order, counts, work, stats, hidden, branch, *active, vectors, rows_in, weight, *targets)
+
+
+def pre_kernel(order, grad_low, slope_a, slope_b, rows_in, weight, *refs):
+    outs = 3 if order.shape[0] > 1 else 1
     grads = refs[:outs]
-    pre_low, bias, weight, turned, spare, sems = refs[outs:]
-    copies = fetch(order, pieces, weight, sems, pl.ds(0, FF))
+    pre_low, bias, turned, spare = refs[outs:]
     place(order, rows_in[...], turned, spare)
-    wait_all(copies)
 
     half = slope_a.shape[1]
     for at in range(0, FF, TILE):
@@ -789,29 +802,25 @@
         split_store(grads, columns, dot(turned[...], pre_low[:, columns]))
 
 
-def pre(order, grad_low, slope, rows_in, pieces, after=()):
-    rows, owners = grad_low.shape[0], len(pieces)
-    grads = split_shapes(owners, FF)
-    return launch(
-        functools.partial(pre_kernel, owners),
+def pre(order, grad_low, slope, rows_in, weight, after=()):
+    rows = grad_low.shape[0]
+    grads = split_shapes(order.shape[0], FF)
+    return launch(
+        pre_kernel,
         12,
-        in_specs=[NUMBERS] + [ROW] * 4 + [FAR] * owners,
+        in_specs=[NUMBERS] + [ROW] * 5,
         out_specs=[ROW] * (len(grads) + 2),
         out_shape=grads + [shape((rows, FF), LOW), shape((8, FF), F32)],
         scratch_shapes=[
-            pltpu.VMEM((D, FF), LOW),
             pltpu.VMEM((D, rows), LOW),
             pltpu.VMEM((D, rows), LOW),
-            pltpu.SemaphoreType.DMA((owners,)),
         ],
         after=after,
-    )(order, grad_low, *slope, rows_in, *pieces)
-
-
-def out_kernel(owners, images, order, counts, masked, pre_low, grad, stats, hidden, attn, vectors, *refs):
-    pieces, refs = refs[:owners], refs[owners:]
-    heads_grad, table, sums, attn_low, weight, work, high, rest, sems = refs
-    wait_all(fetch(order, pieces, weight, sems))
+    )(order, grad_low, *slope, rows_in, weight)
+
+
+def out_kernel(images, counts, masked, pre_low, grad, stats, hidden, attn, vectors, weight, *refs):
+    heads_grad, table, sums, attn_low, work, high, rest = refs
     for at in range(0, D, TILE):
         work[:, at : at + TILE] = dot_t(pre_low[...], weight[at : at + TILE, D:])
     sums[...] = jnp.zeros_like(sums)
@@ -841,23 +850,21 @@
         table[...] = value if index == 0 else table[...] + value
 
 
-def out_back(order, counts, masked, pre_low, grad, stats, hidden, attn, vectors, pieces, after=()):
-    rows, owners = grad.shape[0], len(pieces)
-    return launch(
-        functools.partial(out_kernel, owners, masked.shape[0]),
+def out_back(counts, masked, pre_low, grad, stats, hidden, attn, vectors, weight, after=()):
+    rows = grad.shape[0]
+    return launch(
+        functools.partial(out_kernel, masked.shape[0]),
         14,
-        in_specs=[NUMBERS, NUMBERS] + [ROW] * 7 + [FAR] * owners,
+        in_specs=[NUMBERS] + [ROW] * 8,
         out_specs=[ROW] * 4,
         out_shape=[shape((rows, D), LOW), shape((NAT, D), F32), shape((4, 8, D), F32), shape((rows, D), LOW)],
         scratch_shapes=[
-            pltpu.VMEM((D, D + FF), LOW),
             pltpu.VMEM((rows, D), F32),
             pltpu.VMEM((rows, D), LOW),
             pltpu.VMEM((rows, D), LOW),
-            pltpu.SemaphoreType.DMA((owners,)),
         ],
         after=after,
-    )(order, counts, masked, pre_low, grad, stats, hidden, attn, vectors, *pieces)
+    )(counts, masked, pre_low, grad, stats, hidden, attn, vectors, weight)
 
 
 def attention_back_kernel(counts, queries, kv, heads_grad, masked, kv_low, table, sums, query_low):
@@ -955,11 +962,8 @@
     )(order, rows_in, kv_low, tab_in, table, heads, attn_low)
 
 
-def start_kernel(owners, images, order, counts, masked, kv_low, table, hidden_tab, hat, inv, hat_tab, inv_tab, vectors, head_sums, down_sums, up_bias, out_sums, qkv_sums, *refs):
-    pieces, refs = refs[:owners], refs[owners:]
-    start_low, small_low, weight, work, small, sums, sems = refs
-    copies = fetch(order, pieces, weight, sems, pl.ds(D + TAIL, 3 * D))
-    wait_all(copies)
+def start_kernel(images, counts, masked, kv_low, table, hidden_tab, hat, inv, hat_tab, inv_tab, vectors, head_sums, down_sums, up_bias, out_sums, qkv_sums, weight, *refs):
+    start_low, small_low, work, small, sums = refs
     for at in range(0, D, TILE):
         work[:, at : at + TILE] = dot_t(kv_low[...], weight[at : at + TILE, D:])
     both = high_rest(table[...])
@@ -1011,23 +1015,21 @@
     small_low[...] = small[...].T
 
 
-def start_back(order, counts, masked, kv_low, table, hidden_tab, hat, inv, hat_tab, inv_tab, vectors, head_sums, down_sums, up_bias, out_sums, qkv_sums, pieces, after=()):
-    rows, owners, images = kv_low.shape[0], len(pieces), masked.shape[0]
-    return launch(
-        functools.partial(start_kernel, owners, images),
+def start_back(counts, masked, kv_low, table, hidden_tab, hat, inv, hat_tab, inv_tab, vectors, head_sums, down_sums, up_bias, out_sums, qkv_sums, weight, after=()):
+    rows, images = kv_low.shape[0], masked.shape[0]
+    return launch(
+        functools.partial(start_kernel, images),
         8,
-        in_specs=[NUMBERS, NUMBERS] + [ROW] * 14 + [FAR] * owners,
+        in_specs=[NUMBERS] + [ROW] * 15,
         out_specs=[ROW] * 2,
         out_shape=[shape((rows, D), LOW), shape((D, TAIL), F32)],
         scratch_shapes=[
-            pltpu.VMEM((D, 3 * D), LOW),
             pltpu.VMEM((rows, D), F32),
             pltpu.VMEM((TAIL, D), F32),
             pltpu.VMEM((4, 8, D), F32),
-            pltpu.SemaphoreType.DMA((owners,)),
         ],
         after=after,
-    )(order, counts, masked, kv_low, table, hidden_tab, hat, inv, hat_tab, inv_tab, vectors, head_sums, down_sums, up_bias, out_sums, qkv_sums, *pieces)
+    )(counts, masked, kv_low, table, hidden_tab, hat, inv, hat_tab, inv_tab, vectors, head_sums, down_sums, up_bias, out_sums, qkv_sums, weight)
 
 
 def embed_back_kernel(images, blocks, order, pixels, start_low, small_low, *refs):
@@ -1177,7 +1179,7 @@
         rows = teacher_rows(teacher, near, at ^ 1, after)
         return rows, swap(rows, "layer", 1)
 
-    far_sum = lambda after: add([second_rows, far], [[[(0, None), (1, None)]]], [LOW], after, 1)[0]
+    far_sum = lambda after: far_sums(second_rows, far, after)
     return own_rows, near_sum, far_sum, second_rows
 
 
@@ -1206,40 +1208,46 @@
     own_rows, near_sum, far_sum, second_rows = targets_of(
         teacher[0, 0], masked_at[0], counts, [wide_embed], arrived(pieces_in, 1), arrived(pieces_in, 2)
     )
-    wide_up = part([(wide_master, 4 * D, D + FF)], [second_rows] + arrived(pieces_in, 4))
+    wide_up = part([(wide_master, 4 * D, D + FF)], [own_rows] + arrived(pieces_in, 3))
     pieces_up = gather_part(wide_up)
 
     hat_nat, inv_nat, in_nat, position, vectors, hat_tab, inv_tab, in_tab = embed(
-        order, counts, pixels[0], masked, pieces_in, after=[wide_up]
+        order, counts, pixels[0], masked, pieces_in, after=[wide_up, second_rows]
     )
     targets, waits = [own_rows], arrived(pieces_up, 2)
-    if far_sum:
+    if near_sum:
         near_rows, near = near_sum([in_tab])
-        far = far_sum([near_rows])
-        targets += [near, swap(far, "layer", 2)]
-        waits += [far]
-    kv, queries, heads = attention(order, counts, in_nat, masked, in_tab, vectors, pieces_in, after=waits)
+        far_a, far_b = far_sum([near_rows])
+        waits += [far_a]
+        far_a = swap(far_a, "layer", 2)
+        targets += [near, far_a]
+    kv, queries, heads, qkv_w = attention(
+        order, counts, in_nat, masked, in_tab, vectors, pieces_in, after=waits
+    )
     heads = heads.reshape(images * MOST, D)
+    arrivals = targets[2:]
+    if near_sum:
+        targets.append(swap(far_b, "layer", 2))
     wide_down = part([(tall_low, 0, FF), (wide_master, 5 * D + FF, D)], [heads] + arrived(pieces_up, 4))
     pieces_down = gather_part(wide_down)
-    attn, hidden, stats_mid, in_mid = mid(
-        order, counts, masked, heads, position, vectors, pieces_up, after=[wide_down]
-    )
-    active_a, slope_a = up(0, FF // 2, order, in_mid, vectors, pieces_up)
+    attn, hidden, stats_mid, in_mid, out_up_w = mid(
+        order, counts, masked, heads, position, vectors, pieces_up, after=[wide_down] + arrivals
+    )
+    active_a, slope_a = up(0, FF // 2, in_mid, vectors, out_up_w)
     active_b, slope_b = up(
-        FF // 2, FF // 2, order, in_mid, vectors, pieces_up, after=[active_a] + arrived(pieces_down, 2)
+        FF // 2, FF // 2, in_mid, vectors, out_up_w, after=[active_a] + arrived(pieces_down, 2)
     )
     active, slope = (active_a, active_b), (slope_a, slope_b)
-    branch, stats_out, in_out, work = head(order, active, hidden, vectors, pieces_down)
+    branch, stats_out, in_out, work, down_head_w = head(order, active, hidden, vectors, pieces_down)
     *down_g, loss, head_sums, grad, grad_low, down_sums = down(
-        order, counts, work, stats_out, hidden, branch, active, vectors, in_out, targets, pieces_down
+        order, counts, work, stats_out, hidden, branch, active, vectors, in_out, targets, down_head_w
     )
     down_p = Part(down_g)
-    *up_g, pre_low, up_bias = pre(order, grad_low, slope, in_mid, pieces_down)
+    *up_g, pre_low, up_bias = pre(order, grad_low, slope, in_mid, down_head_w)
     up_p = Part(up_g)
     down_s, up_s = Owned([down_p], False), Owned([up_p], False)
     heads_grad, hidden_tab, out_sums, attn_low = out_back(
-        order, counts, masked, pre_low, grad, stats_mid, hidden, attn, vectors, pieces_up,
+        counts, masked, pre_low, grad, stats_mid, hidden, attn, vectors, out_up_w,
         after=down_p.sums([pre_low]),
     )
     kv_low, table, qkv_sums = attention_back(
@@ -1253,8 +1261,8 @@
     )
     qkv_p = Part(qkv_g)
     start_low, small_low = start_back(
-        order, counts, masked, flat(kv_low), table, hidden_tab, flat(hat_nat), flat(inv_nat),
-        hat_tab, inv_tab, vectors, head_sums, down_sums, up_bias, out_sums, qkv_sums, pieces_in,
+        counts, masked, flat(kv_low), table, hidden_tab, flat(hat_nat), flat(inv_nat),
+        hat_tab, inv_tab, vectors, head_sums, down_sums, up_bias, out_sums, qkv_sums, qkv_w,
         after=up_s.shares([qkv_g[0]]),
     )
     embed_g = embed_back(

time: 344 us -> 338 us (0.983)
  Pallas kernels: 132 us -> 124 us
    pallas_call x37, Pallas kernels: 132 us -> 124 us  [call(): pl.pallas_call(body, grid_spec=spec, out_shape=out_shape, compiler_params...]
    unnamed x107 -> x93, local copies, waits for them, and re-layouts: 16.1 us -> 18.7 us
    ppermute x28 -> x29, waiting for transfers between devices: 52.3 us -> 51.3 us  [swap(): return lax.ppermute(value, axis, flip(lax.axis_size(axis), bit))]
    ppermute x28 -> x29, starting transfers between devices: 18.4 us -> 18.6 us  [swap(): return lax.ppermute(value, axis, flip(lax.axis_size(axis), bit))]
  transfers between devices with their start and end apart: 54 -> 55, of which waited for: 17 -> 16; matrix products, arithmetic and copies ran while one was open for 2% -> 3% of each run, Pallas kernels for 34% -> 33%
where the time goes in v1:
time: 338 us; the launch traced here: 332 us
  Pallas kernels  124 us (37%)
  waiting for transfers between devices  96.9 us (29%)
  starting transfers between devices  61.4 us (18%)
  local copies, waits for them, and re-layouts  26.4 us (8%)
  other arithmetic  18.4 us (5%)
  between operations  5.57 us (2%)
    pallas_call x37, Pallas kernels, call(): pl.pallas_call(body, grid_spec=spec, out_shape=out_shape, compiler_params...  124 us
    ppermute x29, waiting for transfers between devices, swap(): return lax.ppermute(value, axis, flip(lax.axis_size(axis), bit))  51.3 us
    unnamed x93, local copies, waits for them, and re-layouts  18.7 us
    ppermute x29, starting transfers between devices, swap(): return lax.ppermute(value, axis, flip(lax.axis_size(axis), bit))  18.6 us
    ppermute x12, waiting for transfers between devices, over_link(): lax.ppermute(value, 'dp', [(i, i ^ (4 if i & 1 else 2)) for i in range(8)])  17.4 us
    ppermute x12, starting transfers between devices, over_link(): lax.ppermute(value, 'dp', [(i, i ^ (4 if i & 1 else 2)) for i in range(8)])  14.9 us
    ppermute x6, waiting for transfers between devices, over_other(): lax.ppermute(value, 'dp', [(i, i ^ (2 if i & 1 else 4)) for i in range(8)])  14.4 us
    ppermute x2, starting transfers between devices, make(): return [lax.ppermute(sent, 'layer', [(0, 1), (3, 2)])]  10.3 us
  transfers between devices with their start and end apart: 55, of which 16 were waited for; matrix products, arithmetic and copies ran while one was open for 3% of the time, Pallas kernels for 33%

profile of v1, /device:TPU:0, one launch (start us, length us, event | category | flops | bytes accessed | tf_op | source)
XLA Modules:
  0.0 332.5 jit_solution(15376367946620280447)
XLA Ops:
  11.6 4.8 %dynamic-slice_bitcast_fusion = (bf16[5,196,768]{2,1,0:T(8,128)(2,1)S(1)}, bf16[5,196,768]{2,1,0:T(8,128)(2,1)}, bf16[5,196,768]{2,1,0:T(8,128)(2,1)S(1)}, bf16[5,196,768]{2,1,0:T(8,128)(2,1)}) fusion(bf16[1,1,20,196,768]{4,3,2,1,0:T(8,128)(2,1)} %param.11, s32[]{:T(128)S(6)} %select_n.48, s32[]{:T(128)S(6)} %select_n.46, s32[]{:T(128)S(6)} %select_n.45, ...), kind=kLoop, calls=%fused_computation.7 | loop fusion | bytes 12042256 | tf_op jit(solution)/shard_map/dynamic_slice | solution.py:382
  25.9 6.8 %collective-permute-done.2.refs_2_.refs_7_.refs_9_ = bf16[96,3328]{1,0:T(8,128)(2,1)} collective-permute-done((bf16[96,3328]{1,0:T(8,128)(2,1)}, bf16[96,3328]{1,0:T(8,128)(2,1)}, u32[]{:S(2)}, u32[]{:S(2)}) %collective-permute-start.2) | collective-permute-done | bytes 639008 | tf_op jit(solution)/shard_map/ppermute | solution.py:44
  37.2 7.3 %shard_map.198 = (f32[5,208,768]{2,1,0:T(8,128)}, f32[5,208,128]{2,1,0:T(8,128)}, bf16[5,208,768]{2,1,0:T(8,128)(2,1)S(1)}, bf16[208,768]{1,0:T(8,128)(2,1)S(1)}...) custom-call(s32[8]{0:T(128)S(1)} %stack.44.refs_0_, ...), custom_call_target="tpu_custom_call" | custom-call | flops 2500000000 | bytes 1048576 | tf_op jit(solution)/shard_map/pallas_call | solution.py:262
  46.4 5.6 %collective-permute-done.11.refs_1_ = bf16[720,768]{1,0:T(8,128)(2,1)S(1)} collective-permute-done((bf16[720,768]{1,0:T(8,128)(2,1)S(1)}, bf16[720,768]{1,0:T(8,128)(2,1)S(1)}, u32[]{:S(2)}, u32[]{:S(2)}) %collective-permute-start.11) | collective-permute-done | bytes 1105952 | tf_op jit(solution)/shard_map/ppermute | solution.py:40
  56.7 12.1 %shard_map.201 = (bf16[5,208,1536]{2,1,0:T(8,128)(2,1)}, bf16[5,144,768]{2,1,0:T(8,128)(2,1)}, bf16[5,144,768]{2,1,0:T(8,128)(2,1)S(1)}, bf16[768,2304]{1,0:T(8,128)(2,1)}) custom-call(s32[8]{0:T(128)S(1)} %stack.44.refs_0_, s32[5]{0:T(128)S(1)} %bitcast.63, bf16[5,208,768]{2,1,0:T(8,128)(2,1)S(1)} %get-tuple-element.88.refs_2_, s32[5,1,196]{2,1,0:T(1,128)S(1)} %bitcast.55, ...), custom_call_target="tpu_custom_call" | custom-call | flops 30000001024 | bytes 1048576 | tf_op jit(solution)/shard_map/pallas_call | solution.py:262
  68.9 5.2 %collective-permute-done.14.refs_3_.refs_10_ = bf16[96,3840]{1,0:T(8,128)(2,1)S(1)} collective-permute-done((bf16[96,3840]{1,0:T(8,128)(2,1)S(1)}, bf16[96,3840]{1,0:T(8,128)(2,1)S(1)}, u32[]{:S(2)}, u32[]{:S(2)}) %collective-permute-start.14) | collective-permute-done | bytes 737312 | tf_op jit(solution)/shard_map/ppermute | solution.py:48
  74.7 4.5 %collective-permute-done.18.refs_15_.refs_13_ = bf16[720,384]{1,0:T(8,128)(2,1)S(1)} collective-permute-done((bf16[720,384]{1,0:T(8,128)(2,1)S(1)}, bf16[720,384]{1,0:T(8,128)(2,1)S(1)}, u32[]{:S(2)}, u32[]{:S(2)}) %collective-permute-start.18) | collective-permute-done | bytes 552992 | tf_op jit(solution)/shard_map/ppermute | solution.py:40
  81.5 3.4 %collective-permute-start.27 = (bf16[720,384]{1,0:T(8,128)(2,1)S(1)}, bf16[720,384]{1,0:T(8,128)(2,1)S(1)}, u32[]{:S(2)}, u32[]{:S(2)}) collective-permute-start(bf16[720,384]{1,0:T(8,128)(2,1)S(1)} %get-tuple-element.104), channel_id=1, source_target_pairs={{0,16},{8,24},{16,0},{24,8},{1,17},{9,25},{17,1},{25,9},{2,18},{10... | collective-permute-start | bytes 1658888 | tf_op jit(solution)/shard_map/ppermute | solution.py:40
  85.4 5.2 %collective-permute-done.19.refs_4_.refs_7_ = bf16[96,3840]{1,0:T(8,128)(2,1)S(1)} collective-permute-done((bf16[96,3840]{1,0:T(8,128)(2,1)S(1)}, bf16[96,3840]{1,0:T(8,128)(2,1)S(1)}, u32[]{:S(2)}, u32[]{:S(2)}) %collective-permute-start.19) | collective-permute-done | bytes 737312 | tf_op jit(solution)/shard_map/ppermute | solution.py:44
  91.2 4.7 %shard_map.203 = (f32[720,768]{1,0:T(8,128)S(1)}, f32[720,768]{1,0:T(8,128)S(1)}, f32[720,128]{1,0:T(8,128)S(1)}, bf16[720,768]{1,0:T(8,128)(2,1)S(1)}, bf16[768,3840]{1,0:T(8,128)(2,1)S(1)}) custom-call(s32[8]{0:T(128)S(1)} %stack.44.refs_0_, s32[5]{0:T(128)S(1)} %bitcast.64, s32[5,1,196]{2,1,0:T(1,128)S(1)} %bitcast.56, bf16[720,768]{1,0:T(8,128)(2,1)S(1)} %bitcast.50, ...), custom_call_target="tpu_custom_call" | custom-call | flops 15000000512 | bytes 1048576 | tf_op jit(solution)/shard_map/pallas_call | solution.py:262
  95.9 5.1 %shard_map.204 = (bf16[720,1536]{1,0:T(8,128)(2,1)S(1)}, bf16[720,1536]{1,0:T(8,128)(2,1)S(1)}) custom-call(bf16[720,768]{1,0:T(8,128)(2,1)S(1)} %get-tuple-element.94.refs_0_.refs_4_, f32[24,768]{1,0:T(8,128)S(1)} %get-tuple-element.90.refs_5_.refs_1_.refs_4_.refs_8_.refs_7_.refs_9_, bf16[768,3840]{1,0:T(8,128)(2,1)S(1)} %get-tuple-element.95.refs_2_.refs_8_), custom_call_target="tpu_custom_call" | custom-call | flops 17500000256 | bytes 1048576 | tf_op jit(solution)/shard_map/pallas_call | solution.py:262
  101.0 4.6 %collective-permute-done.21.refs_8_ = bf16[96,3840]{1,0:T(8,128)(2,1)S(1)} collective-permute-done((bf16[96,3840]{1,0:T(8,128)(2,1)S(1)}, bf16[96,3840]{1,0:T(8,128)(2,1)S(1)}, u32[]{:S(2)}, u32[]{:S(2)}) %collective-permute-start.21) | collective-permute-done | bytes 737312 | tf_op jit(solution)/shard_map/ppermute | solution.py:44
  106.6 5.1 %shard_map.205 = (bf16[720,1536]{1,0:T(8,128)(2,1)S(1)}, bf16[720,1536]{1,0:T(8,128)(2,1)S(1)}) custom-call(bf16[720,768]{1,0:T(8,128)(2,1)S(1)} %get-tuple-element.94.refs_0_.refs_4_, f32[24,768]{1,0:T(8,128)S(1)} %get-tuple-element.90.refs_5_.refs_1_.refs_4_.refs_8_.refs_7_.refs_9_, bf16[768,3840]{1,0:T(8,128)(2,1)S(1)} %get-tuple-element.95.refs_2_.refs_8_, ...), custom_call_target="tpu_custom_call" | custom-call | flops 17500000256 | bytes 1048576 | tf_op jit(solution)/shard_map/pallas_call | solution.py:262
  111.7 8.9 %shard_map.206 = (f32[720,768]{1,0:T(8,128)S(1)}, f32[720,128]{1,0:T(8,128)S(1)}, bf16[720,768]{1,0:T(8,128)(2,1)S(1)}, f32[720,768]{1,0:T(8,128)S(1)}, bf16[768,3840]{1,0:T(8,128)(2,1)S(1)}) custom-call(s32[8]{0:T(128)S(1)} %stack.44.refs_0_, bf16[720,1536]{1,0:T(8,128)(2,1)S(1)} %get-tuple-element.96.refs_3_.refs_1_.refs_6_, ...), custom_call_target="tpu_custom_call" | custom-call | flops 24999999488 | bytes 1048576 | tf_op jit(solution)/shard_map/pallas_call | solution.py:262
  120.7 12.2 %shard_map.207 = (bf16[2,96,3840]{2,1,0:T(8,128)(2,1)S(1)}, bf16[3,96,3840]{2,1,0:T(8,128)(2,1)S(1)}, bf16[3,96,3840]{2,1,0:T(8,128)(2,1)S(1)}, f32[1,1]{1,0:T(1...) custom-call(s32[8]{0:T(128)S(1)} %stack.44.refs_0_, ...), custom_call_target="tpu_custom_call" | custom-call | flops 37499998208 | bytes 1048576 | tf_op jit(solution)/shard_map/pallas_call | solution.py:262
  136.9 8.9 %shard_map.208 = (bf16[2,96,3072]{2,1,0:T(8,128)(2,1)S(1)}, bf16[3,96,3072]{2,1,0:T(8,128)(2,1)S(1)}, bf16[3,96,3072]{2,1,0:T(8,128)(2,1)S(1)}, bf16[720,3072]{1,0:T(8,128)(2,1)S(1)}, f32[8,3072]{1,0:T(8,128)S(1)}) custom-call(s32[8]{0:T(128)S(1)} %stack.44.refs_0_, bf16[720,768]{1,0:T(8,128)(2,1)S(1)} %get-tuple-element.108.refs_1_, ...), custom_call_target="tpu_custom_call" | custom-call | flops 30000001024 | bytes 1048576 | tf_op jit(solution)/shard_map/pallas_call | solution.py:262
  149.1 12.4 %shard_map.210 = (bf16[720,768]{1,0:T(8,128)(2,1)S(1)}, f32[208,768]{1,0:T(8,128)S(1)}, f32[4,8,768]{2,1,0:T(8,128)S(1)}, bf16[720,768]{1,0:T(8,128)(2,1)S(1)}) custom-call(s32[5]{0:T(128)S(1)} %bitcast.66, s32[5,1,196]{2,1,0:T(1,128)S(1)} %bitcast.57, bf16[720,3072]{1,0:T(8,128)(2,1)S(1)} %get-tuple-element.111.refs_2_, f32[720,768]{1,0:T(8,128)S(1)} %copy-done.35, ...), custom_call_target="tpu_custom_call" | custom-call | flops 35000000512 | bytes 1048576 | tf_op jit(solution)/shard_map/pallas_call | solution.py:262
  169.1 15.0 %shard_map.213 = (bf16[5,208,1536]{2,1,0:T(8,128)(2,1)S(1)}, f32[208,768]{1,0:T(8,128)S(1)}, f32[2,8,768]{2,1,0:T(8,128)S(1)}) custom-call(s32[5]{0:T(128)S(1)} %bitcast.67, bf16[5,144,768]{2,1,0:T(8,128)(2,1)S(1)} %copy-done.38, bf16[5,208,1536]{2,1,0:T(8,128)(2,1)S(1)} %copy-done.33, bf16[5,144,768]{2,1,0:T(8,128)(2,1)S(1)} %bitcast.46, ...), custom_call_target="tpu_custom_call" | custom-call | flops 37499998208 | bytes 1048576 | tf_op jit(solution)/shard_map/pallas_call | solution.py:262
  186.6 3.5 %collective-permute-start.41 = (bf16[96,3840]{1,0:T(8,128)(2,1)S(1)}, bf16[96,3840]{1,0:T(8,128)(2,1)S(1)}, u32[]{:S(2)}, u32[]{:S(2)}) collective-permute-start(bf16[96,3840]{1,0:T(8,128)(2,1)S(1)} %get-tuple-element.133.refs_8_), channel_id=1, source_target_pairs={{0,8},{24,16},{1,9},{25,17},{2,10},{26,18},{3,11},{27,19},{4,12},{... | collective-permute-start | bytes 2211848 | tf_op jit(solution)/shard_map/ppermute | solution.py:171
  190.1 5.9 %shard_map.216 = (bf16[2,96,3072]{2,1,0:T(8,128)(2,1)S(1)}, bf16[3,96,3072]{2,1,0:T(8,128)(2,1)S(1)}, bf16[3,96,3072]{2,1,0:T(8,128)(2,1)S(1)}) custom-call(s32[8]{0:T(128)S(1)} %stack.44.refs_0_, bf16[1040,768]{1,0:T(8,128)(2,1)S(1)} %bitcast.72, bf16[1040,1536]{1,0:T(8,128)(2,1)S(1)} %bitcast.70, bf16[208,768]{1,0:T(8,128)(2,1)S(1)} %copy-done.28, ...), custom_call_target="tpu_custom_call" | custom-call | flops 17500000256 | bytes 1048576 | tf_op jit(solution)/shard_map/pallas_call | solution.py:262
  198.5 6.0 %shard_map.218 = (bf16[1040,768]{1,0:T(8,128)(2,1)S(1)}, f32[768,256]{1,0:T(8,128)S(1)}) custom-call(s32[5]{0:T(128)S(1)} %bitcast.68, s32[5,1,196]{2,1,0:T(1,128)S(1)} %bitcast.59, bf16[1040,1536]{1,0:T(8,128)(2,1)S(1)} %bitcast.71, f32[208,768]{1,0:T(8,128)S(1)} %get-tuple-element.130.refs_3_.refs_4_, f32[208,768]{1,0:T(8,128)S(1)} %get-tuple-element.140.refs_4_, ...), custom_call_target="tpu_custom_call" | custom-call | flops 20000000000 | bytes 1048576 | tf_op jit(solution)/shard_map/pallas_call | solution.py:262
  212.8 6.8 %collective-permute-start.46 = (bf16[96,3072]{1,0:T(8,128)(2,1)}, bf16[96,3072]{1,0:T(8,128)(2,1)S(1)}, u32[]{:S(2)}, u32[]{:S(2)}) collective-permute-start(bf16[96,3072]{1,0:T(8,128)(2,1)} %get-tuple-element.152.refs_17_), channel_id=1, source_target_pairs={{0,8},{24,16},{1,9},{25,17},{2,10},{26,18},{3,11},{27,19},{4,12},{... | collective-permute-start | bytes 1769480 | tf_op jit(solution)/shard_map/ppermute | solution.py:171
  219.7 7.1 %collective-permute-done.39.refs_1_ = bf16[96,3072]{1,0:T(8,128)(2,1)S(1)} collective-permute-done((bf16[96,3072]{1,0:T(8,128)(2,1)S(1)}, bf16[96,3072]{1,0:T(8,128)(2,1)S(1)}, u32[]{:S(2)}, u32[]{:S(2)}) %collective-permute-start.39) | collective-permute-done | bytes 589856 | tf_op jit(solution)/shard_map/ppermute | solution.py:48
  229.8 4.4 %all-to-all-start = ((bf16[4,96,1024]{2,1,0:T(8,128)(2,1)}), bf16[4,96,1024]{2,1,0:T(8,128)(2,1)}, u32[]{:S(2)}, u32[]{:S(2)}) async-start(bf16[4,96,1024]{2,1,0:T(8,128)(2,1)} %shard_map.223.refs_2_), calls=%async_computation | async-start | bytes 1572864 | tf_op jit(solution)/shard_map/all_to_all | solution.py:144
  241.7 4.9 %all-to-all-done.refs_4_ = bf16[4,96,1024]{2,1,0:T(8,128)(2,1)} async-done(((bf16[4,96,1024]{2,1,0:T(8,128)(2,1)}), bf16[4,96,1024]{2,1,0:T(8,128)(2,1)}, u32[]{:S(2)}, u32[]{:S(2)}) %all-to-all-start) | async-done | bytes 786464 | tf_op jit(solution)/shard_map/all_to_all | solution.py:144
  256.0 13.4 %collective-permute-done.47.refs_1_ = bf16[48,4096]{1,0:T(8,128)(2,1)S(1)} collective-permute-done((bf16[48,4096]{1,0:T(8,128)(2,1)}, bf16[48,4096]{1,0:T(8,128)(2,1)S(1)}, u32[]{:S(2)}, u32[]{:S(2)}) %collective-permute-start.47) | collective-permute-done | bytes 393248 | tf_op jit(solution)/shard_map/ppermute | solution.py:40
  271.1 17.9 %collective-permute-done.49.refs_1_ = bf16[48,4096]{1,0:T(8,128)(2,1)S(1)} collective-permute-done((bf16[48,4096]{1,0:T(8,128)(2,1)S(1)}, bf16[48,4096]{1,0:T(8,128)(2,1)S(1)}, u32[]{:S(2)}, u32[]{:S(2)}) %collective-permute-start.49) | collective-permute-done | bytes 393248 | tf_op jit(solution)/shard_map/ppermute | solution.py:40
  290.2 9.9 %collective-permute-done.50 = bf16[48,4096]{1,0:T(8,128)(2,1)S(1)} collective-permute-done((bf16[48,4096]{1,0:T(8,128)(2,1)S(1)}, bf16[48,4096]{1,0:T(8,128)(2,1)S(1)}, u32[]{:S(2)}, u32[]{:S(2)}) %collective-permute-start.50) | collective-permute-done | bytes 393248 | tf_op jit(solution)/shard_map/ppermute | solution.py:40
  306.4 4.0 %all-to-all-start.1 = ((f32[32,1,3]{2,1,0:T(1,128)}), f32[32,1,3]{2,1,0:T(1,128)}, u32[]{:S(2)}, u32[]{:S(2)}) async-start(f32[32,1,3]{2,1,0:T(1,128)} %broadcast_in_dim.19), calls=%async_computation.1 | async-start | bytes 32768 | tf_op jit(solution)/shard_map/all_to_all | solution.py:223
  311.0 6.3 %all-to-all-done.1 = f32[32,1,3]{2,1,0:T(1,128)} async-done(((f32[32,1,3]{2,1,0:T(1,128)}), f32[32,1,3]{2,1,0:T(1,128)}, u32[]{:S(2)}, u32[]{:S(2)}) %all-to-all-start.1) | async-done | bytes 416 | tf_op jit(solution)/shard_map/all_to_all | solution.py:223
  320.1 5.1 %fusion.4 = (bf16[3287,96]{0,1:T(8,128)(2,1)}, f32[3287,96]{0,1:T(8,128)}, f32[3287,96]{0,1:T(8,128)}, f32[3287,96]{0,1:T(8,128)}, f32[3287,96]{0,1:T(8,128)S(1)}) fusion(f32[3287,96]{0,1:T(8,128)} %param.17, f32[3287]{0:T(1024)} %fusion.2, f32[3287,96]{0,1:T(8,128)} %param.18, f32[3287,96]{0,1:T(8,128)} %param.19, f32[96,215]{1,0:T(8,128)} %copy-done.45, ...), kind=kLoop, calls=%fused_computation.41 | loop fusion | flops 5679936 | bytes 10741920 | tf_op jit(solution)/shard_map/convert_element_type | solution.py:1309
  326.5 4.7 %fusion.6 = (bf16[96,7680]{1,0:T(8,128)(2,1)}, f32[96,7680]{1,0:T(8,128)}, f32[96,7680]{1,0:T(8,128)}, f32[96,7680]{1,0:T(8,128)}) fusion(f32[96,7680]{1,0:T(8,128)S(1)} %copy-done.2, f32[96,768]{1,0:T(8,128)S(1)} %copy-done.42, f32[96,3072]{1,0:T(8,128)S(1)} %select_convert_fusion.1, f32[96,3072]{1,0:T(8,128)S(1)} %slice.57, f32[96,768]{1,0:T(8,128)S(1)} %copy-done.44, ...), kind=kLoop, calls=%fused_computation.42 | loop fusion | flops 14745600 | bytes 22118404 | tf_op jit(solution)/shard_map/convert_element_type | solution.py:1305
  (243 shorter events, 95.4 us)
Async XLA Ops:
  7.2 14.7 %collective-permute-start.7 = (s32[5,197]{1,0:T(8,128)S(1)}, s32[5,197]{1,0:T(8,128)S(1)}, u32[]{:S(2)}, u32[]{:S(2)}) collective-permute-start(s32[5,197]{1,0:T(8,128)S(1)} %pad_add_fusion), channel_id=1, source_target_pairs={{0,16},{8,24},{16,0},{24,8},{1,17},{9,25},{17,1},{25,9},{2,18},{10... | collective-permute-start | bytes 11828 | tf_op jit(solution)/shard_map/ppermute | solution.py:40
  16.4 16.3 %collective-permute-start.2 = (bf16[96,3328]{1,0:T(8,128)(2,1)}, bf16[96,3328]{1,0:T(8,128)(2,1)}, u32[]{:S(2)}, u32[]{:S(2)}) collective-permute-start(bf16[96,3328]{1,0:T(8,128)(2,1)} %collective-permute-done.refs_4_.refs_5_.refs_7_), channel_id=1, source_target_pairs={{0,2},{1,5},{2,0},{3,7},{4,6},{5,1},{6,4},{7,3},{8,10},{9,13},{10,... | collective-permute-start | bytes 1916936 | tf_op jit(solution)/shard_map/ppermute | solution.py:44
  16.9 15.8 %collective-permute-start.3 = (bf16[96,3328]{1,0:T(8,128)(2,1)}, bf16[96,3328]{1,0:T(8,128)(2,1)}, u32[]{:S(2)}, u32[]{:S(2)}) collective-permute-start(bf16[96,3328]{1,0:T(8,128)(2,1)} %collective-permute-done.1.refs_5_.refs_6_.refs_8_), channel_id=1, source_target_pairs={{0,4},{1,3},{2,6},{3,1},{4,0},{5,7},{6,2},{7,5},{8,12},{9,11},{10,... | collective-permute-start | bytes 1916936 | tf_op jit(solution)/shard_map/ppermute | solution.py:48
  25.1 26.8 %collective-permute-start.11 = (bf16[720,768]{1,0:T(8,128)(2,1)S(1)}, bf16[720,768]{1,0:T(8,128)(2,1)S(1)}, u32[]{:S(2)}, u32[]{:S(2)}) collective-permute-start(bf16[720,768]{1,0:T(8,128)(2,1)S(1)} %shard_map.196.refs_3_), channel_id=1, source_target_pairs={{0,8},{8,0},{16,24},{24,16},{1,9},{9,1},{17,25},{25,17},{2,10},{10... | collective-permute-start | bytes 3317768 | tf_op jit(solution)/shard_map/ppermute | solution.py:40
  33.7 21.0 %collective-permute-start.10 = (bf16[96,3840]{1,0:T(8,128)(2,1)S(1)}, bf16[96,3840]{1,0:T(8,128)(2,1)S(1)}, u32[]{:S(2)}, u32[]{:S(2)}) collective-permute-start(bf16[96,3840]{1,0:T(8,128)(2,1)S(1)} %shard_map.195.refs_12_.refs_6_), channel_id=1, source_target_pairs={{0,2},{1,5},{2,0},{3,7},{4,6},{5,1},{6,4},{7,3},{8,10},{9,13},{10,... | collective-permute-start | bytes 2211848 | tf_op jit(solution)/shard_map/ppermute | solution.py:44
  35.3 20.3 %collective-permute-start.12 = (bf16[96,3840]{1,0:T(8,128)(2,1)S(1)}, bf16[96,3840]{1,0:T(8,128)(2,1)S(1)}, u32[]{:S(2)}, u32[]{:S(2)}) collective-permute-start(bf16[96,3840]{1,0:T(8,128)(2,1)S(1)} %shard_map.195.refs_12_.refs_6_), channel_id=1, source_target_pairs={{0,1},{1,0},{2,3},{3,2},{4,5},{5,4},{6,7},{7,6},{8,9},{9,8},{10,11... | collective-permute-start | bytes 2211848 | tf_op jit(solution)/shard_map/ppermute | solution.py:40
  52.2 26.9 %collective-permute-start.18 = (bf16[720,384]{1,0:T(8,128)(2,1)S(1)}, bf16[720,384]{1,0:T(8,128)(2,1)S(1)}, u32[]{:S(2)}, u32[]{:S(2)}) collective-permute-start(bf16[720,384]{1,0:T(8,128)(2,1)S(1)} %get-tuple-element.91.refs_15_), channel_id=1, source_target_pairs={{0,16},{8,24},{16,0},{24,8},{1,17},{9,25},{17,1},{25,9},{2,18},{10... | collective-permute-start | bytes 1658888 | tf_op jit(solution)/shard_map/ppermute | solution.py:40
  54.7 19.3 %collective-permute-start.14 = (bf16[96,3840]{1,0:T(8,128)(2,1)S(1)}, bf16[96,3840]{1,0:T(8,128)(2,1)S(1)}, u32[]{:S(2)}, u32[]{:S(2)}) collective-permute-start(bf16[96,3840]{1,0:T(8,128)(2,1)S(1)} %collective-permute-done.10.refs_14_.refs_8_), channel_id=1, source_target_pairs={{0,4},{1,3},{2,6},{3,1},{4,0},{5,7},{6,2},{7,5},{8,12},{9,11},{10,... | collective-permute-start | bytes 2211848 | tf_op jit(solution)/shard_map/ppermute | solution.py:48
  55.2 25.5 %collective-permute-start.15 = (bf16[96,3840]{1,0:T(8,128)(2,1)S(1)}, bf16[96,3840]{1,0:T(8,128)(2,1)S(1)}, u32[]{:S(2)}, u32[]{:S(2)}) collective-permute-start(bf16[96,3840]{1,0:T(8,128)(2,1)S(1)} %collective-permute-done.10.refs_14_.refs_8_), channel_id=1, source_target_pairs={{0,1},{1,0},{2,3},{3,2},{4,5},{5,4},{6,7},{7,6},{8,9},{9,8},{10,11... | collective-permute-start | bytes 2211848 | tf_op jit(solution)/shard_map/ppermute | solution.py:40
  55.6 25.1 %collective-permute-start.13 = (bf16[96,3840]{1,0:T(8,128)(2,1)S(1)}, bf16[96,3840]{1,0:T(8,128)(2,1)S(1)}, u32[]{:S(2)}, u32[]{:S(2)}) collective-permute-start(bf16[96,3840]{1,0:T(8,128)(2,1)S(1)} %collective-permute-done.12.refs_7_), channel_id=1, source_target_pairs={{0,2},{1,5},{2,0},{3,7},{4,6},{5,1},{6,4},{7,3},{8,10},{9,13},{10,... | collective-permute-start | bytes 2211848 | tf_op jit(solution)/shard_map/ppermute | solution.py:44
  80.8 39.9 %collective-permute-start.26 = (bf16[720,768]{1,0:T(8,128)(2,1)S(1)}, bf16[720,768]{1,0:T(8,128)(2,1)S(1)}, u32[]{:S(2)}, u32[]{:S(2)}) collective-permute-start(bf16[720,768]{1,0:T(8,128)(2,1)S(1)} %shard_map.199.refs_2_), channel_id=1, source_target_pairs={{0,8},{8,0},{16,24},{24,16},{1,9},{9,1},{17,25},{25,17},{2,10},{10... | collective-permute-start | bytes 3317768 | tf_op jit(solution)/shard_map/ppermute | solution.py:40
  81.5 39.1 %collective-permute-start.27 = (bf16[720,384]{1,0:T(8,128)(2,1)S(1)}, bf16[720,384]{1,0:T(8,128)(2,1)S(1)}, u32[]{:S(2)}, u32[]{:S(2)}) collective-permute-start(bf16[720,384]{1,0:T(8,128)(2,1)S(1)} %get-tuple-element.104), channel_id=1, source_target_pairs={{0,16},{8,24},{16,0},{24,8},{1,17},{9,25},{17,1},{25,9},{2,18},{10... | collective-permute-start | bytes 1658888 | tf_op jit(solution)/shard_map/ppermute | solution.py:40
  84.9 20.7 %collective-permute-start.21 = (bf16[96,3840]{1,0:T(8,128)(2,1)S(1)}, bf16[96,3840]{1,0:T(8,128)(2,1)S(1)}, u32[]{:S(2)}, u32[]{:S(2)}) collective-permute-start(bf16[96,3840]{1,0:T(8,128)(2,1)S(1)} %collective-permute-done.20.refs_6_), channel_id=1, source_target_pairs={{0,2},{1,5},{2,0},{3,7},{4,6},{5,1},{6,4},{7,3},{8,10},{9,13},{10,... | collective-permute-start | bytes 2211848 | tf_op jit(solution)/shard_map/ppermute | solution.py:44
  90.7 15.0 %collective-permute-start.22 = (bf16[96,3840]{1,0:T(8,128)(2,1)S(1)}, bf16[96,3840]{1,0:T(8,128)(2,1)S(1)}, u32[]{:S(2)}, u32[]{:S(2)}) collective-permute-start(bf16[96,3840]{1,0:T(8,128)(2,1)S(1)} %collective-permute-done.19.refs_4_.refs_7_), channel_id=1, source_target_pairs={{0,4},{1,3},{2,6},{3,1},{4,0},{5,7},{6,2},{7,5},{8,12},{9,11},{10,... | collective-permute-start | bytes 2211848 | tf_op jit(solution)/shard_map/ppermute | solution.py:48
  145.9 15.6 %collective-permute-start.31 = (bf16[3,96,3072]{2,1,0:T(8,128)(2,1)S(1)}, bf16[3,96,3072]{2,1,0:T(8,128)(2,1)S(1)}, u32[]{:S(2)}, u32[]{:S(2)}) collective-permute-start(bf16[3,96,3072]{2,1,0:T(8,128)(2,1)S(1)} %get-tuple-element.125), channel_id=1, source_target_pairs={{0,1},{1,0},{2,3},{3,2},{4,5},{5,4},{6,7},{7,6},{8,9},{9,8},{10,11... | collective-permute-start | bytes 5308424 | tf_op jit(solution)/shard_map/ppermute | solution.py:40
  147.0 19.2 %collective-permute-start.29 = (bf16[96,3840]{1,0:T(8,128)(2,1)S(1)}, bf16[96,3840]{1,0:T(8,128)(2,1)S(1)}, u32[]{:S(2)}, u32[]{:S(2)}) collective-permute-start(bf16[96,3840]{1,0:T(8,128)(2,1)S(1)} %get-tuple-element.119.refs_11_), channel_id=1, source_target_pairs={{0,4},{1,3},{2,6},{3,1},{4,0},{5,7},{6,2},{7,5},{8,12},{9,11},{10,... | collective-permute-start | bytes 2211848 | tf_op jit(solution)/shard_map/ppermute | solution.py:48
  147.6 19.3 %collective-permute-start.30 = (bf16[96,3840]{1,0:T(8,128)(2,1)S(1)}, bf16[96,3840]{1,0:T(8,128)(2,1)S(1)}, u32[]{:S(2)}, u32[]{:S(2)}) collective-permute-start(bf16[96,3840]{1,0:T(8,128)(2,1)S(1)} %get-tuple-element.118.refs_10_), channel_id=1, source_target_pairs={{0,2},{1,5},{2,0},{3,7},{4,6},{5,1},{6,4},{7,3},{8,10},{9,13},{10,... | collective-permute-start | bytes 2211848 | tf_op jit(solution)/shard_map/ppermute | solution.py:44
  161.9 22.2 %collective-permute-start.34 = (bf16[96,3072]{1,0:T(8,128)(2,1)S(1)}, bf16[96,3072]{1,0:T(8,128)(2,1)S(1)}, u32[]{:S(2)}, u32[]{:S(2)}) collective-permute-start(bf16[96,3072]{1,0:T(8,128)(2,1)S(1)} %get-tuple-element.128.refs_9_), channel_id=1, source_target_pairs={{0,4},{1,3},{2,6},{3,1},{4,0},{5,7},{6,2},{7,5},{8,12},{9,11},{10,... | collective-permute-start | bytes 1769480 | tf_op jit(solution)/shard_map/ppermute | solution.py:48
  163.5 20.6 %collective-permute-start.35 = (bf16[96,3072]{1,0:T(8,128)(2,1)S(1)}, bf16[96,3072]{1,0:T(8,128)(2,1)S(1)}, u32[]{:S(2)}, u32[]{:S(2)}) collective-permute-start(bf16[96,3072]{1,0:T(8,128)(2,1)S(1)} %get-tuple-element.127.refs_8_), channel_id=1, source_target_pairs={{0,2},{1,5},{2,0},{3,7},{4,6},{5,1},{6,4},{7,3},{8,10},{9,13},{10,... | collective-permute-start | bytes 1769480 | tf_op jit(solution)/shard_map/ppermute | solution.py:44
  167.2 18.8 %collective-permute-start.32 = (bf16[96,3840]{1,0:T(8,128)(2,1)S(1)}, bf16[96,3840]{1,0:T(8,128)(2,1)S(1)}, u32[]{:S(2)}, u32[]{:S(2)}) collective-permute-start(bf16[96,3840]{1,0:T(8,128)(2,1)S(1)} %get-tuple-element.122.refs_5_), channel_id=1, source_target_pairs={{0,2},{1,5},{2,0},{3,7},{4,6},{5,1},{6,4},{7,3},{8,10},{9,13},{10,... | collective-permute-start | bytes 2211848 | tf_op jit(solution)/shard_map/ppermute | solution.py:44
  168.9 17.2 %collective-permute-start.33 = (bf16[96,3840]{1,0:T(8,128)(2,1)S(1)}, bf16[96,3840]{1,0:T(8,128)(2,1)S(1)}, u32[]{:S(2)}, u32[]{:S(2)}) collective-permute-start(bf16[96,3840]{1,0:T(8,128)(2,1)S(1)} %get-tuple-element.123.refs_6_), channel_id=1, source_target_pairs={{0,1},{1,0},{2,3},{3,2},{4,5},{5,4},{6,7},{7,6},{8,9},{9,8},{10,11... | collective-permute-start | bytes 2211848 | tf_op jit(solution)/shard_map/ppermute | solution.py:40
  186.6 19.5 %collective-permute-start.41 = (bf16[96,3840]{1,0:T(8,128)(2,1)S(1)}, bf16[96,3840]{1,0:T(8,128)(2,1)S(1)}, u32[]{:S(2)}, u32[]{:S(2)}) collective-permute-start(bf16[96,3840]{1,0:T(8,128)(2,1)S(1)} %get-tuple-element.133.refs_8_), channel_id=1, source_target_pairs={{0,8},{24,16},{1,9},{25,17},{2,10},{26,18},{3,11},{27,19},{4,12},{... | collective-permute-start | bytes 2211848 | tf_op jit(solution)/shard_map/ppermute | solution.py:171
  210.5 18.3 %collective-permute-start.44 = (bf16[4,96,1024]{2,1,0:T(8,128)(2,1)S(1)}, bf16[4,96,1024]{2,1,0:T(8,128)(2,1)S(1)}, u32[]{:S(2)}, u32[]{:S(2)}) collective-permute-start(bf16[4,96,1024]{2,1,0:T(8,128)(2,1)S(1)} %get-tuple-element.161), channel_id=1, source_target_pairs={{0,1},{1,0},{2,3},{3,2},{4,5},{5,4},{6,7},{7,6},{8,9},{9,8},{10,11... | collective-permute-start | bytes 2359304 | tf_op jit(solution)/shard_map/ppermute | solution.py:40
  210.6 16.1 %collective-permute-start.39 = (bf16[96,3072]{1,0:T(8,128)(2,1)S(1)}, bf16[96,3072]{1,0:T(8,128)(2,1)S(1)}, u32[]{:S(2)}, u32[]{:S(2)}) collective-permute-start(bf16[96,3072]{1,0:T(8,128)(2,1)S(1)} %get-tuple-element.155.refs_6_), channel_id=1, source_target_pairs={{0,4},{1,3},{2,6},{3,1},{4,0},{5,7},{6,2},{7,5},{8,12},{9,11},{10,... | collective-permute-start | bytes 1769480 | tf_op jit(solution)/shard_map/ppermute | solution.py:48
  211.2 15.6 %collective-permute-start.40 = (bf16[96,3072]{1,0:T(8,128)(2,1)S(1)}, bf16[96,3072]{1,0:T(8,128)(2,1)S(1)}, u32[]{:S(2)}, u32[]{:S(2)}) collective-permute-start(bf16[96,3072]{1,0:T(8,128)(2,1)S(1)} %get-tuple-element.156.refs_5_), channel_id=1, source_target_pairs={{0,2},{1,5},{2,0},{3,7},{4,6},{5,1},{6,4},{7,3},{8,10},{9,13},{10,... | collective-permute-start | bytes 1769480 | tf_op jit(solution)/shard_map/ppermute | solution.py:44
  212.1 25.4 %collective-permute-start.45 = (bf16[96,3840]{1,0:T(8,128)(2,1)S(1)}, bf16[96,3840]{1,0:T(8,128)(2,1)S(1)}, u32[]{:S(2)}, u32[]{:S(2)}) collective-permute-start(bf16[96,3840]{1,0:T(8,128)(2,1)S(1)} %shard_map.220.refs_7_.refs_0_), channel_id=1, source_target_pairs={{8,16},{16,8},{9,17},{17,9},{10,18},{18,10},{11,19},{19,11},{12,20... | collective-permute-start | bytes 2211848 | tf_op jit(solution)/shard_map/ppermute | solution.py:183
  212.8 21.4 %collective-permute-start.46 = (bf16[96,3072]{1,0:T(8,128)(2,1)}, bf16[96,3072]{1,0:T(8,128)(2,1)S(1)}, u32[]{:S(2)}, u32[]{:S(2)}) collective-permute-start(bf16[96,3072]{1,0:T(8,128)(2,1)} %get-tuple-element.152.refs_17_), channel_id=1, source_target_pairs={{0,8},{24,16},{1,9},{25,17},{2,10},{26,18},{3,11},{27,19},{4,12},{... | collective-permute-start | bytes 1769480 | tf_op jit(solution)/shard_map/ppermute | solution.py:171
  229.8 16.8 %all-to-all-start = ((bf16[4,96,1024]{2,1,0:T(8,128)(2,1)}), bf16[4,96,1024]{2,1,0:T(8,128)(2,1)}, u32[]{:S(2)}, u32[]{:S(2)}) async-start(bf16[4,96,1024]{2,1,0:T(8,128)(2,1)} %shard_map.223.refs_2_), calls=%async_computation | async-start | bytes 1572864 | tf_op jit(solution)/shard_map/all_to_all | solution.py:144
  239.7 30.0 %collective-permute-start.52 = (bf16[96,3840]{1,0:T(8,128)(2,1)S(1)}, bf16[96,3840]{1,0:T(8,128)(2,1)}, u32[]{:S(2)}, u32[]{:S(2)}) collective-permute-start(bf16[96,3840]{1,0:T(8,128)(2,1)S(1)} %shard_map.225.refs_5_), channel_id=1, source_target_pairs={{8,0},{16,24},{9,1},{17,25},{10,2},{18,26},{11,3},{19,27},{12,4},{... | collective-permute-start | bytes 2211848 | tf_op jit(solution)/shard_map/ppermute | solution.py:195
  250.3 19.0 %collective-permute-start.47 = (bf16[48,4096]{1,0:T(8,128)(2,1)}, bf16[48,4096]{1,0:T(8,128)(2,1)S(1)}, u32[]{:S(2)}, u32[]{:S(2)}) collective-permute-start(bf16[48,4096]{1,0:T(8,128)(2,1)} %get-tuple-element.163.refs_3_), channel_id=1, source_target_pairs={{0,8},{8,0},{16,24},{24,16},{1,9},{9,1},{17,25},{25,17},{2,10},{10... | collective-permute-start | bytes 1179656 | tf_op jit(solution)/shard_map/ppermute | solution.py:40
  254.7 35.4 %collective-permute-start.51 = (bf16[96,3072]{1,0:T(8,128)(2,1)S(1)}, bf16[96,3072]{1,0:T(8,128)(2,1)S(1)}, u32[]{:S(2)}, u32[]{:S(2)}) collective-permute-start(bf16[96,3072]{1,0:T(8,128)(2,1)S(1)} %shard_map.227.refs_2_), channel_id=1, source_target_pairs={{8,0},{16,24},{9,1},{17,25},{10,2},{18,26},{11,3},{19,27},{12,4},{... | collective-permute-start | bytes 1769480 | tf_op jit(solution)/shard_map/ppermute | solution.py:195
  269.4 19.5 %collective-permute-start.49 = (bf16[48,4096]{1,0:T(8,128)(2,1)S(1)}, bf16[48,4096]{1,0:T(8,128)(2,1)S(1)}, u32[]{:S(2)}, u32[]{:S(2)}) collective-permute-start(bf16[48,4096]{1,0:T(8,128)(2,1)S(1)} %shard_map.228.refs_0_), channel_id=1, source_target_pairs={{0,16},{8,24},{16,0},{24,8},{1,17},{9,25},{17,1},{25,9},{2,18},{10... | collective-permute-start | bytes 1179656 | tf_op jit(solution)/shard_map/ppermute | solution.py:40
  (69 other events, 472.8 us)

commit v2 on v1

--- a/solution.py
+++ b/solution.py
@@ -201,9 +201,16 @@
         shares = [lax.psum_scatter(grad, "dp", scatter_dimension=0, tiled=True) for grad in grads]
         return jnp.concatenate(shares, axis=1)
 
+    def squared(self):
+        if self.plain:
+            return [self.total()]
+        return [*self.sum_all(), *self.back()] if self.by_halves else [self.total()]
+
     def total(self):
         if self.plain:
-            return lax.psum(self.scattered(), "layer").astype(F32)
+            if "total" not in self.made:
+                self.made["total"] = lax.psum(self.scattered(), "layer").astype(F32)
+            return self.made["total"]
         (mine,), (other,) = self.sum_all(), self.back()
         if not self.by_halves:
             return jnp.where((self.place == 1) | (self.place == 2), mine, other).astype(F32)
@@ -212,15 +219,6 @@
         return jnp.concatenate(halves, axis=0).astype(F32)
 
 
-def layer_sums(*owned):
-    lows = [one.shares()[1] if not one.plain else one.scattered() for one in owned]
-    return [total.astype(F32) for total in lax.psum(tuple(lows), "layer")]
-
-
-def gathered_sum(value, axes):
-    size = lax.axis_size(axes)
-    sent = jnp.broadcast_to(value, (size, *value.shape))
-    return jnp.sum(lax.all_to_all(sent, axes, split_axis=0, concat_axis=0), axis=0)
 NAT = 208
 TILE = 256
 CHUNK = 48
@@ -1149,6 +1147,68 @@
     )(half, *terms)
 
 
+def sum_squares(parts):
+    squares = jnp.zeros((1, 1), F32)
+    for part in parts:
+        value = part[...].astype(F32)
+        squares = squares + jnp.sum(jnp.sum(value * value, axis=0, keepdims=True), axis=1, keepdims=True)
+    return squares
+
+
+def open_kernel(loss, counts, *refs):
+    parts, out = refs[:-1], refs[-1]
+    count = counts[0]
+    for index in range(1, counts.shape[0]):
+        count = count + counts[index]
+    lane = lax.broadcasted_iota(jnp.int32, out.shape, 1)
+    last = jnp.where(lane == 1, count.astype(F32), jnp.broadcast_to(sum_squares(parts), out.shape))
+    out[...] = jnp.where(lane == 0, loss[0, 0], last)
+
+
+def close_kernel(early, *refs):
+    parts, out = refs[:-1], refs[-1]
+    lane = lax.broadcasted_iota(jnp.int32, early.shape, 1)
+    row = early[...] + jnp.where(lane == 2, jnp.broadcast_to(sum_squares(parts), early.shape), 0.0)
+    out[...] = jnp.broadcast_to(row, out.shape)
+
+
+def close(loss, counts, parts, last, size):
+    early = launch(
+        open_kernel,
+        0,
+        in_specs=[NUMBERS, NUMBERS] + [ROW] * len(parts),
+        out_specs=ROW,
+        out_shape=shape((1, 128), F32),
+    )(loss, counts, *parts)
+    return launch(
+        close_kernel,
+        0,
+        in_specs=[ROW] * (1 + len(last)),
+        out_specs=ROW,
+        out_shape=shape((size, 128), F32),
+    )(early, *last)
+
+
+def factor_kernel(copies, rows, out):
+    total = jnp.sum(rows[...], axis=0, keepdims=True)
+    loss, masks, squares = total[:, :1], total[:, 1:2], total[:, 2:3] * (1.0 / copies)
+    per_mask = 1.0 / masks
+    norm = jnp.sqrt(squares) * per_mask
+    factor = CLIP_NORM / jnp.maximum(norm, CLIP_NORM) * per_mask
+    lane = lax.broadcasted_iota(jnp.int32, (1, 128), 1)
+    out[...] = jnp.where(lane == 0, loss, jnp.where(lane == 1, masks, jnp.where(lane == 2, norm, factor)))
+
+
+def factors(rows, copies):
+    return launch(
+        functools.partial(factor_kernel, copies),
+        1,
+        in_specs=[ROW],
+        out_specs=ROW,
+        out_shape=shape((1, 128), F32),
+    )(rows)
+
+
 def adam_update(master, first, second, grad, decay):
     first_new = FIRST_DECAY * first + (1.0 - FIRST_DECAY) * grad
     second_new = SECOND_DECAY * second + (1.0 - SECOND_DECAY) * grad * grad
@@ -1277,16 +1337,15 @@
     ready = last_s.shares(ready)
     ready = up_s.sum_all(ready)
     last_s.pairs(ready)
+    squared = [array for one in (down_s, up_s, last_s) for array in one.squared()]
     down_s, up_s, last_s = down_s.total(), up_s.total(), last_s.total()
     qkv_s, embed_s = last_s[:, : 4 * D], last_s[:, 4 * D :]
     wide_share = jnp.concatenate([embed_s[:, :D], qkv_s, up_s, down_s[:, FF:]], axis=1)
     tall_share = jnp.concatenate([down_s[:, :FF], embed_s[:, D : D + P_SIZE + VECS]], axis=1)
-    squares = (jnp.sum(wide_share * wide_share) + jnp.sum(tall_share * tall_share)) / layers
-    count = jnp.sum(mask_count.astype(F32))
-    loss_sum, mask_total, squares = gathered_sum(jnp.stack([loss[0, 0], count, squares]), ("layer", "dp"))
-    per_mask = 1.0 / mask_total
-    grad_norm = jnp.sqrt(squares) * per_mask
-    factor = CLIP_NORM / jnp.maximum(grad_norm, CLIP_NORM) * per_mask
+    axes = ("layer", "dp")
+    rows = close(loss, counts, squared[:-1], squared[-1:], lax.axis_size(axes))
+    rows = lax.all_to_all(rows, axes, split_axis=0, concat_axis=0, tiled=True)
+    loss_sum, mask_total, grad_norm, factor = factors(rows, layers)[0, :4]
     wide_new, wide_first_new, wide_second_new = adam_update(
         wide_master, wide_first, wide_second, factor * wide_share, 1.0
     )

time: 338 us -> 332 us (0.982)
  other arithmetic: 18.4 us -> 13.2 us
  between operations: 5.57 us -> 1.68 us
    reduce_sum x4 -> x0, other arithmetic: 3.65 us -> none  [the longest x1 1.36 us: body(): jnp.sum(wide_share * wide_share) + jnp.sum(tall_share * tall_share)]
    pallas_call x37 -> x40, Pallas kernels: 124 us -> 126 us  [call(): pl.pallas_call(body, grid_spec=spec, out_shape=out_shape, compiler_params...]
    unnamed x93 -> x91, local copies, waits for them, and re-layouts: 18.7 us -> 20.3 us
  transfers between devices with their start and end apart: 55 -> 55, of which waited for: 16 -> 16; matrix products, arithmetic and copies ran while one was open for 3% -> 2% of each run, Pallas kernels for 33% -> 34%
where the time goes in v2:
time: 332 us; the launch traced here: 327 us
  Pallas kernels  126 us (38%)
  waiting for transfers between devices  96.8 us (29%)
  starting transfers between devices  61.3 us (18%)
  local copies, waits for them, and re-layouts  27.8 us (8%)
  other arithmetic  13.2 us (4%)
    pallas_call x40, Pallas kernels, call(): pl.pallas_call(body, grid_spec=spec, out_shape=out_shape, compiler_params...  126 us
    ppermute x29, waiting for transfers between devices, swap(): return lax.ppermute(value, axis, flip(lax.axis_size(axis), bit))  50.1 us
    unnamed x91, local copies, waits for them, and re-layouts  20.3 us
    ppermute x29, starting transfers between devices, swap(): return lax.ppermute(value, axis, flip(lax.axis_size(axis), bit))  18.7 us
    ppermute x12, waiting for transfers between devices, over_link(): lax.ppermute(value, 'dp', [(i, i ^ (4 if i & 1 else 2)) for i in range(8)])  17.6 us
    ppermute x12, starting transfers between devices, over_link(): lax.ppermute(value, 'dp', [(i, i ^ (4 if i & 1 else 2)) for i in range(8)])  14.6 us
    ppermute x6, waiting for transfers between devices, over_other(): lax.ppermute(value, 'dp', [(i, i ^ (2 if i & 1 else 4)) for i in range(8)])  14.6 us
    ppermute x2, starting transfers between devices, make(): return [lax.ppermute(sent, 'layer', [(0, 1), (3, 2)])]  10.3 us
  transfers between devices with their start and end apart: 55, of which 16 were waited for; matrix products, arithmetic and copies ran while one was open for 2% of the time, Pallas kernels for 34%

profile of v2, /device:TPU:0, one launch (start us, length us, event | category | flops | bytes accessed | tf_op | source)
XLA Modules:
  0.0 326.7 jit_solution(18156361253892550416)
XLA Ops:
  11.6 4.8 %dynamic-slice_bitcast_fusion = (bf16[5,196,768]{2,1,0:T(8,128)(2,1)S(1)}, bf16[5,196,768]{2,1,0:T(8,128)(2,1)}, bf16[5,196,768]{2,1,0:T(8,128)(2,1)S(1)}, bf16[5,196,768]{2,1,0:T(8,128)(2,1)}) fusion(bf16[1,1,20,196,768]{4,3,2,1,0:T(8,128)(2,1)} %param.11, s32[]{:T(128)S(6)} %select_n.52, s32[]{:T(128)S(6)} %select_n.50, s32[]{:T(128)S(6)} %select_n.49, ...), kind=kLoop, calls=%fused_computation.6 | loop fusion | bytes 12042256 | tf_op jit(solution)/shard_map/dynamic_slice | solution.py:380
  25.8 6.9 %collective-permute-done.2.refs_2_.refs_7_.refs_9_ = bf16[96,3328]{1,0:T(8,128)(2,1)} collective-permute-done((bf16[96,3328]{1,0:T(8,128)(2,1)}, bf16[96,3328]{1,0:T(8,128)(2,1)}, u32[]{:S(2)}, u32[]{:S(2)}) %collective-permute-start.2) | collective-permute-done | bytes 639008 | tf_op jit(solution)/shard_map/ppermute | solution.py:44
  37.2 7.3 %shard_map.198 = (f32[5,208,768]{2,1,0:T(8,128)}, f32[5,208,128]{2,1,0:T(8,128)}, bf16[5,208,768]{2,1,0:T(8,128)(2,1)S(1)}, bf16[208,768]{1,0:T(8,128)(2,1)S(1)}...) custom-call(s32[8]{0:T(128)S(1)} %stack.35.refs_0_, ...), custom_call_target="tpu_custom_call" | custom-call | flops 2500000000 | bytes 1048576 | tf_op jit(solution)/shard_map/pallas_call | solution.py:260
  46.4 5.6 %collective-permute-done.11.refs_1_ = bf16[720,768]{1,0:T(8,128)(2,1)S(1)} collective-permute-done((bf16[720,768]{1,0:T(8,128)(2,1)S(1)}, bf16[720,768]{1,0:T(8,128)(2,1)S(1)}, u32[]{:S(2)}, u32[]{:S(2)}) %collective-permute-start.11) | collective-permute-done | bytes 1105952 | tf_op jit(solution)/shard_map/ppermute | solution.py:40
  56.8 12.0 %shard_map.201 = (bf16[5,208,1536]{2,1,0:T(8,128)(2,1)}, bf16[5,144,768]{2,1,0:T(8,128)(2,1)}, bf16[5,144,768]{2,1,0:T(8,128)(2,1)S(1)}, bf16[768,2304]{1,0:T(8,128)(2,1)}) custom-call(s32[8]{0:T(128)S(1)} %stack.35.refs_0_, s32[5]{0:T(128)S(1)} %bitcast.66, bf16[5,208,768]{2,1,0:T(8,128)(2,1)S(1)} %get-tuple-element.88.refs_2_, s32[5,1,196]{2,1,0:T(1,128)S(1)} %bitcast.58, ...), custom_call_target="tpu_custom_call" | custom-call | flops 30000001024 | bytes 1048576 | tf_op jit(solution)/shard_map/pallas_call | solution.py:260
  68.8 5.3 %collective-permute-done.14.refs_3_.refs_10_ = bf16[96,3840]{1,0:T(8,128)(2,1)S(1)} collective-permute-done((bf16[96,3840]{1,0:T(8,128)(2,1)S(1)}, bf16[96,3840]{1,0:T(8,128)(2,1)S(1)}, u32[]{:S(2)}, u32[]{:S(2)}) %collective-permute-start.14) | collective-permute-done | bytes 737312 | tf_op jit(solution)/shard_map/ppermute | solution.py:48
  74.7 4.5 %collective-permute-done.18.refs_15_.refs_13_ = bf16[720,384]{1,0:T(8,128)(2,1)S(1)} collective-permute-done((bf16[720,384]{1,0:T(8,128)(2,1)S(1)}, bf16[720,384]{1,0:T(8,128)(2,1)S(1)}, u32[]{:S(2)}, u32[]{:S(2)}) %collective-permute-start.18) | collective-permute-done | bytes 552992 | tf_op jit(solution)/shard_map/ppermute | solution.py:40
  81.5 3.4 %collective-permute-start.27 = (bf16[720,384]{1,0:T(8,128)(2,1)S(1)}, bf16[720,384]{1,0:T(8,128)(2,1)S(1)}, u32[]{:S(2)}, u32[]{:S(2)}) collective-permute-start(bf16[720,384]{1,0:T(8,128)(2,1)S(1)} %get-tuple-element.104), channel_id=1, source_target_pairs={{0,16},{8,24},{16,0},{24,8},{1,17},{9,25},{17,1},{25,9},{2,18},{10... | collective-permute-start | bytes 1658888 | tf_op jit(solution)/shard_map/ppermute | solution.py:40
  85.5 5.2 %collective-permute-done.19.refs_4_.refs_7_ = bf16[96,3840]{1,0:T(8,128)(2,1)S(1)} collective-permute-done((bf16[96,3840]{1,0:T(8,128)(2,1)S(1)}, bf16[96,3840]{1,0:T(8,128)(2,1)S(1)}, u32[]{:S(2)}, u32[]{:S(2)}) %collective-permute-start.19) | collective-permute-done | bytes 737312 | tf_op jit(solution)/shard_map/ppermute | solution.py:44
  91.2 4.7 %shard_map.203 = (f32[720,768]{1,0:T(8,128)S(1)}, f32[720,768]{1,0:T(8,128)S(1)}, f32[720,128]{1,0:T(8,128)S(1)}, bf16[720,768]{1,0:T(8,128)(2,1)S(1)}, bf16[768,3840]{1,0:T(8,128)(2,1)S(1)}) custom-call(s32[8]{0:T(128)S(1)} %stack.35.refs_0_, s32[5]{0:T(128)S(1)} %bitcast.67, s32[5,1,196]{2,1,0:T(1,128)S(1)} %bitcast.59, bf16[720,768]{1,0:T(8,128)(2,1)S(1)} %bitcast.52, ...), custom_call_target="tpu_custom_call" | custom-call | flops 15000000512 | bytes 1048576 | tf_op jit(solution)/shard_map/pallas_call | solution.py:260
  95.9 5.1 %shard_map.204 = (bf16[720,1536]{1,0:T(8,128)(2,1)S(1)}, bf16[720,1536]{1,0:T(8,128)(2,1)S(1)}) custom-call(bf16[720,768]{1,0:T(8,128)(2,1)S(1)} %get-tuple-element.94.refs_0_.refs_4_, f32[24,768]{1,0:T(8,128)S(1)} %get-tuple-element.90.refs_5_.refs_1_.refs_4_.refs_8_.refs_7_.refs_9_, bf16[768,3840]{1,0:T(8,128)(2,1)S(1)} %get-tuple-element.95.refs_2_.refs_8_), custom_call_target="tpu_custom_call" | custom-call | flops 17500000256 | bytes 1048576 | tf_op jit(solution)/shard_map/pallas_call | solution.py:260
  101.1 4.6 %collective-permute-done.21.refs_8_ = bf16[96,3840]{1,0:T(8,128)(2,1)S(1)} collective-permute-done((bf16[96,3840]{1,0:T(8,128)(2,1)S(1)}, bf16[96,3840]{1,0:T(8,128)(2,1)S(1)}, u32[]{:S(2)}, u32[]{:S(2)}) %collective-permute-start.21) | collective-permute-done | bytes 737312 | tf_op jit(solution)/shard_map/ppermute | solution.py:44
  106.6 5.1 %shard_map.205 = (bf16[720,1536]{1,0:T(8,128)(2,1)S(1)}, bf16[720,1536]{1,0:T(8,128)(2,1)S(1)}) custom-call(bf16[720,768]{1,0:T(8,128)(2,1)S(1)} %get-tuple-element.94.refs_0_.refs_4_, f32[24,768]{1,0:T(8,128)S(1)} %get-tuple-element.90.refs_5_.refs_1_.refs_4_.refs_8_.refs_7_.refs_9_, bf16[768,3840]{1,0:T(8,128)(2,1)S(1)} %get-tuple-element.95.refs_2_.refs_8_, ...), custom_call_target="tpu_custom_call" | custom-call | flops 17500000256 | bytes 1048576 | tf_op jit(solution)/shard_map/pallas_call | solution.py:260
  111.7 9.0 %shard_map.206 = (f32[720,768]{1,0:T(8,128)S(1)}, f32[720,128]{1,0:T(8,128)S(1)}, bf16[720,768]{1,0:T(8,128)(2,1)S(1)}, f32[720,768]{1,0:T(8,128)S(1)}, bf16[768,3840]{1,0:T(8,128)(2,1)S(1)}) custom-call(s32[8]{0:T(128)S(1)} %stack.35.refs_0_, bf16[720,1536]{1,0:T(8,128)(2,1)S(1)} %get-tuple-element.96.refs_3_.refs_1_.refs_6_, ...), custom_call_target="tpu_custom_call" | custom-call | flops 24999999488 | bytes 1048576 | tf_op jit(solution)/shard_map/pallas_call | solution.py:260
  120.7 12.2 %shard_map.207 = (bf16[2,96,3840]{2,1,0:T(8,128)(2,1)S(1)}, bf16[3,96,3840]{2,1,0:T(8,128)(2,1)S(1)}, bf16[3,96,3840]{2,1,0:T(8,128)(2,1)S(1)}, f32[1,1]{1,0:T(1...) custom-call(s32[8]{0:T(128)S(1)} %stack.35.refs_0_, ...), custom_call_target="tpu_custom_call" | custom-call | flops 37499998208 | bytes 1048576 | tf_op jit(solution)/shard_map/pallas_call | solution.py:260
  137.0 9.0 %shard_map.208 = (bf16[2,96,3072]{2,1,0:T(8,128)(2,1)S(1)}, bf16[3,96,3072]{2,1,0:T(8,128)(2,1)S(1)}, bf16[3,96,3072]{2,1,0:T(8,128)(2,1)S(1)}, bf16[720,3072]{1,0:T(8,128)(2,1)S(1)}, f32[8,3072]{1,0:T(8,128)S(1)}) custom-call(s32[8]{0:T(128)S(1)} %stack.35.refs_0_, bf16[720,768]{1,0:T(8,128)(2,1)S(1)} %get-tuple-element.109.refs_1_, ...), custom_call_target="tpu_custom_call" | custom-call | flops 30000001024 | bytes 1048576 | tf_op jit(solution)/shard_map/pallas_call | solution.py:260
  149.2 12.4 %shard_map.210 = (bf16[720,768]{1,0:T(8,128)(2,1)S(1)}, f32[208,768]{1,0:T(8,128)S(1)}, f32[4,8,768]{2,1,0:T(8,128)S(1)}, bf16[720,768]{1,0:T(8,128)(2,1)S(1)}) custom-call(s32[5]{0:T(128)S(1)} %bitcast.69, s32[5,1,196]{2,1,0:T(1,128)S(1)} %bitcast.60, bf16[720,3072]{1,0:T(8,128)(2,1)S(1)} %get-tuple-element.112.refs_2_, f32[720,768]{1,0:T(8,128)S(1)} %copy-done.36, ...), custom_call_target="tpu_custom_call" | custom-call | flops 35000000512 | bytes 1048576 | tf_op jit(solution)/shard_map/pallas_call | solution.py:260
  169.3 15.0 %shard_map.213 = (bf16[5,208,1536]{2,1,0:T(8,128)(2,1)S(1)}, f32[208,768]{1,0:T(8,128)S(1)}, f32[2,8,768]{2,1,0:T(8,128)S(1)}) custom-call(s32[5]{0:T(128)S(1)} %bitcast.70, bf16[5,144,768]{2,1,0:T(8,128)(2,1)S(1)} %copy-done.39, bf16[5,208,1536]{2,1,0:T(8,128)(2,1)S(1)} %copy-done.34, bf16[5,144,768]{2,1,0:T(8,128)(2,1)S(1)} %bitcast.48, ...), custom_call_target="tpu_custom_call" | custom-call | flops 37499998208 | bytes 1048576 | tf_op jit(solution)/shard_map/pallas_call | solution.py:260
  186.7 3.4 %collective-permute-start.34 = (bf16[96,3840]{1,0:T(8,128)(2,1)S(1)}, bf16[96,3840]{1,0:T(8,128)(2,1)S(1)}, u32[]{:S(2)}, u32[]{:S(2)}) collective-permute-start(bf16[96,3840]{1,0:T(8,128)(2,1)S(1)} %get-tuple-element.131.refs_8_), channel_id=1, source_target_pairs={{0,8},{24,16},{1,9},{25,17},{2,10},{26,18},{3,11},{27,19},{4,12},{... | collective-permute-start | bytes 2211848 | tf_op jit(solution)/shard_map/ppermute | solution.py:171
  190.2 5.9 %shard_map.216 = (bf16[2,96,3072]{2,1,0:T(8,128)(2,1)S(1)}, bf16[3,96,3072]{2,1,0:T(8,128)(2,1)S(1)}, bf16[3,96,3072]{2,1,0:T(8,128)(2,1)S(1)}) custom-call(s32[8]{0:T(128)S(1)} %stack.35.refs_0_, bf16[1040,768]{1,0:T(8,128)(2,1)S(1)} %bitcast.76, bf16[1040,1536]{1,0:T(8,128)(2,1)S(1)} %bitcast.74, bf16[208,768]{1,0:T(8,128)(2,1)S(1)} %copy-done.29, ...), custom_call_target="tpu_custom_call" | custom-call | flops 17500000256 | bytes 1048576 | tf_op jit(solution)/shard_map/pallas_call | solution.py:260
  198.6 6.2 %shard_map.218 = (bf16[1040,768]{1,0:T(8,128)(2,1)S(1)}, f32[768,256]{1,0:T(8,128)S(1)}) custom-call(s32[5]{0:T(128)S(1)} %bitcast.71, s32[5,1,196]{2,1,0:T(1,128)S(1)} %bitcast.62, bf16[1040,1536]{1,0:T(8,128)(2,1)S(1)} %bitcast.75, f32[208,768]{1,0:T(8,128)S(1)} %get-tuple-element.129.refs_3_.refs_4_, f32[208,768]{1,0:T(8,128)S(1)} %get-tuple-element.133.refs_4_, ...), custom_call_target="tpu_custom_call" | custom-call | flops 20000000000 | bytes 1048576 | tf_op jit(solution)/shard_map/pallas_call | solution.py:260
  212.9 6.9 %collective-permute-start.40 = (bf16[96,3072]{1,0:T(8,128)(2,1)}, bf16[96,3072]{1,0:T(8,128)(2,1)S(1)}, u32[]{:S(2)}, u32[]{:S(2)}) collective-permute-start(bf16[96,3072]{1,0:T(8,128)(2,1)} %get-tuple-element.150.refs_17_), channel_id=1, source_target_pairs={{0,8},{24,16},{1,9},{25,17},{2,10},{26,18},{3,11},{27,19},{4,12},{... | collective-permute-start | bytes 1769480 | tf_op jit(solution)/shard_map/ppermute | solution.py:171
  219.7 7.1 %collective-permute-done.43.refs_1_ = bf16[96,3072]{1,0:T(8,128)(2,1)S(1)} collective-permute-done((bf16[96,3072]{1,0:T(8,128)(2,1)S(1)}, bf16[96,3072]{1,0:T(8,128)(2,1)S(1)}, u32[]{:S(2)}, u32[]{:S(2)}) %collective-permute-start.43) | collective-permute-done | bytes 589856 | tf_op jit(solution)/shard_map/ppermute | solution.py:48
  229.8 4.4 %all-to-all-start = ((bf16[4,96,1024]{2,1,0:T(8,128)(2,1)}), bf16[4,96,1024]{2,1,0:T(8,128)(2,1)}, u32[]{:S(2)}, u32[]{:S(2)}) async-start(bf16[4,96,1024]{2,1,0:T(8,128)(2,1)} %shard_map.223.refs_2_), calls=%async_computation | async-start | bytes 1572864 | tf_op jit(solution)/shard_map/all_to_all | solution.py:144
  241.7 5.0 %all-to-all-done.refs_4_ = bf16[4,96,1024]{2,1,0:T(8,128)(2,1)} async-done(((bf16[4,96,1024]{2,1,0:T(8,128)(2,1)}), bf16[4,96,1024]{2,1,0:T(8,128)(2,1)}, u32[]{:S(2)}, u32[]{:S(2)}) %all-to-all-start) | async-done | bytes 786464 | tf_op jit(solution)/shard_map/all_to_all | solution.py:144
  255.4 13.9 %collective-permute-done.50.refs_1_ = bf16[48,4096]{1,0:T(8,128)(2,1)S(1)} collective-permute-done((bf16[48,4096]{1,0:T(8,128)(2,1)}, bf16[48,4096]{1,0:T(8,128)(2,1)S(1)}, u32[]{:S(2)}, u32[]{:S(2)}) %collective-permute-start.50) | collective-permute-done | bytes 393248 | tf_op jit(solution)/shard_map/ppermute | solution.py:40
  271.0 17.8 %collective-permute-done.51.refs_1_ = bf16[48,4096]{1,0:T(8,128)(2,1)S(1)} collective-permute-done((bf16[48,4096]{1,0:T(8,128)(2,1)S(1)}, bf16[48,4096]{1,0:T(8,128)(2,1)S(1)}, u32[]{:S(2)}, u32[]{:S(2)}) %collective-permute-start.51) | collective-permute-done | bytes 393248 | tf_op jit(solution)/shard_map/ppermute | solution.py:40
  291.7 8.2 %collective-permute-done.52.refs_1_ = bf16[48,4096]{1,0:T(8,128)(2,1)S(1)} collective-permute-done((bf16[48,4096]{1,0:T(8,128)(2,1)S(1)}, bf16[48,4096]{1,0:T(8,128)(2,1)S(1)}, u32[]{:S(2)}, u32[]{:S(2)}) %collective-permute-start.52) | collective-permute-done | bytes 393248 | tf_op jit(solution)/shard_map/ppermute | solution.py:40
  302.0 4.0 %all-to-all-start.1 = ((f32[32,1,128]{2,1,0:T(1,128)}), f32[32,1,128]{2,1,0:T(1,128)S(1)}, u32[]{:S(2)}, u32[]{:S(2)}) async-start(f32[32,1,128]{2,1,0:T(1,128)} %bitcast.27), calls=%async_computation.1 | async-start | bytes 32768 | tf_op jit(solution)/shard_map/all_to_all | solution.py:1347
  306.0 7.1 %all-to-all-done.1 = f32[32,1,128]{2,1,0:T(1,128)S(1)} async-done(((f32[32,1,128]{2,1,0:T(1,128)}), f32[32,1,128]{2,1,0:T(1,128)S(1)}, u32[]{:S(2)}, u32[]{:S(2)}) %all-to-all-start.1) | async-done | bytes 16416 | tf_op jit(solution)/shard_map/all_to_all | solution.py:1347
  315.5 3.6 %fusion.5 = (bf16[3287,96]{0,1:T(8,128)(2,1)}, f32[3287,96]{0,1:T(8,128)}, f32[3287,96]{0,1:T(8,128)}, f32[3287,96]{0,1:T(8,128)}, f32[3287,96]{0,1:T(8,128)S(1)}) fusion(f32[3287,96]{0,1:T(8,128)S(1)} %copy-done.40, f32[3287]{0:T(1024)S(1)} %fusion.3, f32[3287,96]{0,1:T(8,128)S(1)} %copy-done.43, f32[3287,96]{0,1:T(8,128)S(1)} %copy-done.44, ...), kind=kLoop, calls=%fused_computation.37 | loop fusion | flops 5679936 | bytes 10741920 | tf_op jit(solution)/shard_map/convert_element_type | solution.py:1368
  321.1 5.4 %fusion.8 = (bf16[96,7680]{1,0:T(8,128)(2,1)}, f32[96,7680]{1,0:T(8,128)}, f32[96,7680]{1,0:T(8,128)}, f32[96,7680]{1,0:T(8,128)}) fusion(f32[96,7680]{1,0:T(8,128)S(1)} %copy-done.2, f32[96,768]{1,0:T(8,128)S(1)} %slice-done.1, f32[96,3072]{1,0:T(8,128)S(1)} %select_convert_fusion.1.refs_3_, f32[96,3072]{1,0:T(8,128)S(1)} %slice-done.2, ...), kind=kLoop, calls=%fused_computation.38 | loop fusion | flops 14745600 | bytes 22118404 | tf_op jit(solution)/shard_map/convert_element_type | solution.py:1364
  (241 shorter events, 94.4 us)
Async XLA Ops:
  7.2 14.6 %collective-permute-start.7 = (s32[5,197]{1,0:T(8,128)S(1)}, s32[5,197]{1,0:T(8,128)S(1)}, u32[]{:S(2)}, u32[]{:S(2)}) collective-permute-start(s32[5,197]{1,0:T(8,128)S(1)} %pad_add_fusion), channel_id=1, source_target_pairs={{0,16},{8,24},{16,0},{24,8},{1,17},{9,25},{17,1},{25,9},{2,18},{10... | collective-permute-start | bytes 11828 | tf_op jit(solution)/shard_map/ppermute | solution.py:40
  16.4 16.3 %collective-permute-start.2 = (bf16[96,3328]{1,0:T(8,128)(2,1)}, bf16[96,3328]{1,0:T(8,128)(2,1)}, u32[]{:S(2)}, u32[]{:S(2)}) collective-permute-start(bf16[96,3328]{1,0:T(8,128)(2,1)} %collective-permute-done.refs_4_.refs_5_.refs_7_), channel_id=1, source_target_pairs={{0,2},{1,5},{2,0},{3,7},{4,6},{5,1},{6,4},{7,3},{8,10},{9,13},{10,... | collective-permute-start | bytes 1916936 | tf_op jit(solution)/shard_map/ppermute | solution.py:44
  16.9 15.8 %collective-permute-start.3 = (bf16[96,3328]{1,0:T(8,128)(2,1)}, bf16[96,3328]{1,0:T(8,128)(2,1)}, u32[]{:S(2)}, u32[]{:S(2)}) collective-permute-start(bf16[96,3328]{1,0:T(8,128)(2,1)} %collective-permute-done.1.refs_5_.refs_6_.refs_8_), channel_id=1, source_target_pairs={{0,4},{1,3},{2,6},{3,1},{4,0},{5,7},{6,2},{7,5},{8,12},{9,11},{10,... | collective-permute-start | bytes 1916936 | tf_op jit(solution)/shard_map/ppermute | solution.py:48
  25.1 26.8 %collective-permute-start.11 = (bf16[720,768]{1,0:T(8,128)(2,1)S(1)}, bf16[720,768]{1,0:T(8,128)(2,1)S(1)}, u32[]{:S(2)}, u32[]{:S(2)}) collective-permute-start(bf16[720,768]{1,0:T(8,128)(2,1)S(1)} %shard_map.196.refs_3_), channel_id=1, source_target_pairs={{0,8},{8,0},{16,24},{24,16},{1,9},{9,1},{17,25},{25,17},{2,10},{10... | collective-permute-start | bytes 3317768 | tf_op jit(solution)/shard_map/ppermute | solution.py:40
  33.7 21.0 %collective-permute-start.10 = (bf16[96,3840]{1,0:T(8,128)(2,1)S(1)}, bf16[96,3840]{1,0:T(8,128)(2,1)S(1)}, u32[]{:S(2)}, u32[]{:S(2)}) collective-permute-start(bf16[96,3840]{1,0:T(8,128)(2,1)S(1)} %shard_map.195.refs_12_.refs_6_), channel_id=1, source_target_pairs={{0,2},{1,5},{2,0},{3,7},{4,6},{5,1},{6,4},{7,3},{8,10},{9,13},{10,... | collective-permute-start | bytes 2211848 | tf_op jit(solution)/shard_map/ppermute | solution.py:44
  35.3 20.3 %collective-permute-start.12 = (bf16[96,3840]{1,0:T(8,128)(2,1)S(1)}, bf16[96,3840]{1,0:T(8,128)(2,1)S(1)}, u32[]{:S(2)}, u32[]{:S(2)}) collective-permute-start(bf16[96,3840]{1,0:T(8,128)(2,1)S(1)} %shard_map.195.refs_12_.refs_6_), channel_id=1, source_target_pairs={{0,1},{1,0},{2,3},{3,2},{4,5},{5,4},{6,7},{7,6},{8,9},{9,8},{10,11... | collective-permute-start | bytes 2211848 | tf_op jit(solution)/shard_map/ppermute | solution.py:40
  52.3 26.9 %collective-permute-start.18 = (bf16[720,384]{1,0:T(8,128)(2,1)S(1)}, bf16[720,384]{1,0:T(8,128)(2,1)S(1)}, u32[]{:S(2)}, u32[]{:S(2)}) collective-permute-start(bf16[720,384]{1,0:T(8,128)(2,1)S(1)} %get-tuple-element.91.refs_15_), channel_id=1, source_target_pairs={{0,16},{8,24},{16,0},{24,8},{1,17},{9,25},{17,1},{25,9},{2,18},{10... | collective-permute-start | bytes 1658888 | tf_op jit(solution)/shard_map/ppermute | solution.py:40
  54.8 19.3 %collective-permute-start.14 = (bf16[96,3840]{1,0:T(8,128)(2,1)S(1)}, bf16[96,3840]{1,0:T(8,128)(2,1)S(1)}, u32[]{:S(2)}, u32[]{:S(2)}) collective-permute-start(bf16[96,3840]{1,0:T(8,128)(2,1)S(1)} %collective-permute-done.10.refs_14_.refs_8_), channel_id=1, source_target_pairs={{0,4},{1,3},{2,6},{3,1},{4,0},{5,7},{6,2},{7,5},{8,12},{9,11},{10,... | collective-permute-start | bytes 2211848 | tf_op jit(solution)/shard_map/ppermute | solution.py:48
  55.3 25.5 %collective-permute-start.15 = (bf16[96,3840]{1,0:T(8,128)(2,1)S(1)}, bf16[96,3840]{1,0:T(8,128)(2,1)S(1)}, u32[]{:S(2)}, u32[]{:S(2)}) collective-permute-start(bf16[96,3840]{1,0:T(8,128)(2,1)S(1)} %collective-permute-done.10.refs_14_.refs_8_), channel_id=1, source_target_pairs={{0,1},{1,0},{2,3},{3,2},{4,5},{5,4},{6,7},{7,6},{8,9},{9,8},{10,11... | collective-permute-start | bytes 2211848 | tf_op jit(solution)/shard_map/ppermute | solution.py:40
  55.6 25.1 %collective-permute-start.13 = (bf16[96,3840]{1,0:T(8,128)(2,1)S(1)}, bf16[96,3840]{1,0:T(8,128)(2,1)S(1)}, u32[]{:S(2)}, u32[]{:S(2)}) collective-permute-start(bf16[96,3840]{1,0:T(8,128)(2,1)S(1)} %collective-permute-done.12.refs_7_), channel_id=1, source_target_pairs={{0,2},{1,5},{2,0},{3,7},{4,6},{5,1},{6,4},{7,3},{8,10},{9,13},{10,... | collective-permute-start | bytes 2211848 | tf_op jit(solution)/shard_map/ppermute | solution.py:44
  80.8 39.9 %collective-permute-start.26 = (bf16[720,768]{1,0:T(8,128)(2,1)S(1)}, bf16[720,768]{1,0:T(8,128)(2,1)S(1)}, u32[]{:S(2)}, u32[]{:S(2)}) collective-permute-start(bf16[720,768]{1,0:T(8,128)(2,1)S(1)} %shard_map.199.refs_2_), channel_id=1, source_target_pairs={{0,8},{8,0},{16,24},{24,16},{1,9},{9,1},{17,25},{25,17},{2,10},{10... | collective-permute-start | bytes 3317768 | tf_op jit(solution)/shard_map/ppermute | solution.py:40
  81.5 39.1 %collective-permute-start.27 = (bf16[720,384]{1,0:T(8,128)(2,1)S(1)}, bf16[720,384]{1,0:T(8,128)(2,1)S(1)}, u32[]{:S(2)}, u32[]{:S(2)}) collective-permute-start(bf16[720,384]{1,0:T(8,128)(2,1)S(1)} %get-tuple-element.104), channel_id=1, source_target_pairs={{0,16},{8,24},{16,0},{24,8},{1,17},{9,25},{17,1},{25,9},{2,18},{10... | collective-permute-start | bytes 1658888 | tf_op jit(solution)/shard_map/ppermute | solution.py:40
  84.9 20.7 %collective-permute-start.21 = (bf16[96,3840]{1,0:T(8,128)(2,1)S(1)}, bf16[96,3840]{1,0:T(8,128)(2,1)S(1)}, u32[]{:S(2)}, u32[]{:S(2)}) collective-permute-start(bf16[96,3840]{1,0:T(8,128)(2,1)S(1)} %collective-permute-done.20.refs_6_), channel_id=1, source_target_pairs={{0,2},{1,5},{2,0},{3,7},{4,6},{5,1},{6,4},{7,3},{8,10},{9,13},{10,... | collective-permute-start | bytes 2211848 | tf_op jit(solution)/shard_map/ppermute | solution.py:44
  90.7 15.0 %collective-permute-start.22 = (bf16[96,3840]{1,0:T(8,128)(2,1)S(1)}, bf16[96,3840]{1,0:T(8,128)(2,1)S(1)}, u32[]{:S(2)}, u32[]{:S(2)}) collective-permute-start(bf16[96,3840]{1,0:T(8,128)(2,1)S(1)} %collective-permute-done.19.refs_4_.refs_7_), channel_id=1, source_target_pairs={{0,4},{1,3},{2,6},{3,1},{4,0},{5,7},{6,2},{7,5},{8,12},{9,11},{10,... | collective-permute-start | bytes 2211848 | tf_op jit(solution)/shard_map/ppermute | solution.py:48
  146.0 15.6 %collective-permute-start.33 = (bf16[3,96,3072]{2,1,0:T(8,128)(2,1)S(1)}, bf16[3,96,3072]{2,1,0:T(8,128)(2,1)S(1)}, u32[]{:S(2)}, u32[]{:S(2)}) collective-permute-start(bf16[3,96,3072]{2,1,0:T(8,128)(2,1)S(1)} %get-tuple-element.125), channel_id=1, source_target_pairs={{0,1},{1,0},{2,3},{3,2},{4,5},{5,4},{6,7},{7,6},{8,9},{9,8},{10,11... | collective-permute-start | bytes 5308424 | tf_op jit(solution)/shard_map/ppermute | solution.py:40
  147.1 19.1 %collective-permute-start.29 = (bf16[96,3840]{1,0:T(8,128)(2,1)S(1)}, bf16[96,3840]{1,0:T(8,128)(2,1)S(1)}, u32[]{:S(2)}, u32[]{:S(2)}) collective-permute-start(bf16[96,3840]{1,0:T(8,128)(2,1)S(1)} %get-tuple-element.114.refs_11_), channel_id=1, source_target_pairs={{0,4},{1,3},{2,6},{3,1},{4,0},{5,7},{6,2},{7,5},{8,12},{9,11},{10,... | collective-permute-start | bytes 2211848 | tf_op jit(solution)/shard_map/ppermute | solution.py:48
  147.7 19.4 %collective-permute-start.30 = (bf16[96,3840]{1,0:T(8,128)(2,1)S(1)}, bf16[96,3840]{1,0:T(8,128)(2,1)S(1)}, u32[]{:S(2)}, u32[]{:S(2)}) collective-permute-start(bf16[96,3840]{1,0:T(8,128)(2,1)S(1)} %get-tuple-element.115.refs_10_), channel_id=1, source_target_pairs={{0,2},{1,5},{2,0},{3,7},{4,6},{5,1},{6,4},{7,3},{8,10},{9,13},{10,... | collective-permute-start | bytes 2211848 | tf_op jit(solution)/shard_map/ppermute | solution.py:44
  162.0 22.4 %collective-permute-start.35 = (bf16[96,3072]{1,0:T(8,128)(2,1)S(1)}, bf16[96,3072]{1,0:T(8,128)(2,1)S(1)}, u32[]{:S(2)}, u32[]{:S(2)}) collective-permute-start(bf16[96,3072]{1,0:T(8,128)(2,1)S(1)} %get-tuple-element.128.refs_9_), channel_id=1, source_target_pairs={{0,4},{1,3},{2,6},{3,1},{4,0},{5,7},{6,2},{7,5},{8,12},{9,11},{10,... | collective-permute-start | bytes 1769480 | tf_op jit(solution)/shard_map/ppermute | solution.py:48
  163.5 20.8 %collective-permute-start.36 = (bf16[96,3072]{1,0:T(8,128)(2,1)S(1)}, bf16[96,3072]{1,0:T(8,128)(2,1)S(1)}, u32[]{:S(2)}, u32[]{:S(2)}) collective-permute-start(bf16[96,3072]{1,0:T(8,128)(2,1)S(1)} %get-tuple-element.127.refs_8_), channel_id=1, source_target_pairs={{0,2},{1,5},{2,0},{3,7},{4,6},{5,1},{6,4},{7,3},{8,10},{9,13},{10,... | collective-permute-start | bytes 1769480 | tf_op jit(solution)/shard_map/ppermute | solution.py:44
  167.4 18.7 %collective-permute-start.31 = (bf16[96,3840]{1,0:T(8,128)(2,1)S(1)}, bf16[96,3840]{1,0:T(8,128)(2,1)S(1)}, u32[]{:S(2)}, u32[]{:S(2)}) collective-permute-start(bf16[96,3840]{1,0:T(8,128)(2,1)S(1)} %get-tuple-element.120.refs_5_), channel_id=1, source_target_pairs={{0,2},{1,5},{2,0},{3,7},{4,6},{5,1},{6,4},{7,3},{8,10},{9,13},{10,... | collective-permute-start | bytes 2211848 | tf_op jit(solution)/shard_map/ppermute | solution.py:44
  169.0 17.2 %collective-permute-start.32 = (bf16[96,3840]{1,0:T(8,128)(2,1)S(1)}, bf16[96,3840]{1,0:T(8,128)(2,1)S(1)}, u32[]{:S(2)}, u32[]{:S(2)}) collective-permute-start(bf16[96,3840]{1,0:T(8,128)(2,1)S(1)} %get-tuple-element.121.refs_6_), channel_id=1, source_target_pairs={{0,1},{1,0},{2,3},{3,2},{4,5},{5,4},{6,7},{7,6},{8,9},{9,8},{10,11... | collective-permute-start | bytes 2211848 | tf_op jit(solution)/shard_map/ppermute | solution.py:40
  186.7 19.5 %collective-permute-start.34 = (bf16[96,3840]{1,0:T(8,128)(2,1)S(1)}, bf16[96,3840]{1,0:T(8,128)(2,1)S(1)}, u32[]{:S(2)}, u32[]{:S(2)}) collective-permute-start(bf16[96,3840]{1,0:T(8,128)(2,1)S(1)} %get-tuple-element.131.refs_8_), channel_id=1, source_target_pairs={{0,8},{24,16},{1,9},{25,17},{2,10},{26,18},{3,11},{27,19},{4,12},{... | collective-permute-start | bytes 2211848 | tf_op jit(solution)/shard_map/ppermute | solution.py:171
  210.6 18.2 %collective-permute-start.42 = (bf16[4,96,1024]{2,1,0:T(8,128)(2,1)S(1)}, bf16[4,96,1024]{2,1,0:T(8,128)(2,1)S(1)}, u32[]{:S(2)}, u32[]{:S(2)}) collective-permute-start(bf16[4,96,1024]{2,1,0:T(8,128)(2,1)S(1)} %get-tuple-element.159), channel_id=1, source_target_pairs={{0,1},{1,0},{2,3},{3,2},{4,5},{5,4},{6,7},{7,6},{8,9},{9,8},{10,11... | collective-permute-start | bytes 2359304 | tf_op jit(solution)/shard_map/ppermute | solution.py:40
  210.7 16.2 %collective-permute-start.43 = (bf16[96,3072]{1,0:T(8,128)(2,1)S(1)}, bf16[96,3072]{1,0:T(8,128)(2,1)S(1)}, u32[]{:S(2)}, u32[]{:S(2)}) collective-permute-start(bf16[96,3072]{1,0:T(8,128)(2,1)S(1)} %get-tuple-element.157.refs_6_), channel_id=1, source_target_pairs={{0,4},{1,3},{2,6},{3,1},{4,0},{5,7},{6,2},{7,5},{8,12},{9,11},{10,... | collective-permute-start | bytes 1769480 | tf_op jit(solution)/shard_map/ppermute | solution.py:48
  211.2 15.6 %collective-permute-start.44 = (bf16[96,3072]{1,0:T(8,128)(2,1)S(1)}, bf16[96,3072]{1,0:T(8,128)(2,1)S(1)}, u32[]{:S(2)}, u32[]{:S(2)}) collective-permute-start(bf16[96,3072]{1,0:T(8,128)(2,1)S(1)} %get-tuple-element.156.refs_5_), channel_id=1, source_target_pairs={{0,2},{1,5},{2,0},{3,7},{4,6},{5,1},{6,4},{7,3},{8,10},{9,13},{10,... | collective-permute-start | bytes 1769480 | tf_op jit(solution)/shard_map/ppermute | solution.py:44
  212.2 25.3 %collective-permute-start.39 = (bf16[96,3840]{1,0:T(8,128)(2,1)S(1)}, bf16[96,3840]{1,0:T(8,128)(2,1)S(1)}, u32[]{:S(2)}, u32[]{:S(2)}) collective-permute-start(bf16[96,3840]{1,0:T(8,128)(2,1)S(1)} %shard_map.219.refs_7_.refs_0_), channel_id=1, source_target_pairs={{8,16},{16,8},{9,17},{17,9},{10,18},{18,10},{11,19},{19,11},{12,20... | collective-permute-start | bytes 2211848 | tf_op jit(solution)/shard_map/ppermute | solution.py:183
  212.9 21.3 %collective-permute-start.40 = (bf16[96,3072]{1,0:T(8,128)(2,1)}, bf16[96,3072]{1,0:T(8,128)(2,1)S(1)}, u32[]{:S(2)}, u32[]{:S(2)}) collective-permute-start(bf16[96,3072]{1,0:T(8,128)(2,1)} %get-tuple-element.150.refs_17_), channel_id=1, source_target_pairs={{0,8},{24,16},{1,9},{25,17},{2,10},{26,18},{3,11},{27,19},{4,12},{... | collective-permute-start | bytes 1769480 | tf_op jit(solution)/shard_map/ppermute | solution.py:171
  229.8 16.8 %all-to-all-start = ((bf16[4,96,1024]{2,1,0:T(8,128)(2,1)}), bf16[4,96,1024]{2,1,0:T(8,128)(2,1)}, u32[]{:S(2)}, u32[]{:S(2)}) async-start(bf16[4,96,1024]{2,1,0:T(8,128)(2,1)} %shard_map.223.refs_2_), calls=%async_computation | async-start | bytes 1572864 | tf_op jit(solution)/shard_map/all_to_all | solution.py:144
  239.7 30.1 %collective-permute-start.45 = (bf16[96,3840]{1,0:T(8,128)(2,1)S(1)}, bf16[96,3840]{1,0:T(8,128)(2,1)}, u32[]{:S(2)}, u32[]{:S(2)}) collective-permute-start(bf16[96,3840]{1,0:T(8,128)(2,1)S(1)} %shard_map.225.refs_5_), channel_id=1, source_target_pairs={{8,0},{16,24},{9,1},{17,25},{10,2},{18,26},{11,3},{19,27},{12,4},{... | collective-permute-start | bytes 2211848 | tf_op jit(solution)/shard_map/ppermute | solution.py:195
  250.4 19.0 %collective-permute-start.50 = (bf16[48,4096]{1,0:T(8,128)(2,1)}, bf16[48,4096]{1,0:T(8,128)(2,1)S(1)}, u32[]{:S(2)}, u32[]{:S(2)}) collective-permute-start(bf16[48,4096]{1,0:T(8,128)(2,1)} %get-tuple-element.163.refs_3_), channel_id=1, source_target_pairs={{0,8},{8,0},{16,24},{24,16},{1,9},{9,1},{17,25},{25,17},{2,10},{10... | collective-permute-start | bytes 1179656 | tf_op jit(solution)/shard_map/ppermute | solution.py:40
  254.1 35.9 %collective-permute-start.49 = (bf16[96,3072]{1,0:T(8,128)(2,1)S(1)}, bf16[96,3072]{1,0:T(8,128)(2,1)S(1)}, u32[]{:S(2)}, u32[]{:S(2)}) collective-permute-start(bf16[96,3072]{1,0:T(8,128)(2,1)S(1)} %shard_map.227.refs_2_), channel_id=1, source_target_pairs={{8,0},{16,24},{9,1},{17,25},{10,2},{18,26},{11,3},{19,27},{12,4},{... | collective-permute-start | bytes 1769480 | tf_op jit(solution)/shard_map/ppermute | solution.py:195
  269.4 19.4 %collective-permute-start.51 = (bf16[48,4096]{1,0:T(8,128)(2,1)S(1)}, bf16[48,4096]{1,0:T(8,128)(2,1)S(1)}, u32[]{:S(2)}, u32[]{:S(2)}) collective-permute-start(bf16[48,4096]{1,0:T(8,128)(2,1)S(1)} %shard_map.228.refs_0_), channel_id=1, source_target_pairs={{0,16},{8,24},{16,0},{24,8},{1,17},{9,25},{17,1},{25,9},{2,18},{10... | collective-permute-start | bytes 1179656 | tf_op jit(solution)/shard_map/ppermute | solution.py:40
  (71 other events, 459.0 us)
